TPU v7x, 256 devices: a whole 4x4x8 slice. The times are simulated.
256 devices in a mesh: ctx: 32 (over x, z_lo, core), tp: 8 (over y, z_hi).
Axes of the slice: x: 4, y: 4, z: 8 (z_hi: 2, z_lo: 4; z = z_hi * 4 + z_lo), core: 2. Of those that a mesh axis runs over, the one named last changes fastest.
Arguments:
- hyena_feats: bfloat16 [3, 4096, 8192], P(None, 'ctx', 'tp'), may hold values from -6 to 6
- short_taps: float32 [3, 3, 8192], P(None, None, 'tp'), may hold values from -3 to 3
- decay_rate: float32 [16, 8192], P(None, 'tp'), may hold values from 6.1035156e-05 to 0.04
- residue: float32 [16, 8192], P(None, 'tp'), may hold values from -6 to 6
- attn_qkv: bfloat16 [3, 4096, 4096], P(None, 'ctx', 'tp'), may hold values from -7.5 to 7.5
- out_weight: bfloat16 [4096, 8192], P('tp', 'ctx'), may hold values from -0.09375 to 0.09375
Outputs:
- hyena_mixed: bfloat16 [4096, 8192], P('ctx', 'tp')
- attn_mixed: bfloat16 [4096, 8192], P('ctx', 'tp')
All inputs are finite; a program needn't handle non-finite values.
Results may differ from a plain program's by a relative error of at most 0.015.
Values may be sent and summed in bfloat16 or wider, within the bound.
No kernel may reach another device: no remote copies, remote signals or barrier semaphores. Data moves between devices by JAX's collectives and lax.ppermute only.
A program may use at most 128 MiB of HBM per device.

v0:
```python
import jax
import jax.numpy as jnp
from jax import lax
from jax.sharding import PartitionSpec as P

HEAD = 128


sub_rows = 16
neg_large = -1e30


def passed_along(value, axis, steps):
    count = lax.axis_size(axis)
    initial, last = (max(0, -steps), min(count, count - steps))
    return lax.ppermute(value, axis, [(source, source + steps) for source in range(initial, last)])


def prefix_2(part, axis, combine, identity):
    place = lax.axis_index(axis)
    gathered = jax.tree.map(lambda a: lax.all_gather(a, axis), part)
    state = jax.tree.map(lambda a, e: jnp.zeros_like(a) + jnp.asarray(e, a.dtype), part, identity)

    def one(step, state):
        return combine(
            state, jax.tree.map(lambda a: lax.dynamic_index_in_dim(a, step, 0, False), gathered)
        )

    return lax.fori_loop(0, place, one, state)


def filter_tables(decay_rate, residue):
    order_count = decay_rate.shape[0]
    offsets = jnp.arange(sub_rows).astype(jnp.float32)
    weight = residue * jnp.sqrt(-jnp.expm1(-2.0 * decay_rate) / order_count)
    kernel = jnp.sum(weight[None] * jnp.exp(-decay_rate[None] * offsets[:, None, None]), axis=1)
    later = jnp.arange(sub_rows)[:, None]
    earlier = jnp.arange(sub_rows)[None, :]
    lagged = kernel[jnp.maximum(later - earlier, 0)]
    toeplitz = jnp.where((later >= earlier)[:, :, None], lagged, 0.0)
    end_table = jnp.exp(-decay_rate[None] * (sub_rows - 1.0 - offsets)[:, None, None])
    out_table = weight[None] * jnp.exp(-decay_rate[None] * (offsets + 1.0)[:, None, None])
    return (toeplitz, end_table, out_table)


def block_terms(product, toeplitz, end_table):
    chans = product.shape[-1]
    sub_blocks = product.reshape(-1, sub_rows, chans)
    inside = jnp.einsum("tsc,nsc->ntc", toeplitz, sub_blocks, precision=lax.Precision.HIGHEST)
    local_ends = jnp.einsum("src,nsc->nrc", end_table, sub_blocks, precision=lax.Precision.HIGHEST)
    return (inside, local_ends)


def carry_states(local_ends, step_decay):

    def advance(running_state, block_ends):
        return (step_decay * running_state + block_ends, running_state)

    final_state, states_before = lax.scan(
        advance, jnp.zeros(step_decay.shape, jnp.float32), local_ends
    )
    return (states_before, final_state)


def finish_conv(inside, states_before, out_table):
    carried = jnp.einsum("trc,nrc->ntc", out_table, states_before, precision=lax.Precision.HIGHEST)
    return (inside + carried).reshape(-1, inside.shape[-1])


def combine_states(earlier, later):
    return (earlier[0] * later[0], earlier[1] * later[0] + later[1])


def long_mixer(hyena_feats, short_taps, decay_rate, residue):
    rows = hyena_feats.shape[1]
    tap_count = short_taps.shape[1]
    edge_rows = passed_along(hyena_feats[:, rows - (tap_count - 1) :, :], "ctx", 1)
    extended = jnp.concatenate([edge_rows, hyena_feats], axis=1)
    featured = jnp.zeros(hyena_feats.shape, jnp.float32)
    for tap_index in range(tap_count):
        lo_edge = tap_count - 1 - tap_index
        featured = (
            featured + short_taps[:, tap_index, None, :] * extended[:, lo_edge : lo_edge + rows, :]
        )
    product = featured[1] * featured[2]
    toeplitz, end_table, out_table = filter_tables(decay_rate, residue)
    inside, local_ends = block_terms(product, toeplitz, end_table)
    step_decay = jnp.exp(-decay_rate * sub_rows)
    states_before, final_state = carry_states(local_ends, step_decay)
    span_decay = jnp.exp(-decay_rate * rows)
    prefix = prefix_2(
        (span_decay, final_state),
        "ctx",
        combine_states,
        (jnp.ones_like(span_decay), jnp.zeros_like(final_state)),
    )
    incoming = prefix[1]
    block_count = states_before.shape[0]
    block_offsets = (sub_rows * jnp.arange(block_count)).astype(jnp.float32)
    carried_in = jnp.exp(-decay_rate[None] * block_offsets[:, None, None]) * incoming[None]
    conv = finish_conv(inside, states_before + carried_in, out_table)
    return (featured[0] * conv).astype(jnp.bfloat16)


def attention_mixer(attn_qkv, out_weight):
    rows = attn_qkv.shape[1]
    head_width = attn_qkv.shape[2]
    head_count = head_width // HEAD
    half_rows = rows // 2
    scale = 1.0 / HEAD**0.5
    my_index = lax.axis_index("ctx")
    own_queries = attn_qkv[0]
    queries = (own_queries[:half_rows], own_queries[half_rows:])
    firsts = (my_index * rows, my_index * rows + half_rows)
    empty = (
        jnp.full((head_count, half_rows), neg_large, jnp.float32),
        jnp.zeros((head_count, half_rows), jnp.float32),
        jnp.zeros((half_rows, head_count, HEAD), jnp.float32),
    )
    running = (empty, empty)
    pieces = lax.all_gather(attn_qkv[1:3], "ctx", axis=1, tiled=True)
    first_row = jnp.int32(0)
    key_rows = pieces[0].reshape(-1, head_count, HEAD)
    value_rows = pieces[1].reshape(-1, head_count, HEAD)
    key_positions = jnp.arange(key_rows.shape[0])
    results = []
    for attend_half_index in range(2):
        query_rows = queries[attend_half_index].reshape(half_rows, head_count, HEAD)
        query_positions = firsts[attend_half_index] + jnp.arange(half_rows)

        def update(state):
            maxima, totals, weighted = state
            scores = (
                jnp.einsum("rhd,nhd->hrn", query_rows, key_rows, preferred_element_type=jnp.float32)
                * scale
            )
            visible = key_positions[None, None, :] <= query_positions[None, :, None]
            row_max = jnp.max(jnp.where(visible, scores, neg_large), axis=-1)
            new_maxima = jnp.maximum(maxima, row_max)
            expo = jnp.where(visible, jnp.exp(scores - new_maxima[..., None]), 0.0)
            rescale = jnp.exp(maxima - new_maxima)
            new_totals = jnp.sum(expo, axis=-1)
            added = jnp.einsum(
                "hrn,nhd->rhd",
                expo.astype(jnp.bfloat16),
                value_rows,
                preferred_element_type=jnp.float32,
            )
            return (new_maxima, new_totals, weighted * rescale.T[:, :, None] + added)

        def unchanged(state):
            return state

        results.append(
            lax.cond(
                first_row <= firsts[attend_half_index] + half_rows - 1,
                update,
                unchanged,
                running[attend_half_index],
            )
        )
    folded = tuple(results)
    normalized = []
    for half_index in range(2):
        totals = folded[half_index][1]
        weighted = folded[half_index][2]
        normalized.append(
            (weighted / totals.T[:, :, None]).astype(jnp.bfloat16).reshape(half_rows, head_width)
        )
    attended = jnp.concatenate([normalized[0], normalized[1]], axis=0)
    terms = jnp.dot(
        attended,
        lax.all_gather(out_weight, "ctx", axis=1, tiled=True),
        preferred_element_type=jnp.float32,
    )
    return lax.psum_scatter(terms.astype(jnp.bfloat16), "tp", scatter_dimension=1, tiled=True)


def per_device(hyena_feats, short_taps, decay_rate, residue, attn_qkv, out_weight):
    hyena_mixed = long_mixer(hyena_feats, short_taps, decay_rate, residue)
    attn_mixed = attention_mixer(attn_qkv, out_weight)
    return (hyena_mixed, attn_mixed)


def solution(mesh):
    return jax.shard_map(
        per_device,
        mesh=mesh,
        in_specs=(
            P(None, "ctx", "tp"),
            P(None, None, "tp"),
            P(None, "tp"),
            P(None, "tp"),
            P(None, "ctx", "tp"),
            P("tp", "ctx"),
        ),
        out_specs=(P("ctx", "tp"), P("ctx", "tp")),
        check_vma=False,
    )
```

profile of v0, /device:TPU:38, one launch (start us, length us, event | category | flops | bytes accessed | tf_op | source)
XLA Modules:
  0.0 415.8 jit_solution(6190528040517112186)
XLA Ops:
  7.2 1.0 slice.58
  10.7 1.9 collective-permute-start
  12.6 1.6 sqrt_multiply_fusion
  14.2 0.9 fusion.62
  15.7 2.4 multiply_add_fusion
  18.2 2.6 copy.39
  20.8 11.1 %fusion.48 = f32[8,16,1024]{1,0,2:T(8,128)} fusion(f32[8,16,1024]{1,0,2:T(8,128)} %copy.39, f32[16]{0:T(128)S(1)} %broadcast_subtract_fusion, f32[16,1024]{0,1:T(8,128)S(1)} %copy.36), kind=kOutput, calls=%fused_computation.58 | convolution fusion | flops 25427968 | bytes 1114176 | tf_op jit(solution)/shard_map/src,nsc->nrc/dot_general | solution.py:50
  31.9 2.8 copy.41
  34.7 5.3 %while.26 = (s32[]{:T(128)}, f32[16,1024]{1,0:T(8,128)S(1)}, f32[8,16,1024]{2,1,0:T(8,128)}, f32[16,1024]{1,0:T(8,128)S(1)}, f32[8,16,1024]{2,1,0:T(8,128)S(1)}, /*index=5*/s32[]{:T(128)}, s32[]{:T(128)}) while((s32[]{:T(128)}, f32[16,1024]{1,0:T(8,128)S(1)}, f32[8,16,1024]{2,1,0:T(8,128)}, f32[16,1024]{1,0:T(8,128)S(1)}, ...), condition=%wide.region_2.3_spmd.clone, body=%wide.region_1.2_spmd.clone.sunk | while | flops 65539 | bytes 393820 | solution.py:59
  40.9 57.4 %all-gather.7.cloned.1.call-done = bf16[2,4096,512]{1,2,0:T(8,128)(2,1)} async-done(((bf16[2,128,512]{1,2,0:T(8,128)(2,1)}), bf16[2,4096,512]{1,2,0:T(8,128)(2,1)}) %all-gather.7.cloned.1.call-update) | async-done | bytes 8388624 | tf_op jit(solution)/shard_map/all_gather | solution.py:121
  98.4 6.0 %fusion.61 = (bf16[1,4096,512]{1,2,0:T(8,128)(2,1)}, bf16[1,4096,512]{1,2,0:T(8,128)(2,1)}) fusion(bf16[2,4096,512]{1,2,0:T(8,128)(2,1)} %all-gather.7.cloned.1.call-done), kind=kLoop, calls=%fused_computation.93 | loop fusion | bytes 16777216 | tf_op jit(solution)/shard_map/slice | solution.py:124
  104.4 7.6 %conditional.2 = (f32[4,64]{1,0:T(4,128)S(1)}, f32[64,4,128]{2,0,1:T(8,128)S(1)}) conditional(s32[]{:T(128)} %convert_element_type.63, () %tuple.37, (s32[4096]{0:T(1024)S(1)}, s32[]{:T(128)}, s32[64]{0:T(128)S(1)}, bf16[3,128,512]{2,1,0:T(8,128)(2,1)}, bf16[4096,4,128]{0,2,1:T(8,128)(2,1)}, /*index=5*/bf16[4096,4,128]{0,2,1:T(8,128)(2,1)}) %tuple.106), branch_computations={%region_5.6_spmd, %region_6.9_spmd} | conditional | flops 546603328 | bytes 39281456 | solution.py:155
  105.5 3.8 select_reduce_fusion
  109.3 1.7 fusion.10
  111.0 1.0 fusion.1
  112.0 7.6 %conditional.3 = (f32[4,64]{1,0:T(4,128)S(1)}, f32[64,4,128]{2,0,1:T(8,128)S(1)}) conditional(s32[]{:T(128)} %convert_element_type.65, () %tuple.39, (s32[4096]{0:T(1024)S(1)}, s32[]{:T(128)}, s32[64]{0:T(128)S(1)}, bf16[3,128,512]{2,1,0:T(8,128)(2,1)}, bf16[4096,4,128]{0,2,1:T(8,128)(2,1)}, /*index=5*/bf16[4096,4,128]{0,2,1:T(8,128)(2,1)}) %tuple.107), branch_computations={%region_9.10_spmd, %region_10.13_spmd.clone} | conditional | flops 546603328 | bytes 39281468 | solution.py:155
  113.1 3.8 select_reduce_fusion.1
  116.9 1.7 fusion.25
  118.6 1.0 fusion.16
  119.8 67.4 %all-gather.9.cloned.1.call-done = bf16[512,8192]{1,0:T(8,128)(2,1)} async-done(((bf16[512,256]{1,0:T(8,128)(2,1)}), bf16[512,8192]{1,0:T(8,128)(2,1)}) %all-gather.9.cloned.1.call-update) | async-done | bytes 8388624 | tf_op jit(solution)/shard_map/all_gather | solution.py:173
  187.2 6.0 %convolution_convert_fusion = bf16[128,8192]{1,0:T(8,128)(2,1)} fusion(bf16[512,8192]{1,0:T(8,128)(2,1)} %all-gather.9.cloned.1.call-done, bf16[64,512]{1,0:T(8,128)(2,1)S(1)} %get-tuple-element.239, bf16[64,512]{1,0:T(8,128)(2,1)S(1)} %get-tuple-element.240), kind=kOutput, calls=%fused_computation.39 | convolution fusion | flops 1075052544 | bytes 10616832 | tf_op jit(solution)/shard_map/dot_general | solution.py:171
  193.4 3.5 multiply_reduce_fusion
  197.2 2.0 gather_fusion
  199.2 7.0 %copy.38 = f32[16,16,1024]{1,0,2:T(8,128)} copy(f32[16,16,1024]{2,1,0:T(8,128)} %bitcast.81) | data formatting | bytes 2097152 | tf_op jit(solution)/shard_map/gather | solution.py:39
  206.3 42.8 %all-gather.11.cloned.1.call-done = f32[512,1024]{1,0:T(8,128)} async-done(((f32[16,1024]{1,0:T(8,128)}), f32[512,1024]{1,0:T(8,128)}) %all-gather.11.cloned.1.call-update) | async-done | bytes 2097168 | tf_op jit(solution)/shard_map/all_gather | solution.py:21
  249.0 60.9 %all-gather.13.cloned.1.call-done = f32[512,1024]{1,0:T(8,128)} async-done(((f32[16,1024]{1,0:T(8,128)}), f32[512,1024]{1,0:T(8,128)}) %all-gather.13.cloned.1.call-update) | async-done | bytes 2097168 | tf_op jit(solution)/shard_map/all_gather | solution.py:21
  309.9 24.2 %while.25 = (s32[]{:T(128)}, f32[16,1024]{1,0:T(8,128)S(1)}, s32[]{:T(128)}, f32[32,16,1024]{2,1,0:T(8,128)}, f32[32,16,1024]{2,1,0:T(8,128)}, /*index=5*/s32[]{:T(128)}, s32[]{:T(128)}, s32[]{:T(128)}) while((s32[]{:T(128)}, f32[16,1024]{1,0:T(8,128)S(1)}, s32[]{:T(128)}, f32[32,16,1024]{2,1,0:T(8,128)}, f32[32,16,1024]{2,1,0:T(8,128)}, ...), condition=%wide.region_4.5_spmd, body=%wide.region_3.4_spmd.sunk | while | flops 32773 | bytes 262267 | solution.py:29
  310.8 0.9 bitcast_add_fusion.4
  311.8 0.9 bitcast_add_fusion.4
  312.7 0.9 bitcast_add_fusion.4
  313.6 0.9 bitcast_add_fusion.4
  314.6 0.9 bitcast_add_fusion.4
  315.5 0.9 bitcast_add_fusion.4
  316.4 0.9 bitcast_add_fusion.4
  317.3 0.9 bitcast_add_fusion.4
  318.3 0.9 bitcast_add_fusion.4
  319.2 0.9 bitcast_add_fusion.4
  320.1 0.9 bitcast_add_fusion.4
  321.1 0.9 bitcast_add_fusion.4
  322.0 0.9 bitcast_add_fusion.4
  325.7 0.9 bitcast_add_fusion.4
  326.6 0.9 bitcast_add_fusion.4
  334.1 1.2 multiply_add_fusion.1
  335.3 2.6 copy.42
  337.9 16.0 %fusion.30 = f32[1024,8,16]{2,1,0:T(8,128)S(1)} fusion(f32[8,16,1024]{1,0,2:T(8,128)} %copy.42, f32[16]{0:T(128)S(1)} %broadcast_add_fusion.2, f32[16,1024]{0,1:T(8,128)S(1)} %copy.36, f32[16,1024]{0,1:T(8,128)S(1)} %copy.35), kind=kOutput, calls=%fused_computation.40 | convolution fusion | flops 25690112 | bytes 1179712 | tf_op jit(solution)/shard_map/trc,nrc->ntc/dot_general | solution.py:66
  353.9 16.6 %add_bitcast_fusion = f32[8,16,1024]{1,0,2:T(8,128)} fusion(f32[1024,8,16]{2,1,0:T(8,128)S(1)} %fusion.30, f32[8,16,1024]{1,0,2:T(8,128)S(1)} %copy-done, f32[16,16,1024]{1,0,2:T(8,128)} %copy.38, pred[16,16]{1,0:T(8,128)(4,1)S(1)} %iota_compare_fusion), kind=kOutput, calls=%fused_computation.50 | convolution fusion | flops 25559040 | bytes 2621696 | tf_op jit(solution)/shard_map/tsc,nsc->ntc/dot_general | solution.py:49
  370.5 2.8 copy.43
  374.1 35.1 %reduce-scatter.2.cloned.1.call-done = bf16[128,1024]{1,0:T(8,128)(2,1)} async-done(((bf16[128,8192]{1,0:T(8,128)(2,1)}), bf16[128,1024]{1,0:T(8,128)(2,1)}) %reduce-scatter.2.cloned.1.call-update) | async-done | bytes 262160 | tf_op jit(solution)/shard_map/reduce_scatter | solution.py:176
  (79 shorter events, 22.7 us)
Async XLA Ops:
  7.2 91.2 %all-gather.7.cloned.1.call-start = ((), (), s32[]{:S(2)}) async-start(), calls=%async_computation.1 | async-start | bytes 8650752 | tf_op jit(solution)/shard_map/all_gather | solution.py:121
  9.0 178.1 %all-gather.9.cloned.1.call-start = ((), (), s32[]{:S(2)}) async-start(), calls=%async_computation.2 | async-start | bytes 8650752 | tf_op jit(solution)/shard_map/all_gather | solution.py:173
  9.8 239.2 %all-gather.11.cloned.1.call-start = ((), (), s32[]{:S(2)}) async-start(), calls=%async_computation.4 | async-start | bytes 2162688 | tf_op jit(solution)/shard_map/all_gather | solution.py:21
  10.7 5.0 %collective-permute-start = (bf16[3,2,1024]{2,1,0:T(2,128)(2,1)S(1)}, bf16[3,2,1024]{2,1,0:T(2,128)(2,1)S(1)}, u32[]{:S(2)}, u32[]{:S(2)}) collective-permute-start(bf16[3,2,1024]{2,1,0:T(2,128)(2,1)S(1)} %slice.51), channel_id=1, source_target_pairs={{0,8},{8,16},{16,24},{24,32},{32,40},{40,48},{48,56},{56,64},{64,7... | collective-permute-start | bytes 36872 | tf_op jit(solution)/shard_map/ppermute | solution.py:16
  14.2 295.7 %all-gather.13.cloned.1.call-start = ((), (), s32[]{:S(2)}) async-start(), calls=%async_computation.5 | async-start | bytes 2162688 | tf_op jit(solution)/shard_map/all_gather | solution.py:21
  40.1 0.6 copy-start.3
  40.7 368.6 %reduce-scatter.2.cloned.1.call-start = ((), (), s32[]{:S(2)}) async-start(), calls=%async_computation.3 | async-start | bytes 2359296 | tf_op jit(solution)/shard_map/reduce_scatter | solution.py:176
  105.5 3.8 copy-start.1
  113.1 3.8 copy-start.2
  337.9 16.0 %copy-start = (f32[8,16,1024]{1,0,2:T(8,128)S(1)}, f32[8,16,1024]{1,0,2:T(8,128)}, u32[]{:S(2)}) copy-start(f32[8,16,1024]{1,0,2:T(8,128)} %copy.39) | copy-start | bytes 1572868
Sparse Core Ops, SparseCore 0:
  10.3 87.9 all-gather.6
  100.1 86.9 all-gather.8
  189.6 59.3 all-gather.10
  250.7 59.1 all-gather.12
  314.4 94.8 reduce-scatter.1
where the time goes:
time: 419 us; the launch traced here: 416 us
  waiting for transfers between devices  265 us (63%)
  matrix products  60.6 us (14%)
  other arithmetic  40.9 us (10%)
  local copies, waits for them, and re-layouts  32.6 us (8%)
  between operations  14 us (3%)
    all_gather x2, waiting for transfers between devices, prefix_2(): gathered = jax.tree.map(lambda a: lax.all_gather(a, axis), part)  104 us
    all_gather x1, waiting for transfers between devices, attention_mixer(): lax.all_gather(out_weight, 'ctx', axis=1, tiled=True)  67.4 us
    all_gather x1, waiting for transfers between devices, attention_mixer(): pieces = lax.all_gather(attn_qkv[1:3], 'ctx', axis=1, tiled=True)  57.4 us
    reduce_scatter x1, waiting for transfers between devices, attention_mixer(): lax.psum_scatter(terms.astype(jnp.bfloat16), 'tp', scatter_dimension=1, t...  35.1 us
    add x26, other arithmetic, combine_states(): return (earlier[0] * later[0], earlier[1] * later[0] + later[1])  23.6 us
    dot_general x1, matrix products, block_terms(): jnp.einsum('tsc,nsc->ntc', toeplitz, sub_blocks, precision=lax.Precision....  16.6 us
    dot_general x1, matrix products, finish_conv(): jnp.einsum('trc,nrc->ntc', out_table, states_before, precision=lax.Precis...  16 us
    dot_general x1, matrix products, block_terms(): jnp.einsum('src,nsc->nrc', end_table, sub_blocks, precision=lax.Precision...  11.1 us
  transfers between devices with their start and end apart: 6, of which 6 were waited for; matrix products, arithmetic and copies ran while one was open for 32% of the time, Pallas kernels for 0%

commit v1 on v0

v1 whole, which is shorter than its diff:
```python
import math

import jax
import jax.numpy as jnp
from jax import lax
from jax.experimental import pallas as pl
from jax.experimental.pallas import tpu as pltpu
from jax.sharding import Mesh, PartitionSpec as P

HEAD = 128
NX, NZ1, NZ0, NK, NY, NH = 4, 2, 2, 2, 4, 2
NZ = NZ1 * NZ0
ALL = ("x", "z1", "z0", "k", "y", "h")
SIZES = dict(x=NX, z1=NZ1, z0=NZ0, k=NK, y=NY, h=NH)
SCALE = math.log2(math.e) / math.sqrt(HEAD)
VMEM = 48 * 1024 * 1024


def linear(**c):
    index = 0
    for name in ALL:
        index = index * SIZES[name] + c[name]
    return index


def places():
    for index in range(256):
        rest, c = index, {}
        for name in reversed(ALL):
            c[name] = rest % SIZES[name]
            rest //= SIZES[name]
        yield c


def moved(change):
    pairs = []
    for c in places():
        d = change(**c)
        if d is not None:
            pairs.append((linear(**c), linear(**dict(c, **d))))
    return pairs


def next_ctx(x, z1, z0, k, **_):
    place = ((x * NZ1 + z1) * NZ0 + z0) * NK + k + 1
    if place == NX * NZ * NK:
        return None
    return dict(x=place // (NZ * NK), z1=place // 4 % 2, z0=place // 2 % 2, k=place % 2)


def along_z(steps):
    def change(z1, z0, **_):
        z = (2 * z1 + z0 + steps) % NZ
        return dict(z1=z // 2, z0=z % 2)

    return moved(change)


def place_weight(x, z1, z0, k, y, h):
    return dict(x=(x + y) % NX, z1=h, z0=z0, k=k, y=x, h=z1)


SMEM = pl.BlockSpec(memory_space=pltpu.SMEM)
FAST = pl.BlockSpec(memory_space=pltpu.VMEM)
SLOW = pl.BlockSpec(memory_space=pltpu.HBM)
ANY = pl.BlockSpec(memory_space=pl.ANY)


def local_call(kernel, out_shape, specs, name, flops, scratch=(), after=()):
    count = len(specs)

    def body(*refs):
        kernel(*refs[:count], *refs[count + len(after) :])

    call = pl.pallas_call(
        body,
        out_shape=out_shape,
        in_specs=list(specs) + [ANY] * len(after),
        out_specs=jax.tree.map(lambda _: FAST, out_shape),
        scratch_shapes=list(scratch),
        compiler_params=pltpu.CompilerParams(vmem_limit_bytes=VMEM),
        cost_estimate=pl.CostEstimate(flops=flops, bytes_accessed=2_000_000, transcendentals=0),
        name=name,
    )

    def placed(operand, spec):
        return pltpu.with_memory_space_constraint(operand, pltpu.HBM) if spec is SLOW else operand

    return lambda *operands: call(*map(placed, operands, specs), *after)


def gate(value, *after):
    return pl.pallas_call(
        lambda *refs: None,
        out_shape=jax.ShapeDtypeStruct(value.shape, value.dtype),
        in_specs=[ANY] * (1 + len(after)),
        out_specs=ANY,
        input_output_aliases={0: 0},
        name="gate",
    )(value, *after)


def started(sems, pairs):
    copies = [pltpu.make_async_copy(a, b, sems.at[i]) for i, (a, b) in enumerate(pairs)]
    for copy in copies:
        copy.start()
    return copies


def finished(copies):
    for copy in copies:
        copy.wait()


def fill_ext(x, halo_ref, ext, streams):
    for slot, stream in enumerate(streams):
        ext[slot, 6:8] = halo_ref[stream]
        for lo in range(0, x.shape[1], 32):
            ext[slot, lo + 8 : lo + 40] = x[slot, lo : lo + 32].astype(jnp.float32)


def featured_rows(ext, taps_ref, slot, stream, lo, rows):
    taps = taps_ref[stream]
    total = taps[0:1] * ext[slot, lo + 8 : lo + 8 + rows]
    for j in (1, 2):
        total += taps[j : j + 1] * ext[slot, lo + 8 - j : lo + 8 - j + rows]
    return total


def ends_kernel(
    feats, halo_ref, taps_hbm, decay_hbm, out_ref, prod, gate_rows, rate, x, taps, ext, sems
):
    finished(started(sems, ((feats, x), (taps_hbm, taps), (decay_hbm, rate))))
    rows, order = x.shape[1], rate.shape[0]
    fill_ext(x, halo_ref, ext, (0, 1, 2))
    for lo in range(0, rows, 16):
        gate_rows[lo : lo + 16] = featured_rows(ext, taps, 0, 0, lo, 16)
        first = featured_rows(ext, taps, 1, 1, lo, 16)
        prod[lo : lo + 16] = first * featured_rows(ext, taps, 2, 2, lo, 16)
    decay = jnp.exp(-rate[...])

    def body(i, state):
        block = prod[pl.ds(pl.multiple_of(i * 8, 8), 8), :]
        for j in range(8):
            state = decay * state + block[j : j + 1]
        return state

    state = lax.fori_loop(0, rows // 8, body, jnp.zeros(rate.shape, jnp.float32))
    for j in range(state.shape[1] // HEAD):
        block = state[:, j * HEAD : (j + 1) * HEAD]
        high = block.astype(jnp.bfloat16)
        out_ref[0, j * order : (j + 1) * order] = high
        out_ref[1, j * order : (j + 1) * order] = (block - high.astype(jnp.float32)).astype(
            jnp.bfloat16
        )


def combine_kernel(place_ref, decay_ref, own_ref, other_ref, out_ref, ends):
    x, z, k = place_ref[0], place_ref[1], place_ref[2]
    rate = decay_ref[...]
    order = rate.shape[0]

    def over(blocks):
        return jnp.exp(rate * (-128.0 * jnp.maximum(blocks, 0).astype(jnp.float32)))

    for row in range(NX):
        for side, ref in enumerate((own_ref, other_ref)):
            both = ref[row, 2 * NZ].astype(jnp.float32) + ref[row, 2 * NZ + 1].astype(jnp.float32)
            for j in range(rate.shape[1] // HEAD):
                lanes = slice(j * HEAD, (j + 1) * HEAD)
                ends[row, side, :, lanes] = both[j * order : (j + 1) * order]

    def end_of(row, core):
        return ends[row, jnp.where(k == core, 0, 1)]

    step, across, rest = over(jnp.int32(1)), over(jnp.int32(NZ * NK)), over(NZ * NK - NK * z - NK)
    earlier = jnp.zeros(rate.shape, jnp.float32)
    for row in range(NX - 1):
        whole = rest * (step * end_of(row, 0) + end_of(row, 1))
        earlier = jnp.where(x > row, across * earlier + whole, earlier)
    for target in range(NZ):
        total = over(NK * target + k) * earlier
        for core in range(NK):
            blocks = (NK * target + k) - (NK * z + core) - 1
            total = total + jnp.where(blocks >= 0, over(blocks) * end_of(x, core), 0.0)
        out_ref[target] = total


def mix_kernel(decay_ref, rho_ref, parts_ref, prod, gate_rows, out_ref):
    rows, width = prod.shape
    decay = jnp.exp(-decay_ref[...])
    start = parts_ref[0]
    for z in range(1, NZ):
        start = start + parts_ref[z]
    rho = rho_ref[...]
    sub = lax.broadcasted_iota(jnp.int32, (8, width), 0)

    def body(i, state):
        base = pl.multiple_of(i * 16, 16)
        mixed = []
        for half in range(2):
            block = prod[pl.ds(base + 8 * half, 8), :]
            conv = jnp.zeros((8, width), jnp.float32)
            for j in range(8):
                state = decay * state + block[j : j + 1]
                row = jnp.sum(rho * state, axis=0, keepdims=True)
                conv = jnp.where(sub == j, row, conv)
            mixed.append(conv * gate_rows[pl.ds(base + 8 * half, 8), :])
        out_ref[pl.ds(base, 16), :] = jnp.concatenate(mixed, axis=0).astype(jnp.bfloat16)
        return state

    lax.fori_loop(0, rows // 16, body, start)


def pack_kernel(qkv, feats, out_ref, halo_ref, tail, sems):
    rows = qkv.shape[1]
    pairs = [(feats.at[:, pl.ds(rows - 16, 16), :], tail)]
    for head in range(NZ):
        lanes = pl.ds(head * HEAD, HEAD)
        pairs += [(qkv.at[i, :, lanes], out_ref.at[head, i]) for i in range(3)]
    finished(started(sems, pairs))
    halo_ref[...] = tail[:, 14:16].astype(jnp.float32)


def halves_kernel(place_ref, weight_ref, same_ref, other_ref):
    for half in range(NZ0):

        @pl.when(place_ref[0] % NZ0 == half)
        def _():
            for ref, z0 in ((same_ref, half), (other_ref, 1 - half)):
                for part in range(NZ1):
                    lo = (2 * part + z0) * HEAD
                    ref[part] = weight_ref[lo : lo + HEAD]


def stack_kernel(place_ref, *refs):
    for steps, ref in enumerate(refs[:-1]):
        refs[-1][(place_ref[0] + NZ - steps) % NZ] = ref[...]


def spread_kernel(qkv_ref, ends_ref, kv_ref, out_ref):
    for z in range(NZ):
        kv_ref[z] = qkv_ref[z, 1:]
        for i in range(out_ref.shape[0]):
            out_ref[i, 2 * z : 2 * z + 2] = qkv_ref[z, 1:]
    for i in range(out_ref.shape[0]):
        out_ref[i, 2 * NZ :] = ends_ref[...]


def folded(q, sets, top, total, acc, visible=None):
    keys = jnp.concatenate([a[:, 0].reshape(-1, HEAD) for a in sets], axis=0)
    values = jnp.concatenate([a[:, 1].reshape(-1, HEAD) for a in sets], axis=0)
    s = lax.dot_general(keys, q, (((1,), (1,)), ((), ())), preferred_element_type=jnp.float32)
    if visible is not None:
        s = jnp.where(visible, s, -1e30)
    new = jnp.maximum(top, jnp.max(s, axis=0, keepdims=True))
    p = jnp.exp2((s - new) * SCALE)
    again = jnp.exp2((top - new) * SCALE)
    added = jnp.dot(values.T, p.astype(jnp.bfloat16), preferred_element_type=jnp.float32)
    return new, total * again + jnp.sum(p, axis=0, keepdims=True), acc * again + added


def near_kernel(place_ref, qkv_ref, a, b, top_ref, total_ref, acc_ref):
    k = place_ref[1]
    rows = NZ * HEAD
    col = lax.broadcasted_iota(jnp.int32, (1, rows), 1)
    row = lax.broadcasted_iota(jnp.int32, (2 * rows, 1), 0)
    core = jnp.where(row < rows, k, 1 - k)
    here = (2 * (col // HEAD) + k) * HEAD + col % HEAD
    there = (2 * ((row % rows) // HEAD) + core) * HEAD + row % HEAD
    lowest = jnp.full((1, rows), -1e30, jnp.float32)
    top_ref[...], total_ref[...], acc_ref[...] = folded(
        qkv_ref[:, 0].reshape(rows, HEAD),
        (a[...], b[...]),
        lowest,
        jnp.zeros((1, rows), jnp.float32),
        jnp.zeros((HEAD, rows), jnp.float32),
        there <= here,
    )


def pairs_of(ref, row):
    return ref[row, 0 : 2 * NZ].reshape(NZ, 2, HEAD, HEAD)


def far_kernel(
    place_ref, qkv_ref, top_ref, total_ref, acc_ref, a_ref, b_ref, out_ref, top, total, acc
):
    q = qkv_ref[:, 0].reshape(NZ * HEAD, HEAD)
    top[...], total[...], acc[...] = top_ref[...], total_ref[...], acc_ref[...]
    for row in range(NX - 1):

        @pl.when(place_ref[0] > row)
        def _():
            top[...], total[...], acc[...] = folded(
                q, (pairs_of(a_ref, row), pairs_of(b_ref, row)), top[...], total[...], acc[...]
            )

    result = (acc[...] / total[...]).T.astype(jnp.bfloat16).reshape(out_ref.shape[1:])
    for h in range(NH):
        out_ref[h] = result


def project_kernel(place_ref, g0, g1, g2, g3, w_hbm, mine_ref, other_ref, held, parts, acc, sems):
    y, z0 = place_ref[0], place_ref[1]
    copies = started(sems, [(w_hbm.at[i], parts.at[i]) for i in range(NX)])
    for step, group in zip((0, 1, 3, 2), (g0, g1, g2, g3)):
        held[step] = group[...]
    for i in range(NX):
        step = (2 * y - i + NX) % NX
        heads = jnp.concatenate([held[step, j] for j in range(NH * NZ1)], axis=1)
        copies[i].wait()
        for k in range(NK):
            for b in range(2):
                columns = [parts[i, k, 2 * h + b].reshape(2 * HEAD, 256) for h in range(NH)]
                term = jnp.dot(
                    heads, jnp.concatenate(columns, axis=0), preferred_element_type=jnp.float32
                )
                lanes = slice(b * 256, b * 256 + 256)
                if i == 0:
                    acc[k, :, lanes] = term
                else:
                    acc[k, :, lanes] += term
    rows = mine_ref.shape[0]
    near_rows = pl.ds(pl.multiple_of(z0 * rows, rows), rows)
    far_rows = pl.ds(pl.multiple_of((1 - z0) * rows, rows), rows)
    for b in range(2):
        for k in range(NK):
            lo = (2 * b + k) * 256
            lanes = slice(b * 256, b * 256 + 256)
            mine_ref[:, lo : lo + 256] = acc[k, near_rows, lanes]
            other_ref[:, lo : lo + 256] = acc[k, far_rows, lanes].astype(jnp.bfloat16)


def per_device(hyena_feats, short_taps, decay_rate, residue, attn_qkv, out_weight):
    rows, width = hyena_feats.shape[1:]
    x, k, y = lax.axis_index("x"), lax.axis_index("k"), lax.axis_index("y")
    z1, z0 = lax.axis_index("z1"), lax.axis_index("z0")
    swap = [(0, 1), (1, 0)]
    short = jax.ShapeDtypeStruct
    bf16, f32 = jnp.bfloat16, jnp.float32
    dma = pltpu.SemaphoreType.DMA

    packed, tail = local_call(
        pack_kernel,
        (short((NZ, 3, rows, HEAD), bf16), short((3, 2, width), f32)),
        (SLOW, SLOW),
        "pack",
        10**8,
        (pltpu.VMEM((3, 16, width), bf16), dma((1 + 3 * NZ,))),
    )(attn_qkv, hyena_feats)
    qkv = lax.all_to_all(packed, ("z1", "z0"), 0, 0)
    halo = lax.ppermute(tail, ALL, moved(next_ctx))
    plane = short((rows, width), f32)
    poles = short(decay_rate.shape, f32)
    ends, prod, gate_rows, rate = local_call(
        ends_kernel,
        (short((2, rows, HEAD), bf16), plane, plane, poles),
        (SLOW, FAST, SLOW, SLOW),
        "ends",
        10**9,
        (
            pltpu.VMEM((3, rows, width), bf16),
            pltpu.VMEM(short_taps.shape, f32),
            pltpu.VMEM((3, rows + 8, width), f32),
            dma((3,)),
        ),
    )(hyena_feats, halo, short_taps, decay_rate)
    moved_weight = lax.ppermute(out_weight, ALL, moved(place_weight))
    kv, spread = local_call(
        spread_kernel,
        (short((NZ, 2, rows, HEAD), bf16), short((NX, 2 * NZ + 2, rows, HEAD), bf16)),
        (FAST, FAST),
        "spread",
        10**8,
        after=(moved_weight,),
    )(qkv, ends)
    near = lax.ppermute(kv, "k", swap)
    far_own = lax.all_to_all(spread, "x", 0, 0)
    far_other = lax.ppermute(far_own, "k", swap)

    z = (2 * z1 + z0).reshape(1)
    half = short((NZ1, HEAD, out_weight.shape[1]), bf16)
    same, opposite = local_call(
        halves_kernel, (half, half), (SMEM, FAST), "halves", 10**8, after=(spread,)
    )(z, moved_weight)
    arrived = [same] + [
        lax.ppermute(opposite if steps % 2 else same, ALL, along_z(steps)) for steps in (1, 2, 3)
    ]
    placed = local_call(
        stack_kernel, short((NZ, *half.shape), bf16), (SMEM,) + (FAST,) * NZ, "stack", 10**8,
        after=(far_own,),
    )(z, *arrived)
    weight = lax.all_gather(placed, ("x", "k")).reshape(NX, NK, *placed.shape)

    where = jnp.stack([x, k])
    line = short((1, NZ * rows), f32)
    square = short((HEAD, NZ * rows), f32)
    partial = local_call(
        near_kernel, (line, line, square), (SMEM, FAST, FAST, FAST), "near", 2 * 10**9
    )(where, qkv, kv, near)
    attended = local_call(
        far_kernel,
        short((NH, NZ1, NZ0 * rows, HEAD), bf16),
        (SMEM,) + (FAST,) * 6,
        "far",
        4 * 10**9,
        [pltpu.VMEM(part.shape, f32) for part in (line, line, square)],
    )(where, qkv, *partial, far_own, far_other)
    group = lax.all_to_all(attended.reshape(NH * NZ1, NZ0 * rows, HEAD), ("h", "z1"), 0, 0)
    groups = [group] + [
        lax.ppermute(group, "y", [(i, (i + step) % NY) for i in range(NY)]) for step in (1, 3, 2)
    ]

    parts = local_call(
        combine_kernel,
        short((NZ, *poles.shape), f32),
        (SMEM, FAST, FAST, FAST),
        "combine",
        10**8,
        (pltpu.VMEM((NX, NK, *poles.shape), f32),),
        after=(group,),
    )(jnp.stack([x, 2 * z1 + z0, k]), rate, far_own, far_other)
    parts = lax.all_to_all(parts, ("z1", "z0"), 0, 0)

    mine, other = local_call(
        project_kernel,
        (short((rows, width), f32), short((rows, width), bf16)),
        (SMEM,) + (FAST,) * 4 + (SLOW,),
        "project",
        2 * 10**9,
        (
            pltpu.VMEM((NY, *group.shape), bf16),
            pltpu.VMEM(weight.shape, bf16),
            pltpu.VMEM((NK, NZ0 * rows, width // 2), f32),
            dma((NX,)),
        ),
    )(jnp.stack([y, z0]), *groups, weight)
    received = lax.ppermute(other, "z0", swap)

    rho = residue * jnp.sqrt(-jnp.expm1(-2.0 * rate) / rate.shape[0])
    hyena_mixed = local_call(
        mix_kernel,
        short((rows, width), bf16),
        (FAST,) * 5,
        "mix",
        4 * 10**9,
    )(rate, rho, parts, prod, gate_rows)
    return hyena_mixed, (mine + received.astype(f32)).astype(bf16)


def solution(mesh):
    fine = Mesh(mesh.devices.reshape(NX, NZ1, NZ0, NK, NY, NH), ALL)
    ctx, tp = ("x", "z1", "z0", "k"), ("y", "h")
    return jax.shard_map(
        per_device,
        mesh=fine,
        in_specs=(
            P(None, ctx, tp),
            P(None, None, tp),
            P(None, tp),
            P(None, tp),
            P(None, ctx, tp),
            P(tp, ctx),
        ),
        out_specs=(P(ctx, tp), P(ctx, tp)),
        check_vma=False,
    )
```

time: 419 us -> 118 us (0.28)
  waiting for transfers between devices: 265 us -> 32.4 us
  matrix products: 60.6 us -> 0 us
  starting transfers between devices: 2.3 us -> 48 us
  other arithmetic: 40.9 us -> 1.05 us
  local copies, waits for them, and re-layouts: 32.6 us -> 0.82 us
  Pallas kernels: 0 us -> 21.2 us
    all_gather x4 -> x1, waiting for transfers between devices: 228 us -> 0.01 us  [per_device(): weight = lax.all_gather(placed, ('x', 'k')).reshape(NX, NK, *placed.shape)]
    dot_general x8 -> x0, matrix products: 60.6 us -> none  [the longest x1 16.6 us: block_terms(): jnp.einsum('tsc,nsc->ntc', toeplitz, sub_blocks, precision=lax.Precision....]
    reduce_scatter x1 -> x0, waiting for transfers between devices: 35.1 us -> none  [attention_mixer(): lax.psum_scatter(terms.astype(jnp.bfloat16), 'tp', scatter_dimension=1, t...]
    add x39 -> x0, other arithmetic: 27.4 us -> none  [the longest x26 23.6 us: combine_states(): return (earlier[0] * later[0], earlier[1] * later[0] + later[1])]
    all_to_all x0 -> x4, starting transfers between devices: none -> 25.1 us  [the longest x1 10.1 us: per_device(): lax.all_to_all(attended.reshape(NH * NZ1, NZ0 * rows, HEAD), ('h', 'z1'),...]
    ppermute x1 -> x11, waiting for transfers between devices: 0.24 us -> 22.1 us  [the longest x3 7.92 us: per_device(): lax.ppermute(opposite if steps % 2 else same, ALL, along_z(steps))]
    pallas_call x0 -> x10, Pallas kernels: none -> 21.2 us  [local_call(): return lambda *operands: call(*map(placed, operands, specs), *after)]
    ppermute x1 -> x11, starting transfers between devices: 1.92 us -> 22.9 us  [the longest x3 11.4 us: per_device(): lax.ppermute(opposite if steps % 2 else same, ALL, along_z(steps))]
  transfers between devices with their start and end apart: 6 -> 16, of which waited for: 6 -> 9; matrix products, arithmetic and copies ran while one was open for 32% -> 0% of each run, Pallas kernels for 0% -> 15%
where the time goes in v1:
time: 118 us
  starting transfers between devices  48 us (41%)
  waiting for transfers between devices  32.4 us (27%)
  Pallas kernels  21.2 us (18%)
  between operations  14.2 us (12%)
    pallas_call x10, Pallas kernels, local_call(): return lambda *operands: call(*map(placed, operands, specs), *after)  21.2 us
    ppermute x3, starting transfers between devices, per_device(): lax.ppermute(opposite if steps % 2 else same, ALL, along_z(steps))  11.4 us
    all_to_all x1, waiting for transfers between devices, per_device(): lax.all_to_all(attended.reshape(NH * NZ1, NZ0 * rows, HEAD), ('h', 'z1'),...  10.2 us
    all_to_all x1, starting transfers between devices, per_device(): lax.all_to_all(attended.reshape(NH * NZ1, NZ0 * rows, HEAD), ('h', 'z1'),...  10.1 us
    ppermute x3, waiting for transfers between devices, per_device(): lax.ppermute(opposite if steps % 2 else same, ALL, along_z(steps))  7.92 us
    all_to_all x1, starting transfers between devices, per_device(): qkv = lax.all_to_all(packed, ('z1', 'z0'), 0, 0)  6.01 us
    all_to_all x1, starting transfers between devices, per_device(): far_own = lax.all_to_all(spread, 'x', 0, 0)  4.95 us
    ppermute x1, starting transfers between devices, per_device(): moved_weight = lax.ppermute(out_weight, ALL, moved(place_weight))  4.91 us
  transfers between devices with their start and end apart: 16, of which 9 were waited for; matrix products, arithmetic and copies ran while one was open for 0% of the time, Pallas kernels for 15%

profile of v1, /device:TPU:38, one launch (start us, length us, event | category | flops | bytes accessed | tf_op | source)
XLA Modules:
  0.0 117.7 jit_solution(7561895174546190709)
XLA Ops:
  7.2 0.0 copy-start.5
  7.2 1.9 %pack.1 = (bf16[4,3,128,128]{3,2,1,0:T(8,128)(2,1)}, f32[3,2,1024]{2,1,0:T(2,128)S(1)}) custom-call(bf16[3,128,512]{2,1,0:T(8,128)(2,1)} %refs_0_.2, bf16[3,128,1024]{2,1,0:T(8,128)(2,1)} %refs_0_.3), custom_call_target="tpu_custom_call" | custom-call | flops 100000000 | bytes 2000000 | tf_op jit(solution)/shard_map/pack/pallas_call | solution.py:89
  9.1 6.0 %all-to-all-start = ((bf16[4,3,128,128]{3,2,1,0:T(8,128)(2,1)}), bf16[4,3,128,128]{3,2,1,0:T(8,128)(2,1)S(1)}, u32[]{:S(2)}, u32[]{:S(2)}) async-start(bf16[4,3,128,128]{3,2,1,0:T(8,128)(2,1)} %get-tuple-element.19), calls=%async_computation | async-start | bytes 786432 | tf_op jit(solution)/shard_map/all_to_all | solution.py:352
  15.1 0.0 copy-done.5
  15.1 4.9 %collective-permute-start.1 = (bf16[512,256]{1,0:T(8,128)(2,1)S(1)}, bf16[512,256]{1,0:T(8,128)(2,1)S(1)}, u32[]{:S(2)}, u32[]{:S(2)}) collective-permute-start(bf16[512,256]{1,0:T(8,128)(2,1)S(1)} %copy-done.5), channel_id=1, source_target_pairs={{0,0},{1,32},{2,64},{3,96},{4,128},{5,160},{6,192},{7,224},{8,8},{... | collective-permute-start | bytes 786440 | tf_op jit(solution)/shard_map/ppermute | solution.py:369
  20.0 1.9 %collective-permute-start = (f32[3,2,1024]{2,1,0:T(2,128)S(1)}, f32[3,2,1024]{2,1,0:T(2,128)S(1)}, u32[]{:S(2)}, u32[]{:S(2)}) collective-permute-start(f32[3,2,1024]{2,1,0:T(2,128)S(1)} %get-tuple-element.17), channel_id=1, source_target_pairs={{0,8},{1,9},{2,10},{3,11},{4,12},{5,13},{6,14},{7,15},{8,16},{9,17... | collective-permute-start | bytes 73736 | tf_op jit(solution)/shard_map/ppermute | solution.py:353
  21.9 3.2 %collective-permute-done.refs_1_ = f32[3,2,1024]{2,1,0:T(2,128)S(1)} collective-permute-done((f32[3,2,1024]{2,1,0:T(2,128)S(1)}, f32[3,2,1024]{2,1,0:T(2,128)S(1)}, u32[]{:S(2)}, u32[]{:S(2)}) %collective-permute-start) | collective-permute-done | bytes 24608 | tf_op jit(solution)/shard_map/ppermute | solution.py:353
  25.1 2.5 %ends.1 = (bf16[2,128,128]{2,1,0:T(8,128)(2,1)S(1)}, f32[128,1024]{1,0:T(8,128)S(1)}, f32[128,1024]{1,0:T(8,128)S(1)}, f32[16,1024]{1,0:T(8,128)S(1)}) custom-call(bf16[3,128,1024]{2,1,0:T(8,128)(2,1)} %refs_0_.3, f32[3,2,1024]{2,1,0:T(2,128)S(1)} %collective-permute-done.refs_1_, f32[3,3,1024]{2,1,0:T(4,128)} %refs_2_.1, f32[16,1024]{1,0:T(8,128)} %refs_3_.1), custom_call_target="tpu_custom_call" | custom-call | flops 1000000000 | bytes 2000000 | tf_op jit(solution)/shard_map/ends/pallas_call | solution.py:89
  27.7 0.8 copy-done
  28.5 0.0 collective-permute-done.1.refs_2_.refs_1_
  28.5 0.0 all-to-all-done.refs_0_.refs_1_
  28.5 1.3 %spread.1 = (bf16[4,2,128,128]{3,2,1,0:T(8,128)(2,1)S(1)}, bf16[4,10,128,128]{3,2,1,0:T(8,128)(2,1)}) custom-call(bf16[4,3,128,128]{3,2,1,0:T(8,128)(2,1)S(1)} %all-to-all-done.refs_0_.refs_1_, bf16[2,128,128]{2,1,0:T(8,128)(2,1)S(1)} %get-tuple-element.20.refs_1_, bf16[512,256]{1,0:T(8,128)(2,1)S(1)} %collective-permute-done.1.refs_2_.refs_1_), custom_call_target="tpu_custom_call" | custom-call | flops 100000000 | bytes 2000000 | tf_op jit(solution)/shard_map/spread/pallas_call | solution.py:89
  29.7 0.0 copy-done.2
  29.8 4.9 %all-to-all-start.1 = ((bf16[4,10,128,128]{3,2,1,0:T(8,128)(2,1)}), bf16[4,10,128,128]{3,2,1,0:T(8,128)(2,1)S(1)}, u32[]{:S(2)}, u32[]{:S(2)}) async-start(bf16[4,10,128,128]{3,2,1,0:T(8,128)(2,1)} %get-tuple-element.21.refs_2_), calls=%async_computation.1 | async-start | bytes 2621440 | tf_op jit(solution)/shard_map/all_to_all | solution.py:379
  34.7 9.9 %collective-permute-start.7 = (bf16[2,128,256]{2,1,0:T(8,128)(2,1)S(1)}, bf16[2,128,256]{2,1,0:T(8,128)(2,1)S(1)}, u32[]{:S(2)}, u32[]{:S(2)}) collective-permute-start(bf16[2,128,256]{2,1,0:T(8,128)(2,1)S(1)} %get-tuple-element.29), channel_id=1, source_target_pairs={{0,16},{1,17},{2,18},{3,19},{4,20},{5,21},{6,22},{7,23},{8,24},{9,... | collective-permute-start | bytes 393224 | tf_op jit(solution)/shard_map/ppermute | solution.py:388
  44.6 0.0 collective-permute-start.8
  44.6 1.6 %collective-permute-start.9 = (bf16[2,128,256]{2,1,0:T(8,128)(2,1)S(1)}, bf16[2,128,256]{2,1,0:T(8,128)(2,1)S(1)}, u32[]{:S(2)}, u32[]{:S(2)}) collective-permute-start(bf16[2,128,256]{2,1,0:T(8,128)(2,1)S(1)} %get-tuple-element.29), channel_id=1, source_target_pairs={{0,48},{1,49},{2,50},{3,51},{4,52},{5,53},{6,54},{7,55},{8,56},{9,... | collective-permute-start | bytes 393224 | tf_op jit(solution)/shard_map/ppermute | solution.py:388
  46.2 6.5 %collective-permute-done.7.refs_2_ = bf16[2,128,256]{2,1,0:T(8,128)(2,1)S(1)} collective-permute-done((bf16[2,128,256]{2,1,0:T(8,128)(2,1)S(1)}, bf16[2,128,256]{2,1,0:T(8,128)(2,1)S(1)}, u32[]{:S(2)}, u32[]{:S(2)}) %collective-permute-start.7) | collective-permute-done | bytes 131104 | tf_op jit(solution)/shard_map/ppermute | solution.py:388
  52.7 1.4 %collective-permute-done.8.refs_3_ = bf16[2,128,256]{2,1,0:T(8,128)(2,1)S(1)} collective-permute-done((bf16[2,128,256]{2,1,0:T(8,128)(2,1)S(1)}, bf16[2,128,256]{2,1,0:T(8,128)(2,1)S(1)}, u32[]{:S(2)}, u32[]{:S(2)}) %collective-permute-start.8) | collective-permute-done | bytes 131104 | tf_op jit(solution)/shard_map/ppermute | solution.py:388
  54.1 0.0 collective-permute-done.9.refs_4_
  54.1 0.0 all-to-all-done.1.refs_5_.refs_2_
  54.1 0.8 stack.35
  54.9 0.0 all-gather.3.cloned.1.call-update
  55.0 0.1 collective-permute-start.2
  55.1 0.5 collective-permute-start.3
  55.6 0.1 pad_add_fusion.1.refs_0_
  55.6 2.6 %collective-permute-done.3.refs_3_ = bf16[4,2,128,128]{3,2,1,0:T(8,128)(2,1)} collective-permute-done((bf16[4,2,128,128]{3,2,1,0:T(8,128)(2,1)S(1)}, bf16[4,2,128,128]{3,2,1,0:T(8,128)(2,1)}, u32[]{:S(2)}, u32[]{:S(2)}) %collective-permute-start.3) | collective-permute-done | bytes 262176 | tf_op jit(solution)/shard_map/ppermute | solution.py:378
  58.2 2.0 %near.1 = (f32[1,512]{1,0:T(1,128)S(1)}, f32[1,512]{1,0:T(1,128)S(1)}, f32[128,512]{1,0:T(8,128)S(1)}) custom-call(s32[2]{0:T(128)S(1)} %pad_add_fusion.1.refs_0_, bf16[4,3,128,128]{3,2,1,0:T(8,128)(2,1)S(1)} %all-to-all-done.refs_0_.refs_1_, bf16[4,2,128,128]{3,2,1,0:T(8,128)(2,1)S(1)} %get-tuple-element.22.refs_2_, ...), custom_call_target="tpu_custom_call" | custom-call | flops 2000000000 | bytes 2000000 | tf_op jit(solution)/shard_map/near/pallas_call | solution.py:89
  60.3 0.0 collective-permute-done.2.refs_6_.refs_3_
  60.3 4.5 %far.1 = bf16[2,2,256,128]{3,2,1,0:T(8,128)(2,1)} custom-call(s32[2]{0:T(128)S(1)} %pad_add_fusion.1.refs_0_, bf16[4,3,128,128]{3,2,1,0:T(8,128)(2,1)S(1)} %all-to-all-done.refs_0_.refs_1_, f32[1,512]{1,0:T(1,128)S(1)} %get-tuple-element.23.refs_2_, f32[1,512]{1,0:T(1,128)S(1)} %get-tuple-element.24.refs_3_, f32[128,512]{1,0:T(8,128)S(1)} %get-tuple-element.25.refs_4_, ...), custom_call_target="tpu_custom_call" | custom-call | flops 4000000000 | bytes 2000000 | tf_op jit(solution)/shard_map/far/pallas_call | solution.py:89
  64.8 10.1 %all-to-all-start.2 = ((bf16[4,256,128]{2,1,0:T(8,128)(2,1)}), bf16[4,256,128]{2,1,0:T(8,128)(2,1)S(1)}, u32[]{:S(2)}, u32[]{:S(2)}) async-start(bf16[4,256,128]{2,1,0:T(8,128)(2,1)} %bitcast.3), calls=%async_computation.2 | async-start | bytes 524288 | tf_op jit(solution)/shard_map/all_to_all | solution.py:410
  74.9 0.1 pad_add_fusion.refs_0_
  75.0 10.2 %all-to-all-done.2.refs_4_.refs_1_ = bf16[4,256,128]{2,1,0:T(8,128)(2,1)S(1)} async-done(((bf16[4,256,128]{2,1,0:T(8,128)(2,1)}), bf16[4,256,128]{2,1,0:T(8,128)(2,1)S(1)}, u32[]{:S(2)}, u32[]{:S(2)}) %all-to-all-start.2) | async-done | bytes 262176 | tf_op jit(solution)/shard_map/all_to_all | solution.py:410
  85.2 0.2 collective-permute-start.4
  85.5 3.0 %collective-permute-start.5 = (bf16[4,256,128]{2,1,0:T(8,128)(2,1)S(1)}, bf16[4,256,128]{2,1,0:T(8,128)(2,1)}, u32[]{:S(2)}, u32[]{:S(2)}) collective-permute-start(bf16[4,256,128]{2,1,0:T(8,128)(2,1)S(1)} %all-to-all-done.2.refs_4_.refs_1_), channel_id=1, source_target_pairs={{0,6},{2,0},{4,2},{6,4},{1,7},{3,1},{5,3},{7,5},{8,14},{10,8},{12,... | collective-permute-start | bytes 786440 | tf_op jit(solution)/shard_map/ppermute | solution.py:412
  88.5 0.7 collective-permute-start.6
  89.2 0.1 pad_add_fusion.2.refs_0_
  89.3 1.5 %combine.1 = f32[4,16,1024]{2,1,0:T(8,128)} custom-call(s32[3]{0:T(128)S(1)} %pad_add_fusion.refs_0_, f32[16,1024]{1,0:T(8,128)S(1)} %get-tuple-element.18.refs_1_.refs_0_, bf16[4,10,128,128]{3,2,1,0:T(8,128)(2,1)S(1)} %all-to-all-done.1.refs_5_.refs_2_, bf16[4,10,128,128]{3,2,1,0:T(8,128)(2,1)S(1)} %collective-permute-done.2.refs_6_.refs_3_, ...), custom_call_target="tpu_custom_call" | custom-call | flops 100000000 | bytes 2000000 | tf_op jit(solution)/shard_map/combine/pallas_call | solution.py:89
  90.8 4.0 %all-to-all-start.3 = ((f32[4,16,1024]{2,1,0:T(8,128)}), f32[4,16,1024]{2,1,0:T(8,128)S(1)}, u32[]{:S(2)}, u32[]{:S(2)}) async-start(f32[4,16,1024]{2,1,0:T(8,128)} %combine.1), calls=%async_computation.3 | async-start | bytes 524288 | tf_op jit(solution)/shard_map/all_to_all | solution.py:424
  94.8 0.1 collective-permute-done.4.refs_2_
  95.0 3.1 %collective-permute-done.5.refs_3_ = bf16[4,256,128]{2,1,0:T(8,128)(2,1)} collective-permute-done((bf16[4,256,128]{2,1,0:T(8,128)(2,1)S(1)}, bf16[4,256,128]{2,1,0:T(8,128)(2,1)}, u32[]{:S(2)}, u32[]{:S(2)}) %collective-permute-start.5) | collective-permute-done | bytes 262176 | tf_op jit(solution)/shard_map/ppermute | solution.py:412
  98.1 1.6 %collective-permute-done.6.refs_4_ = bf16[4,256,128]{2,1,0:T(8,128)(2,1)} collective-permute-done((bf16[4,256,128]{2,1,0:T(8,128)(2,1)S(1)}, bf16[4,256,128]{2,1,0:T(8,128)(2,1)}, u32[]{:S(2)}, u32[]{:S(2)}) %collective-permute-start.6) | collective-permute-done | bytes 262176 | tf_op jit(solution)/shard_map/ppermute | solution.py:412
  99.7 3.9 %project.1 = (f32[128,1024]{1,0:T(8,128)S(1)}, bf16[128,1024]{1,0:T(8,128)(2,1)S(1)}) custom-call(s32[2]{0:T(128)S(1)} %pad_add_fusion.2.refs_0_, bf16[4,256,128]{2,1,0:T(8,128)(2,1)S(1)} %all-to-all-done.2.refs_4_.refs_1_, bf16[4,256,128]{2,1,0:T(8,128)(2,1)S(1)} %collective-permute-done.4.refs_2_, bf16[4,256,128]{2,1,0:T(8,128)(2,1)} %collective-permute-done.5.refs_3_, ...), custom_call_target="tpu_custom_call" | custom-call | flops 2000000000 | bytes 2000000 | tf_op jit(solution)/shard_map/project/pallas_call | solution.py:89
  103.6 0.1 collective-permute-start.10
  103.7 0.0 all-to-all-done.3.refs_2_
  103.7 2.7 %mix.1 = bf16[128,1024]{1,0:T(8,128)(2,1)} custom-call(f32[16,1024]{1,0:T(8,128)S(1)} %get-tuple-element.18.refs_1_.refs_0_, f32[16,1024]{1,0:T(8,128)S(1)} %sqrt_multiply_fusion.refs_1_, f32[4,16,1024]{2,1,0:T(8,128)S(1)} %all-to-all-done.3.refs_2_, f32[128,1024]{1,0:T(8,128)S(1)} %copy-done.1, f32[128,1024]{1,0:T(8,128)S(1)} %copy-done.3), custom_call_target="tpu_custom_call" | custom-call | flops 4000000000 | bytes 2000000 | tf_op jit(solution)/shard_map/mix/pallas_call | solution.py:89
  106.5 3.6 %collective-permute-done.10 = bf16[128,1024]{1,0:T(8,128)(2,1)S(1)} collective-permute-done((bf16[128,1024]{1,0:T(8,128)(2,1)S(1)}, bf16[128,1024]{1,0:T(8,128)(2,1)S(1)}, u32[]{:S(2)}, u32[]{:S(2)}) %collective-permute-start.10) | collective-permute-done | bytes 262176 | tf_op jit(solution)/shard_map/ppermute | solution.py:439
  110.0 0.8 add_convert_fusion
  (12 shorter events, 0.1 us)
Async XLA Ops:
  7.2 7.9 %copy-start.5 = (bf16[512,256]{1,0:T(8,128)(2,1)S(1)}, bf16[512,256]{1,0:T(8,128)(2,1)}, u32[]{:S(2)}) copy-start(bf16[512,256]{1,0:T(8,128)(2,1)} %param.11) | copy-start | bytes 786436
  9.1 19.4 %all-to-all-start = ((bf16[4,3,128,128]{3,2,1,0:T(8,128)(2,1)}), bf16[4,3,128,128]{3,2,1,0:T(8,128)(2,1)S(1)}, u32[]{:S(2)}, u32[]{:S(2)}) async-start(bf16[4,3,128,128]{3,2,1,0:T(8,128)(2,1)} %get-tuple-element.19), calls=%async_computation | async-start | bytes 786432 | tf_op jit(solution)/shard_map/all_to_all | solution.py:352
  15.1 13.4 %collective-permute-start.1 = (bf16[512,256]{1,0:T(8,128)(2,1)S(1)}, bf16[512,256]{1,0:T(8,128)(2,1)S(1)}, u32[]{:S(2)}, u32[]{:S(2)}) collective-permute-start(bf16[512,256]{1,0:T(8,128)(2,1)S(1)} %copy-done.5), channel_id=1, source_target_pairs={{0,0},{1,32},{2,64},{3,96},{4,128},{5,160},{6,192},{7,224},{8,8},{... | collective-permute-start | bytes 786440 | tf_op jit(solution)/shard_map/ppermute | solution.py:369
  20.0 5.1 %collective-permute-start = (f32[3,2,1024]{2,1,0:T(2,128)S(1)}, f32[3,2,1024]{2,1,0:T(2,128)S(1)}, u32[]{:S(2)}, u32[]{:S(2)}) collective-permute-start(f32[3,2,1024]{2,1,0:T(2,128)S(1)} %get-tuple-element.17), channel_id=1, source_target_pairs={{0,8},{1,9},{2,10},{3,11},{4,12},{5,13},{6,14},{7,15},{8,16},{9,17... | collective-permute-start | bytes 73736 | tf_op jit(solution)/shard_map/ppermute | solution.py:353
  27.7 0.8 copy-start
  28.5 1.3 %copy-start.2 = (f32[128,1024]{1,0:T(8,128)}, f32[128,1024]{1,0:T(8,128)S(1)}, u32[]{:S(2)}) copy-start(f32[128,1024]{1,0:T(8,128)S(1)} %get-tuple-element.27.refs_4_) | copy-start | bytes 1572868
  29.8 24.3 %all-to-all-start.1 = ((bf16[4,10,128,128]{3,2,1,0:T(8,128)(2,1)}), bf16[4,10,128,128]{3,2,1,0:T(8,128)(2,1)S(1)}, u32[]{:S(2)}, u32[]{:S(2)}) async-start(bf16[4,10,128,128]{3,2,1,0:T(8,128)(2,1)} %get-tuple-element.21.refs_2_), calls=%async_computation.1 | async-start | bytes 2621440 | tf_op jit(solution)/shard_map/all_to_all | solution.py:379
  34.7 65.0 %all-gather.3.cloned.1.call-start = ((), (), s32[]{:S(2)}) async-start(), calls=%async_computation.4 | async-start | bytes 4718592 | tf_op jit(solution)/shard_map/all_gather | solution.py:394
  34.7 18.0 %collective-permute-start.7 = (bf16[2,128,256]{2,1,0:T(8,128)(2,1)S(1)}, bf16[2,128,256]{2,1,0:T(8,128)(2,1)S(1)}, u32[]{:S(2)}, u32[]{:S(2)}) collective-permute-start(bf16[2,128,256]{2,1,0:T(8,128)(2,1)S(1)} %get-tuple-element.29), channel_id=1, source_target_pairs={{0,16},{1,17},{2,18},{3,19},{4,20},{5,21},{6,22},{7,23},{8,24},{9,... | collective-permute-start | bytes 393224 | tf_op jit(solution)/shard_map/ppermute | solution.py:388
  44.6 9.5 %collective-permute-start.8 = (bf16[2,128,256]{2,1,0:T(8,128)(2,1)S(1)}, bf16[2,128,256]{2,1,0:T(8,128)(2,1)S(1)}, u32[]{:S(2)}, u32[]{:S(2)}) collective-permute-start(bf16[2,128,256]{2,1,0:T(8,128)(2,1)S(1)} %get-tuple-element.28.refs_1_), channel_id=1, source_target_pairs={{0,32},{1,33},{2,34},{3,35},{4,36},{5,37},{6,38},{7,39},{8,40},{9,... | collective-permute-start | bytes 393224 | tf_op jit(solution)/shard_map/ppermute | solution.py:388
  44.6 9.5 %collective-permute-start.9 = (bf16[2,128,256]{2,1,0:T(8,128)(2,1)S(1)}, bf16[2,128,256]{2,1,0:T(8,128)(2,1)S(1)}, u32[]{:S(2)}, u32[]{:S(2)}) collective-permute-start(bf16[2,128,256]{2,1,0:T(8,128)(2,1)S(1)} %get-tuple-element.29), channel_id=1, source_target_pairs={{0,48},{1,49},{2,50},{3,51},{4,52},{5,53},{6,54},{7,55},{8,56},{9,... | collective-permute-start | bytes 393224 | tf_op jit(solution)/shard_map/ppermute | solution.py:388
  55.0 5.3 %collective-permute-start.2 = (bf16[4,10,128,128]{3,2,1,0:T(8,128)(2,1)S(1)}, bf16[4,10,128,128]{3,2,1,0:T(8,128)(2,1)S(1)}, u32[]{:S(2)}, u32[]{:S(2)}) collective-permute-start(bf16[4,10,128,128]{3,2,1,0:T(8,128)(2,1)S(1)} %all-to-all-done.1.refs_5_.refs_2_), channel_id=1, source_target_pairs={{0,8},{8,0},{1,9},{9,1},{2,10},{10,2},{3,11},{11,3},{4,12},{12,4},... | collective-permute-start | bytes 3932168 | tf_op jit(solution)/shard_map/ppermute | solution.py:380
  55.1 3.2 %collective-permute-start.3 = (bf16[4,2,128,128]{3,2,1,0:T(8,128)(2,1)S(1)}, bf16[4,2,128,128]{3,2,1,0:T(8,128)(2,1)}, u32[]{:S(2)}, u32[]{:S(2)}) collective-permute-start(bf16[4,2,128,128]{3,2,1,0:T(8,128)(2,1)S(1)} %get-tuple-element.22.refs_2_), channel_id=1, source_target_pairs={{0,8},{8,0},{1,9},{9,1},{2,10},{10,2},{3,11},{11,3},{4,12},{12,4},... | collective-permute-start | bytes 786440 | tf_op jit(solution)/shard_map/ppermute | solution.py:378
  64.8 20.4 %all-to-all-start.2 = ((bf16[4,256,128]{2,1,0:T(8,128)(2,1)}), bf16[4,256,128]{2,1,0:T(8,128)(2,1)S(1)}, u32[]{:S(2)}, u32[]{:S(2)}) async-start(bf16[4,256,128]{2,1,0:T(8,128)(2,1)} %bitcast.3), calls=%async_computation.2 | async-start | bytes 524288 | tf_op jit(solution)/shard_map/all_to_all | solution.py:410
  85.2 9.7 %collective-permute-start.4 = (bf16[4,256,128]{2,1,0:T(8,128)(2,1)S(1)}, bf16[4,256,128]{2,1,0:T(8,128)(2,1)S(1)}, u32[]{:S(2)}, u32[]{:S(2)}) collective-permute-start(bf16[4,256,128]{2,1,0:T(8,128)(2,1)S(1)} %all-to-all-done.2.refs_4_.refs_1_), channel_id=1, source_target_pairs={{0,2},{2,4},{4,6},{6,0},{1,3},{3,5},{5,7},{7,1},{8,10},{10,12},{12... | collective-permute-start | bytes 786440 | tf_op jit(solution)/shard_map/ppermute | solution.py:412
  85.5 12.6 %collective-permute-start.5 = (bf16[4,256,128]{2,1,0:T(8,128)(2,1)S(1)}, bf16[4,256,128]{2,1,0:T(8,128)(2,1)}, u32[]{:S(2)}, u32[]{:S(2)}) collective-permute-start(bf16[4,256,128]{2,1,0:T(8,128)(2,1)S(1)} %all-to-all-done.2.refs_4_.refs_1_), channel_id=1, source_target_pairs={{0,6},{2,0},{4,2},{6,4},{1,7},{3,1},{5,3},{7,5},{8,14},{10,8},{12,... | collective-permute-start | bytes 786440 | tf_op jit(solution)/shard_map/ppermute | solution.py:412
  88.5 11.2 %collective-permute-start.6 = (bf16[4,256,128]{2,1,0:T(8,128)(2,1)S(1)}, bf16[4,256,128]{2,1,0:T(8,128)(2,1)}, u32[]{:S(2)}, u32[]{:S(2)}) collective-permute-start(bf16[4,256,128]{2,1,0:T(8,128)(2,1)S(1)} %all-to-all-done.2.refs_4_.refs_1_), channel_id=1, source_target_pairs={{0,4},{2,6},{4,0},{6,2},{1,5},{3,7},{5,1},{7,3},{8,12},{10,14},{12... | collective-permute-start | bytes 786440 | tf_op jit(solution)/shard_map/ppermute | solution.py:412
  89.3 5.5 %copy-start.4 = (f32[16,1024]{1,0:T(8,128)S(1)}, f32[16,1024]{1,0:T(8,128)}, u32[]{:S(2)}) copy-start(f32[16,1024]{1,0:T(8,128)} %param.9) | copy-start | bytes 196612
  90.8 12.9 %all-to-all-start.3 = ((f32[4,16,1024]{2,1,0:T(8,128)}), f32[4,16,1024]{2,1,0:T(8,128)S(1)}, u32[]{:S(2)}, u32[]{:S(2)}) async-start(f32[4,16,1024]{2,1,0:T(8,128)} %combine.1), calls=%async_computation.3 | async-start | bytes 524288 | tf_op jit(solution)/shard_map/all_to_all | solution.py:424
  99.7 4.0 %copy-start.1 = (f32[128,1024]{1,0:T(8,128)S(1)}, f32[128,1024]{1,0:T(8,128)}, u32[]{:S(2)}) copy-start(f32[128,1024]{1,0:T(8,128)} %copy-done) | copy-start | bytes 1572868
  99.7 4.1 %copy-start.3 = (f32[128,1024]{1,0:T(8,128)S(1)}, f32[128,1024]{1,0:T(8,128)}, u32[]{:S(2)}) copy-start(f32[128,1024]{1,0:T(8,128)} %copy-done.2) | copy-start | bytes 1572868
  103.6 6.5 %collective-permute-start.10 = (bf16[128,1024]{1,0:T(8,128)(2,1)S(1)}, bf16[128,1024]{1,0:T(8,128)(2,1)S(1)}, u32[]{:S(2)}, u32[]{:S(2)}) collective-permute-start(bf16[128,1024]{1,0:T(8,128)(2,1)S(1)} %get-tuple-element.31), channel_id=1, source_target_pairs={{0,16},{16,0},{1,17},{17,1},{2,18},{18,2},{3,19},{19,3},{4,20},{20... | collective-permute-start | bytes 786440 | tf_op jit(solution)/shard_map/ppermute | solution.py:439
Sparse Core Ops, SparseCore 0:
  55.1 36.4 all-gather.2

commit v2 on v1

--- a/solution.py
+++ b/solution.py
@@ -212,14 +212,18 @@
     lax.fori_loop(0, rows // 16, body, start)
 
 
-def pack_kernel(qkv, feats, out_ref, halo_ref, tail, sems):
-    rows = qkv.shape[1]
-    pairs = [(feats.at[:, pl.ds(rows - 16, 16), :], tail)]
+def tail_kernel(feats, halo_ref, tail, sems):
+    rows = feats.shape[1]
+    finished(started(sems, [(feats.at[:, pl.ds(rows - 16, 16), :], tail)]))
+    halo_ref[...] = tail[:, 14:16].astype(jnp.float32)
+
+
+def pack_kernel(qkv, out_ref, sems):
+    pairs = []
     for head in range(NZ):
         lanes = pl.ds(head * HEAD, HEAD)
         pairs += [(qkv.at[i, :, lanes], out_ref.at[head, i]) for i in range(3)]
     finished(started(sems, pairs))
-    halo_ref[...] = tail[:, 14:16].astype(jnp.float32)
 
 
 def halves_kernel(place_ref, weight_ref, same_ref, other_ref):
@@ -238,18 +242,17 @@
         refs[-1][(place_ref[0] + NZ - steps) % NZ] = ref[...]
 
 
-def spread_kernel(qkv_ref, ends_ref, kv_ref, out_ref):
+def spread_kernel(qkv_ref, ends_ref, out_ref):
     for z in range(NZ):
-        kv_ref[z] = qkv_ref[z, 1:]
         for i in range(out_ref.shape[0]):
             out_ref[i, 2 * z : 2 * z + 2] = qkv_ref[z, 1:]
     for i in range(out_ref.shape[0]):
         out_ref[i, 2 * NZ :] = ends_ref[...]
 
 
-def folded(q, sets, top, total, acc, visible=None):
-    keys = jnp.concatenate([a[:, 0].reshape(-1, HEAD) for a in sets], axis=0)
-    values = jnp.concatenate([a[:, 1].reshape(-1, HEAD) for a in sets], axis=0)
+def folded(q, pairs, top, total, acc, visible=None):
+    keys = pairs[:, 0].reshape(-1, HEAD)
+    values = pairs[:, 1].reshape(-1, HEAD)
     s = lax.dot_general(keys, q, (((1,), (1,)), ((), ())), preferred_element_type=jnp.float32)
     if visible is not None:
         s = jnp.where(visible, s, -1e30)
@@ -260,42 +263,48 @@
     return new, total * again + jnp.sum(p, axis=0, keepdims=True), acc * again + added
 
 
-def near_kernel(place_ref, qkv_ref, a, b, top_ref, total_ref, acc_ref):
-    k = place_ref[1]
-    rows = NZ * HEAD
-    col = lax.broadcasted_iota(jnp.int32, (1, rows), 1)
-    row = lax.broadcasted_iota(jnp.int32, (2 * rows, 1), 0)
-    core = jnp.where(row < rows, k, 1 - k)
-    here = (2 * (col // HEAD) + k) * HEAD + col % HEAD
-    there = (2 * ((row % rows) // HEAD) + core) * HEAD + row % HEAD
-    lowest = jnp.full((1, rows), -1e30, jnp.float32)
-    top_ref[...], total_ref[...], acc_ref[...] = folded(
-        qkv_ref[:, 0].reshape(rows, HEAD),
-        (a[...], b[...]),
-        lowest,
-        jnp.zeros((1, rows), jnp.float32),
-        jnp.zeros((HEAD, rows), jnp.float32),
-        there <= here,
-    )
-
-
 def pairs_of(ref, row):
     return ref[row, 0 : 2 * NZ].reshape(NZ, 2, HEAD, HEAD)
 
 
-def far_kernel(
-    place_ref, qkv_ref, top_ref, total_ref, acc_ref, a_ref, b_ref, out_ref, top, total, acc
-):
-    q = qkv_ref[:, 0].reshape(NZ * HEAD, HEAD)
-    top[...], total[...], acc[...] = top_ref[...], total_ref[...], acc_ref[...]
+def fold_rows(x, q, ref, top, total, acc):
     for row in range(NX - 1):
 
-        @pl.when(place_ref[0] > row)
+        @pl.when(x > row)
         def _():
             top[...], total[...], acc[...] = folded(
-                q, (pairs_of(a_ref, row), pairs_of(b_ref, row)), top[...], total[...], acc[...]
+                q, pairs_of(ref, row), top[...], total[...], acc[...]
             )
 
+
+def own_kernel(place_ref, qkv_ref, kv_ref, top_ref, total_ref, acc_ref):
+    x = place_ref[0]
+    rows = NZ * HEAD
+    q = qkv_ref[:, 0].reshape(rows, HEAD)
+    col = lax.broadcasted_iota(jnp.int32, (1, rows), 1)
+    row = lax.broadcasted_iota(jnp.int32, (rows, 1), 0)
+    lowest = jnp.full((1, rows), -1e30, jnp.float32)
+    nothing = jnp.zeros((1, rows), jnp.float32), jnp.zeros((HEAD, rows), jnp.float32)
+    top_ref[...], total_ref[...], acc_ref[...] = folded(
+        q, pairs_of(kv_ref, x), lowest, *nothing, row <= col
+    )
+    fold_rows(x, q, kv_ref, top_ref, total_ref, acc_ref)
+
+
+def other_kernel(
+    place_ref, qkv_ref, top_ref, total_ref, acc_ref, kv_ref, out_ref, top, total, acc
+):
+    x, k = place_ref[0], place_ref[1]
+    rows = NZ * HEAD
+    q = qkv_ref[:, 0].reshape(rows, HEAD)
+    col = lax.broadcasted_iota(jnp.int32, (1, rows), 1)
+    row = lax.broadcasted_iota(jnp.int32, (rows, 1), 0)
+    here = (2 * (col // HEAD) + k) * HEAD + col % HEAD
+    there = (2 * (row // HEAD) + 1 - k) * HEAD + row % HEAD
+    top[...], total[...], acc[...] = folded(
+        q, pairs_of(kv_ref, x), top_ref[...], total_ref[...], acc_ref[...], there <= here
+    )
+    fold_rows(x, q, kv_ref, top, total, acc)
     result = (acc[...] / total[...]).T.astype(jnp.bfloat16).reshape(out_ref.shape[1:])
     for h in range(NH):
         out_ref[h] = result
@@ -341,14 +350,23 @@
     bf16, f32 = jnp.bfloat16, jnp.float32
     dma = pltpu.SemaphoreType.DMA
 
-    packed, tail = local_call(
+    tail = local_call(
+        tail_kernel,
+        short((3, 2, width), f32),
+        (SLOW,),
+        "tail",
+        10**8,
+        (pltpu.VMEM((3, 16, width), bf16), dma((1,))),
+    )(hyena_feats)
+    packed = local_call(
         pack_kernel,
-        (short((NZ, 3, rows, HEAD), bf16), short((3, 2, width), f32)),
-        (SLOW, SLOW),
+        short((NZ, 3, rows, HEAD), bf16),
+        (SLOW,),
         "pack",
         10**8,
-        (pltpu.VMEM((3, 16, width), bf16), dma((1 + 3 * NZ,))),
-    )(attn_qkv, hyena_feats)
+        (dma((3 * NZ,)),),
+        after=(tail,),
+    )(attn_qkv)
     qkv = lax.all_to_all(packed, ("z1", "z0"), 0, 0)
     halo = lax.ppermute(tail, ALL, moved(next_ctx))
     plane = short((rows, width), f32)
@@ -367,15 +385,14 @@
         ),
     )(hyena_feats, halo, short_taps, decay_rate)
     moved_weight = lax.ppermute(out_weight, ALL, moved(place_weight))
-    kv, spread = local_call(
+    spread = local_call(
         spread_kernel,
-        (short((NZ, 2, rows, HEAD), bf16), short((NX, 2 * NZ + 2, rows, HEAD), bf16)),
+        short((NX, 2 * NZ + 2, rows, HEAD), bf16),
         (FAST, FAST),
         "spread",
         10**8,
         after=(moved_weight,),
     )(qkv, ends)
-    near = lax.ppermute(kv, "k", swap)
     far_own = lax.all_to_all(spread, "x", 0, 0)
     far_other = lax.ppermute(far_own, "k", swap)
 
@@ -397,16 +414,17 @@
     line = short((1, NZ * rows), f32)
     square = short((HEAD, NZ * rows), f32)
     partial = local_call(
-        near_kernel, (line, line, square), (SMEM, FAST, FAST, FAST), "near", 2 * 10**9
-    )(where, qkv, kv, near)
+        own_kernel, (line, line, square), (SMEM, FAST, FAST), "own", 2 * 10**9
+    )(where, qkv, far_own)
     attended = local_call(
-        far_kernel,
+        other_kernel,
         short((NH, NZ1, NZ0 * rows, HEAD), bf16),
-        (SMEM,) + (FAST,) * 6,
-        "far",
-        4 * 10**9,
+        (SMEM,) + (FAST,) * 5,
+        "other",
+        2 * 10**9,
         [pltpu.VMEM(part.shape, f32) for part in (line, line, square)],
-    )(where, qkv, *partial, far_own, far_other)
+    )(where, qkv, *partial, far_other)
+    rate = gate(rate, attended)
     group = lax.all_to_all(attended.reshape(NH * NZ1, NZ0 * rows, HEAD), ("h", "z1"), 0, 0)
     groups = [group] + [
         lax.ppermute(group, "y", [(i, (i + step) % NY) for i in range(NY)]) for step in (1, 3, 2)

time: 118 us -> 117 us (level)
  waiting for transfers between devices: 32.4 us -> 28.4 us
  local copies, waits for them, and re-layouts: 0.82 us -> 3.1 us
  starting transfers between devices: 48 us -> 46.1 us
  Pallas kernels: 21.2 us -> 22.7 us
    ppermute x1 -> x0, waiting for transfers between devices: 2.59 us -> none  [per_device(): near = lax.ppermute(kv, 'k', swap)]
    unnamed x12 -> x14, local copies, waits for them, and re-layouts: 0.82 us -> 3.1 us
    ppermute x3, waiting for transfers between devices: 4.82 us -> 3.27 us  [per_device(): lax.ppermute(group, 'y', [(i, (i + step) % NY) for i in range(NY)])]
    pallas_call x10 -> x11, Pallas kernels: 21.2 us -> 22.7 us  [local_call(): return lambda *operands: call(*map(placed, operands, specs), *after)]
    ppermute x3, starting transfers between devices: 11.4 us -> 9.99 us  [per_device(): lax.ppermute(opposite if steps % 2 else same, ALL, along_z(steps))]
  transfers between devices with their start and end apart: 16 -> 15, of which waited for: 9 -> 7; matrix products, arithmetic and copies ran while one was open for 0% -> 1% of each run, Pallas kernels for 15% -> 15%
where the time goes in v2:
time: 117 us; the launch traced here: 116 us
  starting transfers between devices  46.1 us (39%)
  waiting for transfers between devices  28.4 us (24%)
  Pallas kernels  22.7 us (19%)
  between operations  14.2 us (12%)
  local copies, waits for them, and re-layouts  3.1 us (3%)
  other arithmetic  1.87 us (2%)
    pallas_call x11, Pallas kernels, local_call(): return lambda *operands: call(*map(placed, operands, specs), *after)  22.7 us
    all_to_all x1, waiting for transfers between devices, per_device(): lax.all_to_all(attended.reshape(NH * NZ1, NZ0 * rows, HEAD), ('h', 'z1'),...  10.3 us
    all_to_all x1, starting transfers between devices, per_device(): lax.all_to_all(attended.reshape(NH * NZ1, NZ0 * rows, HEAD), ('h', 'z1'),...  10.1 us
    ppermute x3, starting transfers between devices, per_device(): lax.ppermute(opposite if steps % 2 else same, ALL, along_z(steps))  9.99 us
    ppermute x3, waiting for transfers between devices, per_device(): lax.ppermute(opposite if steps % 2 else same, ALL, along_z(steps))  7.92 us
    all_to_all x1, starting transfers between devices, per_device(): qkv = lax.all_to_all(packed, ('z1', 'z0'), 0, 0)  6.01 us
    all_to_all x1, starting transfers between devices, per_device(): far_own = lax.all_to_all(spread, 'x', 0, 0)  4.95 us
    ppermute x1, starting transfers between devices, per_device(): moved_weight = lax.ppermute(out_weight, ALL, moved(place_weight))  4.91 us
  transfers between devices with their start and end apart: 15, of which 7 were waited for; matrix products, arithmetic and copies ran while one was open for 1% of the time, Pallas kernels for 15%

profile of v2, /device:TPU:38, one launch (start us, length us, event | category | flops | bytes accessed | tf_op | source)
XLA Modules:
  0.0 116.3 jit_solution(2674223877915427737)
XLA Ops:
  7.2 1.0 tail.1.refs_1_
  8.1 1.8 %pack.1 = bf16[4,3,128,128]{3,2,1,0:T(8,128)(2,1)} custom-call(bf16[3,128,512]{2,1,0:T(8,128)(2,1)} %refs_0_.5, f32[3,2,1024]{2,1,0:T(2,128)S(1)} %tail.1.refs_1_), custom_call_target="tpu_custom_call" | custom-call | flops 100000000 | bytes 2000000 | tf_op jit(solution)/shard_map/pack/pallas_call | solution.py:89
  10.0 6.0 %all-to-all-start = ((bf16[4,3,128,128]{3,2,1,0:T(8,128)(2,1)}), bf16[4,3,128,128]{3,2,1,0:T(8,128)(2,1)S(1)}, u32[]{:S(2)}, u32[]{:S(2)}) async-start(bf16[4,3,128,128]{3,2,1,0:T(8,128)(2,1)} %pack.1), calls=%async_computation | async-start | bytes 786432 | tf_op jit(solution)/shard_map/all_to_all | solution.py:370
  16.0 4.9 %collective-permute-start.1 = (bf16[512,256]{1,0:T(8,128)(2,1)S(1)}, bf16[512,256]{1,0:T(8,128)(2,1)S(1)}, u32[]{:S(2)}, u32[]{:S(2)}) collective-permute-start(bf16[512,256]{1,0:T(8,128)(2,1)S(1)} %copy-done.6), channel_id=1, source_target_pairs={{0,0},{1,32},{2,64},{3,96},{4,128},{5,160},{6,192},{7,224},{8,8},{... | collective-permute-start | bytes 786440 | tf_op jit(solution)/shard_map/ppermute | solution.py:387
  20.9 1.9 %collective-permute-start = (f32[3,2,1024]{2,1,0:T(2,128)S(1)}, f32[3,2,1024]{2,1,0:T(2,128)S(1)}, u32[]{:S(2)}, u32[]{:S(2)}) collective-permute-start(f32[3,2,1024]{2,1,0:T(2,128)S(1)} %tail.1.refs_1_), channel_id=1, source_target_pairs={{0,8},{1,9},{2,10},{3,11},{4,12},{5,13},{6,14},{7,15},{8,16},{9,17... | collective-permute-start | bytes 73736 | tf_op jit(solution)/shard_map/ppermute | solution.py:371
  22.8 3.2 %collective-permute-done.refs_1_ = f32[3,2,1024]{2,1,0:T(2,128)S(1)} collective-permute-done((f32[3,2,1024]{2,1,0:T(2,128)S(1)}, f32[3,2,1024]{2,1,0:T(2,128)S(1)}, u32[]{:S(2)}, u32[]{:S(2)}) %collective-permute-start) | collective-permute-done | bytes 24608 | tf_op jit(solution)/shard_map/ppermute | solution.py:371
  26.0 2.5 %ends.1 = (bf16[2,128,128]{2,1,0:T(8,128)(2,1)S(1)}, f32[128,1024]{1,0:T(8,128)S(1)}, f32[128,1024]{1,0:T(8,128)S(1)}, f32[16,1024]{1,0:T(8,128)S(1)}) custom-call(bf16[3,128,1024]{2,1,0:T(8,128)(2,1)} %refs_0_.4, f32[3,2,1024]{2,1,0:T(2,128)S(1)} %collective-permute-done.refs_1_, f32[3,3,1024]{2,1,0:T(4,128)} %refs_2_.1, f32[16,1024]{1,0:T(8,128)} %refs_3_.1), custom_call_target="tpu_custom_call" | custom-call | flops 1000000000 | bytes 2000000 | tf_op jit(solution)/shard_map/ends/pallas_call | solution.py:89
  28.5 0.0 copy-start
  28.6 0.6 copy-done
  29.2 0.8 copy-done.2
  30.0 0.8 copy-done.4
  30.8 0.0 collective-permute-done.1.refs_2_.refs_1_
  30.8 0.0 all-to-all-done.refs_0_.refs_1_
  30.8 1.3 %spread.1.refs_2_ = bf16[4,10,128,128]{3,2,1,0:T(8,128)(2,1)} custom-call(bf16[4,3,128,128]{3,2,1,0:T(8,128)(2,1)S(1)} %all-to-all-done.refs_0_.refs_1_, bf16[2,128,128]{2,1,0:T(8,128)(2,1)S(1)} %get-tuple-element.14.refs_1_, bf16[512,256]{1,0:T(8,128)(2,1)S(1)} %collective-permute-done.1.refs_2_.refs_1_), custom_call_target="tpu_custom_call" | custom-call | flops 100000000 | bytes 2000000 | tf_op jit(solution)/shard_map/spread/pallas_call | solution.py:89
  32.1 4.9 %all-to-all-start.1 = ((bf16[4,10,128,128]{3,2,1,0:T(8,128)(2,1)}), bf16[4,10,128,128]{3,2,1,0:T(8,128)(2,1)S(1)}, u32[]{:S(2)}, u32[]{:S(2)}) async-start(bf16[4,10,128,128]{3,2,1,0:T(8,128)(2,1)} %spread.1.refs_2_), calls=%async_computation.1 | async-start | bytes 2621440 | tf_op jit(solution)/shard_map/all_to_all | solution.py:396
  37.0 8.4 %collective-permute-start.6 = (bf16[2,128,256]{2,1,0:T(8,128)(2,1)S(1)}, bf16[2,128,256]{2,1,0:T(8,128)(2,1)S(1)}, u32[]{:S(2)}, u32[]{:S(2)}) collective-permute-start(bf16[2,128,256]{2,1,0:T(8,128)(2,1)S(1)} %get-tuple-element.21), channel_id=1, source_target_pairs={{0,16},{1,17},{2,18},{3,19},{4,20},{5,21},{6,22},{7,23},{8,24},{9,... | collective-permute-start | bytes 393224 | tf_op jit(solution)/shard_map/ppermute | solution.py:405
  45.5 0.0 collective-permute-start.7
  45.5 1.6 %collective-permute-start.8 = (bf16[2,128,256]{2,1,0:T(8,128)(2,1)S(1)}, bf16[2,128,256]{2,1,0:T(8,128)(2,1)S(1)}, u32[]{:S(2)}, u32[]{:S(2)}) collective-permute-start(bf16[2,128,256]{2,1,0:T(8,128)(2,1)S(1)} %get-tuple-element.21), channel_id=1, source_target_pairs={{0,48},{1,49},{2,50},{3,51},{4,52},{5,53},{6,54},{7,55},{8,56},{9,... | collective-permute-start | bytes 393224 | tf_op jit(solution)/shard_map/ppermute | solution.py:405
  47.0 6.5 %collective-permute-done.6.refs_2_ = bf16[2,128,256]{2,1,0:T(8,128)(2,1)S(1)} collective-permute-done((bf16[2,128,256]{2,1,0:T(8,128)(2,1)S(1)}, bf16[2,128,256]{2,1,0:T(8,128)(2,1)S(1)}, u32[]{:S(2)}, u32[]{:S(2)}) %collective-permute-start.6) | collective-permute-done | bytes 131104 | tf_op jit(solution)/shard_map/ppermute | solution.py:405
  53.6 1.4 %collective-permute-done.7.refs_3_ = bf16[2,128,256]{2,1,0:T(8,128)(2,1)S(1)} collective-permute-done((bf16[2,128,256]{2,1,0:T(8,128)(2,1)S(1)}, bf16[2,128,256]{2,1,0:T(8,128)(2,1)S(1)}, u32[]{:S(2)}, u32[]{:S(2)}) %collective-permute-start.7) | collective-permute-done | bytes 131104 | tf_op jit(solution)/shard_map/ppermute | solution.py:405
  55.0 0.0 collective-permute-done.8.refs_4_
  55.0 0.0 all-to-all-done.1.refs_2_.refs_5_
  55.0 0.9 stack.35
  55.8 0.0 all-gather.3.cloned.1.call-update
  55.8 0.1 collective-permute-start.2
  55.9 0.1 pad_add_fusion.refs_0_
  56.0 3.1 %own.1 = (f32[1,512]{1,0:T(1,128)S(1)}, f32[1,512]{1,0:T(1,128)S(1)}, f32[128,512]{1,0:T(8,128)S(1)}) custom-call(s32[2]{0:T(128)S(1)} %pad_add_fusion.refs_0_, bf16[4,3,128,128]{3,2,1,0:T(8,128)(2,1)S(1)} %all-to-all-done.refs_0_.refs_1_, bf16[4,10,128,128]{3,2,1,0:T(8,128)(2,1)S(1)} %all-to-all-done.1.refs_2_.refs_5_), custom_call_target="tpu_custom_call" | custom-call | flops 2000000000 | bytes 2000000 | tf_op jit(solution)/shard_map/own/pallas_call | solution.py:89
  59.2 0.0 collective-permute-done.2.refs_5_.refs_3_
  59.2 4.1 %other.1.refs_1_ = bf16[2,2,256,128]{3,2,1,0:T(8,128)(2,1)} custom-call(s32[2]{0:T(128)S(1)} %pad_add_fusion.refs_0_, bf16[4,3,128,128]{3,2,1,0:T(8,128)(2,1)S(1)} %all-to-all-done.refs_0_.refs_1_, f32[1,512]{1,0:T(1,128)S(1)} %get-tuple-element.15.refs_2_, f32[1,512]{1,0:T(1,128)S(1)} %get-tuple-element.16.refs_3_, ...), custom_call_target="tpu_custom_call" | custom-call | flops 2000000000 | bytes 2000000 | tf_op jit(solution)/shard_map/other/pallas_call | solution.py:89
  63.3 10.1 %all-to-all-start.2 = ((bf16[4,256,128]{2,1,0:T(8,128)(2,1)}), bf16[4,256,128]{2,1,0:T(8,128)(2,1)S(1)}, u32[]{:S(2)}, u32[]{:S(2)}) async-start(bf16[4,256,128]{2,1,0:T(8,128)(2,1)} %bitcast.3), calls=%async_computation.2 | async-start | bytes 524288 | tf_op jit(solution)/shard_map/all_to_all | solution.py:428
  73.4 0.1 pad_add_fusion.1.refs_0_
  73.5 10.3 %all-to-all-done.2.refs_4_.refs_1_ = bf16[4,256,128]{2,1,0:T(8,128)(2,1)S(1)} async-done(((bf16[4,256,128]{2,1,0:T(8,128)(2,1)}), bf16[4,256,128]{2,1,0:T(8,128)(2,1)S(1)}, u32[]{:S(2)}, u32[]{:S(2)}) %all-to-all-start.2) | async-done | bytes 262176 | tf_op jit(solution)/shard_map/all_to_all | solution.py:428
  83.8 0.2 collective-permute-start.3
  84.0 3.0 %collective-permute-start.4 = (bf16[4,256,128]{2,1,0:T(8,128)(2,1)S(1)}, bf16[4,256,128]{2,1,0:T(8,128)(2,1)S(1)}, u32[]{:S(2)}, u32[]{:S(2)}) collective-permute-start(bf16[4,256,128]{2,1,0:T(8,128)(2,1)S(1)} %all-to-all-done.2.refs_4_.refs_1_), channel_id=1, source_target_pairs={{0,6},{2,0},{4,2},{6,4},{1,7},{3,1},{5,3},{7,5},{8,14},{10,8},{12,... | collective-permute-start | bytes 786440 | tf_op jit(solution)/shard_map/ppermute | solution.py:430
  87.1 0.7 collective-permute-start.5
  87.8 0.1 pad_add_fusion.2.refs_0_
  87.9 0.8 copy-done.1
  88.7 1.5 %combine.1 = f32[4,16,1024]{2,1,0:T(8,128)} custom-call(s32[3]{0:T(128)S(1)} %pad_add_fusion.1.refs_0_, f32[16,1024]{1,0:T(8,128)S(1)} %copy-done.1, bf16[4,10,128,128]{3,2,1,0:T(8,128)(2,1)S(1)} %all-to-all-done.1.refs_2_.refs_5_, bf16[4,10,128,128]{3,2,1,0:T(8,128)(2,1)S(1)} %collective-permute-done.2.refs_5_.refs_3_, ...), custom_call_target="tpu_custom_call" | custom-call | flops 100000000 | bytes 2000000 | tf_op jit(solution)/shard_map/combine/pallas_call | solution.py:89
  90.2 4.0 %all-to-all-start.3 = ((f32[4,16,1024]{2,1,0:T(8,128)}), f32[4,16,1024]{2,1,0:T(8,128)S(1)}, u32[]{:S(2)}, u32[]{:S(2)}) async-start(f32[4,16,1024]{2,1,0:T(8,128)} %combine.1), calls=%async_computation.3 | async-start | bytes 524288 | tf_op jit(solution)/shard_map/all_to_all | solution.py:442
  94.2 0.9 sqrt_multiply_fusion.refs_1_
  95.1 0.0 collective-permute-done.3.refs_2_
  95.1 1.7 %collective-permute-done.4.refs_3_ = bf16[4,256,128]{2,1,0:T(8,128)(2,1)S(1)} collective-permute-done((bf16[4,256,128]{2,1,0:T(8,128)(2,1)S(1)}, bf16[4,256,128]{2,1,0:T(8,128)(2,1)S(1)}, u32[]{:S(2)}, u32[]{:S(2)}) %collective-permute-start.4) | collective-permute-done | bytes 262176 | tf_op jit(solution)/shard_map/ppermute | solution.py:430
  96.8 1.6 %collective-permute-done.5.refs_4_ = bf16[4,256,128]{2,1,0:T(8,128)(2,1)} collective-permute-done((bf16[4,256,128]{2,1,0:T(8,128)(2,1)S(1)}, bf16[4,256,128]{2,1,0:T(8,128)(2,1)}, u32[]{:S(2)}, u32[]{:S(2)}) %collective-permute-start.5) | collective-permute-done | bytes 262176 | tf_op jit(solution)/shard_map/ppermute | solution.py:430
  98.4 3.8 %project.1 = (f32[128,1024]{1,0:T(8,128)S(1)}, bf16[128,1024]{1,0:T(8,128)(2,1)S(1)}) custom-call(s32[2]{0:T(128)S(1)} %pad_add_fusion.2.refs_0_, bf16[4,256,128]{2,1,0:T(8,128)(2,1)S(1)} %all-to-all-done.2.refs_4_.refs_1_, bf16[4,256,128]{2,1,0:T(8,128)(2,1)S(1)} %collective-permute-done.3.refs_2_, bf16[4,256,128]{2,1,0:T(8,128)(2,1)S(1)} %collective-permute-done.4.refs_3_, ...), custom_call_target="tpu_custom_call" | custom-call | flops 2000000000 | bytes 2000000 | tf_op jit(solution)/shard_map/project/pallas_call | solution.py:89
  102.2 0.1 collective-permute-start.9
  102.4 2.7 %mix.1 = bf16[128,1024]{1,0:T(8,128)(2,1)} custom-call(f32[16,1024]{1,0:T(8,128)S(1)} %copy-done.1, f32[16,1024]{1,0:T(8,128)S(1)} %sqrt_multiply_fusion.refs_1_, f32[4,16,1024]{2,1,0:T(8,128)S(1)} %all-to-all-done.3.refs_2_, f32[128,1024]{1,0:T(8,128)S(1)} %copy-done.3, f32[128,1024]{1,0:T(8,128)S(1)} %copy-done.5), custom_call_target="tpu_custom_call" | custom-call | flops 4000000000 | bytes 2000000 | tf_op jit(solution)/shard_map/mix/pallas_call | solution.py:89
  105.1 3.6 %collective-permute-done.9 = bf16[128,1024]{1,0:T(8,128)(2,1)S(1)} collective-permute-done((bf16[128,1024]{1,0:T(8,128)(2,1)S(1)}, bf16[128,1024]{1,0:T(8,128)(2,1)S(1)}, u32[]{:S(2)}, u32[]{:S(2)}) %collective-permute-start.9) | collective-permute-done | bytes 262176 | tf_op jit(solution)/shard_map/ppermute | solution.py:457
  108.7 0.8 add_convert_fusion
  (14 shorter events, 0.0 us)
Async XLA Ops:
  7.2 8.8 %copy-start.6 = (bf16[512,256]{1,0:T(8,128)(2,1)S(1)}, bf16[512,256]{1,0:T(8,128)(2,1)}, u32[]{:S(2)}) copy-start(bf16[512,256]{1,0:T(8,128)(2,1)} %param.11) | copy-start | bytes 786436
  10.0 20.9 %all-to-all-start = ((bf16[4,3,128,128]{3,2,1,0:T(8,128)(2,1)}), bf16[4,3,128,128]{3,2,1,0:T(8,128)(2,1)S(1)}, u32[]{:S(2)}, u32[]{:S(2)}) async-start(bf16[4,3,128,128]{3,2,1,0:T(8,128)(2,1)} %pack.1), calls=%async_computation | async-start | bytes 786432 | tf_op jit(solution)/shard_map/all_to_all | solution.py:370
  16.0 14.8 %collective-permute-start.1 = (bf16[512,256]{1,0:T(8,128)(2,1)S(1)}, bf16[512,256]{1,0:T(8,128)(2,1)S(1)}, u32[]{:S(2)}, u32[]{:S(2)}) collective-permute-start(bf16[512,256]{1,0:T(8,128)(2,1)S(1)} %copy-done.6), channel_id=1, source_target_pairs={{0,0},{1,32},{2,64},{3,96},{4,128},{5,160},{6,192},{7,224},{8,8},{... | collective-permute-start | bytes 786440 | tf_op jit(solution)/shard_map/ppermute | solution.py:387
  20.9 5.1 %collective-permute-start = (f32[3,2,1024]{2,1,0:T(2,128)S(1)}, f32[3,2,1024]{2,1,0:T(2,128)S(1)}, u32[]{:S(2)}, u32[]{:S(2)}) collective-permute-start(f32[3,2,1024]{2,1,0:T(2,128)S(1)} %tail.1.refs_1_), channel_id=1, source_target_pairs={{0,8},{1,9},{2,10},{3,11},{4,12},{5,13},{6,14},{7,15},{8,16},{9,17... | collective-permute-start | bytes 73736 | tf_op jit(solution)/shard_map/ppermute | solution.py:371
  28.5 0.6 copy-start
  29.2 0.8 copy-start.2
  30.0 0.8 copy-start.4
  32.1 22.9 %all-to-all-start.1 = ((bf16[4,10,128,128]{3,2,1,0:T(8,128)(2,1)}), bf16[4,10,128,128]{3,2,1,0:T(8,128)(2,1)S(1)}, u32[]{:S(2)}, u32[]{:S(2)}) async-start(bf16[4,10,128,128]{3,2,1,0:T(8,128)(2,1)} %spread.1.refs_2_), calls=%async_computation.1 | async-start | bytes 2621440 | tf_op jit(solution)/shard_map/all_to_all | solution.py:396
  37.0 61.4 %all-gather.3.cloned.1.call-start = ((), (), s32[]{:S(2)}) async-start(), calls=%async_computation.4 | async-start | bytes 4718592 | tf_op jit(solution)/shard_map/all_gather | solution.py:411
  37.0 16.5 %collective-permute-start.6 = (bf16[2,128,256]{2,1,0:T(8,128)(2,1)S(1)}, bf16[2,128,256]{2,1,0:T(8,128)(2,1)S(1)}, u32[]{:S(2)}, u32[]{:S(2)}) collective-permute-start(bf16[2,128,256]{2,1,0:T(8,128)(2,1)S(1)} %get-tuple-element.21), channel_id=1, source_target_pairs={{0,16},{1,17},{2,18},{3,19},{4,20},{5,21},{6,22},{7,23},{8,24},{9,... | collective-permute-start | bytes 393224 | tf_op jit(solution)/shard_map/ppermute | solution.py:405
  45.5 9.5 %collective-permute-start.7 = (bf16[2,128,256]{2,1,0:T(8,128)(2,1)S(1)}, bf16[2,128,256]{2,1,0:T(8,128)(2,1)S(1)}, u32[]{:S(2)}, u32[]{:S(2)}) collective-permute-start(bf16[2,128,256]{2,1,0:T(8,128)(2,1)S(1)} %get-tuple-element.20.refs_1_), channel_id=1, source_target_pairs={{0,32},{1,33},{2,34},{3,35},{4,36},{5,37},{6,38},{7,39},{8,40},{9,... | collective-permute-start | bytes 393224 | tf_op jit(solution)/shard_map/ppermute | solution.py:405
  45.5 9.5 %collective-permute-start.8 = (bf16[2,128,256]{2,1,0:T(8,128)(2,1)S(1)}, bf16[2,128,256]{2,1,0:T(8,128)(2,1)S(1)}, u32[]{:S(2)}, u32[]{:S(2)}) collective-permute-start(bf16[2,128,256]{2,1,0:T(8,128)(2,1)S(1)} %get-tuple-element.21), channel_id=1, source_target_pairs={{0,48},{1,49},{2,50},{3,51},{4,52},{5,53},{6,54},{7,55},{8,56},{9,... | collective-permute-start | bytes 393224 | tf_op jit(solution)/shard_map/ppermute | solution.py:405
  55.8 3.3 %collective-permute-start.2 = (bf16[4,10,128,128]{3,2,1,0:T(8,128)(2,1)S(1)}, bf16[4,10,128,128]{3,2,1,0:T(8,128)(2,1)S(1)}, u32[]{:S(2)}, u32[]{:S(2)}) collective-permute-start(bf16[4,10,128,128]{3,2,1,0:T(8,128)(2,1)S(1)} %all-to-all-done.1.refs_2_.refs_5_), channel_id=1, source_target_pairs={{0,8},{8,0},{1,9},{9,1},{2,10},{10,2},{3,11},{11,3},{4,12},{12,4},... | collective-permute-start | bytes 3932168 | tf_op jit(solution)/shard_map/ppermute | solution.py:397
  63.3 20.5 %all-to-all-start.2 = ((bf16[4,256,128]{2,1,0:T(8,128)(2,1)}), bf16[4,256,128]{2,1,0:T(8,128)(2,1)S(1)}, u32[]{:S(2)}, u32[]{:S(2)}) async-start(bf16[4,256,128]{2,1,0:T(8,128)(2,1)} %bitcast.3), calls=%async_computation.2 | async-start | bytes 524288 | tf_op jit(solution)/shard_map/all_to_all | solution.py:428
  83.8 11.3 %collective-permute-start.3 = (bf16[4,256,128]{2,1,0:T(8,128)(2,1)S(1)}, bf16[4,256,128]{2,1,0:T(8,128)(2,1)S(1)}, u32[]{:S(2)}, u32[]{:S(2)}) collective-permute-start(bf16[4,256,128]{2,1,0:T(8,128)(2,1)S(1)} %all-to-all-done.2.refs_4_.refs_1_), channel_id=1, source_target_pairs={{0,2},{2,4},{4,6},{6,0},{1,3},{3,5},{5,7},{7,1},{8,10},{10,12},{12... | collective-permute-start | bytes 786440 | tf_op jit(solution)/shard_map/ppermute | solution.py:430
  84.0 12.7 %collective-permute-start.4 = (bf16[4,256,128]{2,1,0:T(8,128)(2,1)S(1)}, bf16[4,256,128]{2,1,0:T(8,128)(2,1)S(1)}, u32[]{:S(2)}, u32[]{:S(2)}) collective-permute-start(bf16[4,256,128]{2,1,0:T(8,128)(2,1)S(1)} %all-to-all-done.2.refs_4_.refs_1_), channel_id=1, source_target_pairs={{0,6},{2,0},{4,2},{6,4},{1,7},{3,1},{5,3},{7,5},{8,14},{10,8},{12,... | collective-permute-start | bytes 786440 | tf_op jit(solution)/shard_map/ppermute | solution.py:430
  87.1 11.3 %collective-permute-start.5 = (bf16[4,256,128]{2,1,0:T(8,128)(2,1)S(1)}, bf16[4,256,128]{2,1,0:T(8,128)(2,1)}, u32[]{:S(2)}, u32[]{:S(2)}) collective-permute-start(bf16[4,256,128]{2,1,0:T(8,128)(2,1)S(1)} %all-to-all-done.2.refs_4_.refs_1_), channel_id=1, source_target_pairs={{0,4},{2,6},{4,0},{6,2},{1,5},{3,7},{5,1},{7,3},{8,12},{10,14},{12... | collective-permute-start | bytes 786440 | tf_op jit(solution)/shard_map/ppermute | solution.py:430
  87.9 0.8 copy-start.1
  90.2 12.1 %all-to-all-start.3 = ((f32[4,16,1024]{2,1,0:T(8,128)}), f32[4,16,1024]{2,1,0:T(8,128)S(1)}, u32[]{:S(2)}, u32[]{:S(2)}) async-start(f32[4,16,1024]{2,1,0:T(8,128)} %combine.1), calls=%async_computation.3 | async-start | bytes 524288 | tf_op jit(solution)/shard_map/all_to_all | solution.py:442
  98.4 4.0 %copy-start.3 = (f32[128,1024]{1,0:T(8,128)S(1)}, f32[128,1024]{1,0:T(8,128)}, u32[]{:S(2)}) copy-start(f32[128,1024]{1,0:T(8,128)} %copy-done.2) | copy-start | bytes 1572868
  98.4 4.0 %copy-start.5 = (f32[128,1024]{1,0:T(8,128)S(1)}, f32[128,1024]{1,0:T(8,128)}, u32[]{:S(2)}) copy-start(f32[128,1024]{1,0:T(8,128)} %copy-done.4) | copy-start | bytes 1572868
  102.2 6.5 %collective-permute-start.9 = (bf16[128,1024]{1,0:T(8,128)(2,1)S(1)}, bf16[128,1024]{1,0:T(8,128)(2,1)S(1)}, u32[]{:S(2)}, u32[]{:S(2)}) collective-permute-start(bf16[128,1024]{1,0:T(8,128)(2,1)S(1)} %get-tuple-element.23), channel_id=1, source_target_pairs={{0,16},{16,0},{1,17},{17,1},{2,18},{18,2},{3,19},{19,3},{4,20},{20... | collective-permute-start | bytes 786440 | tf_op jit(solution)/shard_map/ppermute | solution.py:457
Sparse Core Ops, SparseCore 0:
  56.0 36.4 all-gather.2

commit v3 on v2

--- a/solution.py
+++ b/solution.py
@@ -66,6 +66,10 @@
 ANY = pl.BlockSpec(memory_space=pl.ANY)
 
 
+def placed_out(out):
+    return FAST if isinstance(out, jax.ShapeDtypeStruct) else SLOW
+
+
 def local_call(kernel, out_shape, specs, name, flops, scratch=(), after=()):
     count = len(specs)
 
@@ -76,7 +80,7 @@
         body,
         out_shape=out_shape,
         in_specs=list(specs) + [ANY] * len(after),
-        out_specs=jax.tree.map(lambda _: FAST, out_shape),
+        out_specs=jax.tree.map(placed_out, out_shape),
         scratch_shapes=list(scratch),
         compiler_params=pltpu.CompilerParams(vmem_limit_bytes=VMEM),
         cost_estimate=pl.CostEstimate(flops=flops, bytes_accessed=2_000_000, transcendentals=0),
@@ -128,7 +132,8 @@
 
 
 def ends_kernel(
-    feats, halo_ref, taps_hbm, decay_hbm, out_ref, prod, gate_rows, rate, x, taps, ext, sems
+    feats, halo_ref, taps_hbm, decay_hbm, out_ref, prod_hbm, gate_hbm, rate_hbm,
+    x, taps, rate, prod, gate_rows, ext, sems, out_sems,
 ):
     finished(started(sems, ((feats, x), (taps_hbm, taps), (decay_hbm, rate))))
     rows, order = x.shape[1], rate.shape[0]
@@ -137,6 +142,7 @@
         gate_rows[lo : lo + 16] = featured_rows(ext, taps, 0, 0, lo, 16)
         first = featured_rows(ext, taps, 1, 1, lo, 16)
         prod[lo : lo + 16] = first * featured_rows(ext, taps, 2, 2, lo, 16)
+    written = started(out_sems, ((prod, prod_hbm), (gate_rows, gate_hbm), (rate, rate_hbm)))
     decay = jnp.exp(-rate[...])
 
     def body(i, state):
@@ -153,11 +159,13 @@
         out_ref[1, j * order : (j + 1) * order] = (block - high.astype(jnp.float32)).astype(
             jnp.bfloat16
         )
-
-
-def combine_kernel(place_ref, decay_ref, own_ref, other_ref, out_ref, ends):
+    finished(written)
+
+
+def combine_kernel(place_ref, rate_hbm, own_ref, other_ref, out_ref, rate_ref, ends, sems):
+    finished(started(sems, ((rate_hbm, rate_ref),)))
     x, z, k = place_ref[0], place_ref[1], place_ref[2]
-    rate = decay_ref[...]
+    rate = rate_ref[...]
     order = rate.shape[0]
 
     def over(blocks):
@@ -186,9 +194,12 @@
         out_ref[target] = total
 
 
-def mix_kernel(decay_ref, rho_ref, parts_ref, prod, gate_rows, out_ref):
+def mix_kernel(
+    rate_hbm, rho_ref, parts_ref, prod_hbm, gate_hbm, out_ref, rate, prod, gate_rows, sems
+):
+    finished(started(sems, ((rate_hbm, rate), (prod_hbm, prod), (gate_hbm, gate_rows))))
     rows, width = prod.shape
-    decay = jnp.exp(-decay_ref[...])
+    decay = jnp.exp(-rate[...])
     start = parts_ref[0]
     for z in range(1, NZ):
         start = start + parts_ref[z]
@@ -219,11 +230,8 @@
 
 
 def pack_kernel(qkv, out_ref, sems):
-    pairs = []
-    for head in range(NZ):
-        lanes = pl.ds(head * HEAD, HEAD)
-        pairs += [(qkv.at[i, :, lanes], out_ref.at[head, i]) for i in range(3)]
-    finished(started(sems, pairs))
+    lanes = [pl.ds(head * HEAD, HEAD) for head in range(NZ)]
+    finished(started(sems, [(qkv.at[:, :, lanes[i]], out_ref.at[i]) for i in range(NZ)]))
 
 
 def halves_kernel(place_ref, weight_ref, same_ref, other_ref):
@@ -364,23 +372,32 @@
         (SLOW,),
         "pack",
         10**8,
-        (dma((3 * NZ,)),),
+        (dma((NZ,)),),
         after=(tail,),
     )(attn_qkv)
-    qkv = lax.all_to_all(packed, ("z1", "z0"), 0, 0)
     halo = lax.ppermute(tail, ALL, moved(next_ctx))
+    qkv = lax.all_to_all(gate(packed, halo), ("z1", "z0"), 0, 0)
     plane = short((rows, width), f32)
     poles = short(decay_rate.shape, f32)
     ends, prod, gate_rows, rate = local_call(
         ends_kernel,
-        (short((2, rows, HEAD), bf16), plane, plane, poles),
+        (
+            short((2, rows, HEAD), bf16),
+            pltpu.HBM(plane.shape, f32),
+            pltpu.HBM(plane.shape, f32),
+            pltpu.HBM(poles.shape, f32),
+        ),
         (SLOW, FAST, SLOW, SLOW),
         "ends",
         10**9,
         (
             pltpu.VMEM((3, rows, width), bf16),
             pltpu.VMEM(short_taps.shape, f32),
+            pltpu.VMEM(poles.shape, f32),
+            pltpu.VMEM(plane.shape, f32),
+            pltpu.VMEM(plane.shape, f32),
             pltpu.VMEM((3, rows + 8, width), f32),
+            dma((3,)),
             dma((3,)),
         ),
     )(hyena_feats, halo, short_taps, decay_rate)
@@ -424,7 +441,6 @@
         2 * 10**9,
         [pltpu.VMEM(part.shape, f32) for part in (line, line, square)],
     )(where, qkv, *partial, far_other)
-    rate = gate(rate, attended)
     group = lax.all_to_all(attended.reshape(NH * NZ1, NZ0 * rows, HEAD), ("h", "z1"), 0, 0)
     groups = [group] + [
         lax.ppermute(group, "y", [(i, (i + step) % NY) for i in range(NY)]) for step in (1, 3, 2)
@@ -433,12 +449,12 @@
     parts = local_call(
         combine_kernel,
         short((NZ, *poles.shape), f32),
-        (SMEM, FAST, FAST, FAST),
+        (SMEM, SLOW, FAST, FAST),
         "combine",
         10**8,
-        (pltpu.VMEM((NX, NK, *poles.shape), f32),),
+        (pltpu.VMEM(poles.shape, f32), pltpu.VMEM((NX, NK, *poles.shape), f32), dma((1,))),
         after=(group,),
-    )(jnp.stack([x, 2 * z1 + z0, k]), rate, far_own, far_other)
+    )(jnp.stack([x, 2 * z1 + z0, k]), decay_rate, far_own, far_other)
     parts = lax.all_to_all(parts, ("z1", "z0"), 0, 0)
 
     mine, other = local_call(
@@ -460,10 +476,16 @@
     hyena_mixed = local_call(
         mix_kernel,
         short((rows, width), bf16),
-        (FAST,) * 5,
+        (SLOW, FAST, FAST, SLOW, SLOW),
         "mix",
         4 * 10**9,
-    )(rate, rho, parts, prod, gate_rows)
+        (
+            pltpu.VMEM(poles.shape, f32),
+            pltpu.VMEM(plane.shape, f32),
+            pltpu.VMEM(plane.shape, f32),
+            dma((3,)),
+        ),
+    )(decay_rate, rho, parts, prod, gate_rows)
     return hyena_mixed, (mine + received.astype(f32)).astype(bf16)
 
 

time: 117 us -> 123 us (1.051)
  starting transfers between devices: 46.1 us -> 50.6 us
  Pallas kernels: 22.7 us -> 24.3 us
    ppermute x1, waiting for transfers between devices: 0.01 us -> 3.34 us  [per_device(): moved_weight = lax.ppermute(out_weight, ALL, moved(place_weight))]
    ppermute x1, waiting for transfers between devices: 3.22 us -> 1.37 us  [per_device(): halo = lax.ppermute(tail, ALL, moved(next_ctx))]
    all_to_all x1, starting transfers between devices: 10.1 us -> 11.9 us  [per_device(): lax.all_to_all(attended.reshape(NH * NZ1, NZ0 * rows, HEAD), ('h', 'z1'),...]
    ppermute x3, starting transfers between devices: 9.99 us -> 11.7 us  [per_device(): lax.ppermute(opposite if steps % 2 else same, ALL, along_z(steps))]
    pallas_call x11, Pallas kernels: 22.7 us -> 24.3 us  [local_call(): return lambda *operands: call(*map(placed, operands, specs), *after)]
    ppermute x1, waiting for transfers between devices: 3.59 us -> 2.34 us  [per_device(): received = lax.ppermute(other, 'z0', swap)]
    unnamed x14 -> x10, local copies, waits for them, and re-layouts: 3.1 us -> 2.1 us
  transfers between devices with their start and end apart: 15 -> 15, of which waited for: 7 -> 9; matrix products, arithmetic and copies ran while one was open for 1% -> 1% of each run, Pallas kernels for 15% -> 17%
where the time goes in v3:
time: 123 us; the launch traced here: 122 us
  starting transfers between devices  50.6 us (41%)
  waiting for transfers between devices  29.2 us (24%)
  Pallas kernels  24.3 us (20%)
  between operations  14.2 us (12%)
  local copies, waits for them, and re-layouts  2.1 us (2%)
  other arithmetic  1.87 us (2%)
    pallas_call x11, Pallas kernels, local_call(): return lambda *operands: call(*map(placed, operands, specs), *after)  24.3 us
    all_to_all x1, starting transfers between devices, per_device(): lax.all_to_all(attended.reshape(NH * NZ1, NZ0 * rows, HEAD), ('h', 'z1'),...  11.9 us
    ppermute x3, starting transfers between devices, per_device(): lax.ppermute(opposite if steps % 2 else same, ALL, along_z(steps))  11.7 us
    all_to_all x1, waiting for transfers between devices, per_device(): lax.all_to_all(attended.reshape(NH * NZ1, NZ0 * rows, HEAD), ('h', 'z1'),...  10.3 us
    ppermute x3, waiting for transfers between devices, per_device(): lax.ppermute(opposite if steps % 2 else same, ALL, along_z(steps))  8.51 us
    all_to_all x1, starting transfers between devices, per_device(): qkv = lax.all_to_all(gate(packed, halo), ('z1', 'z0'), 0, 0)  6.23 us
    all_to_all x1, starting transfers between devices, per_device(): far_own = lax.all_to_all(spread, 'x', 0, 0)  5.36 us
    ppermute x1, starting transfers between devices, per_device(): moved_weight = lax.ppermute(out_weight, ALL, moved(place_weight))  4.91 us
  transfers between devices with their start and end apart: 15, of which 9 were waited for; matrix products, arithmetic and copies ran while one was open for 1% of the time, Pallas kernels for 17%

profile of v3, /device:TPU:38, one launch (start us, length us, event | category | flops | bytes accessed | tf_op | source)
XLA Modules:
  0.0 122.2 jit_solution(15524518931292639896)
XLA Ops:
  7.2 0.9 tail.1.refs_1_
  8.1 0.0 copy-start.4
  8.1 2.1 %collective-permute-start = (f32[3,2,1024]{2,1,0:T(2,128)S(1)}, f32[3,2,1024]{2,1,0:T(2,128)S(1)}, u32[]{:S(2)}, u32[]{:S(2)}) collective-permute-start(f32[3,2,1024]{2,1,0:T(2,128)S(1)} %tail.1.refs_1_), channel_id=1, source_target_pairs={{0,8},{1,9},{2,10},{3,11},{4,12},{5,13},{6,14},{7,15},{8,16},{9,17... | collective-permute-start | bytes 73736 | tf_op jit(solution)/shard_map/ppermute | solution.py:378
  10.2 1.1 pack.1.refs_0_
  11.3 0.7 copy-done
  12.0 1.4 %collective-permute-done.refs_1_ = f32[3,2,1024]{2,1,0:T(2,128)S(1)} collective-permute-done((f32[3,2,1024]{2,1,0:T(2,128)S(1)}, f32[3,2,1024]{2,1,0:T(2,128)S(1)}, u32[]{:S(2)}, u32[]{:S(2)}) %collective-permute-start) | collective-permute-done | bytes 24608 | tf_op jit(solution)/shard_map/ppermute | solution.py:378
  13.4 0.6 copy-done.1
  14.0 6.2 %all-to-all-start = ((bf16[4,3,128,128]{3,2,1,0:T(8,128)(2,1)}), bf16[4,3,128,128]{3,2,1,0:T(8,128)(2,1)S(1)}, u32[]{:S(2)}, u32[]{:S(2)}) async-start(bf16[4,3,128,128]{3,2,1,0:T(8,128)(2,1)} %gate.1), calls=%async_computation | async-start | bytes 786432 | tf_op jit(solution)/shard_map/all_to_all | solution.py:379
  20.2 4.9 %collective-permute-start.1 = (bf16[512,256]{1,0:T(8,128)(2,1)S(1)}, bf16[512,256]{1,0:T(8,128)(2,1)S(1)}, u32[]{:S(2)}, u32[]{:S(2)}) collective-permute-start(bf16[512,256]{1,0:T(8,128)(2,1)S(1)} %copy-done.4), channel_id=1, source_target_pairs={{0,0},{1,32},{2,64},{3,96},{4,128},{5,160},{6,192},{7,224},{8,8},{... | collective-permute-start | bytes 786440 | tf_op jit(solution)/shard_map/ppermute | solution.py:404
  25.1 0.0 copy-start.2
  25.2 0.7 copy-done.2
  25.9 2.9 %ends.1 = (bf16[2,128,128]{2,1,0:T(8,128)(2,1)S(1)}, f32[128,1024]{1,0:T(8,128)}, f32[128,1024]{1,0:T(8,128)}, f32[16,1024]{1,0:T(8,128)}) custom-call(bf16[3,128,1024]{2,1,0:T(8,128)(2,1)} %refs_0_.5, f32[3,2,1024]{2,1,0:T(2,128)S(1)} %copy-done.2, f32[3,3,1024]{2,1,0:T(4,128)} %refs_2_.1, f32[16,1024]{1,0:T(8,128)} %refs_0_.7), custom_call_target="tpu_custom_call" | custom-call | flops 1000000000 | bytes 2000000 | tf_op jit(solution)/shard_map/ends/pallas_call | solution.py:93
  28.8 3.3 %collective-permute-done.1.refs_2_.refs_1_ = bf16[512,256]{1,0:T(8,128)(2,1)S(1)} collective-permute-done((bf16[512,256]{1,0:T(8,128)(2,1)S(1)}, bf16[512,256]{1,0:T(8,128)(2,1)S(1)}, u32[]{:S(2)}, u32[]{:S(2)}) %collective-permute-start.1) | collective-permute-done | bytes 262176 | tf_op jit(solution)/shard_map/ppermute | solution.py:404
  32.1 0.0 all-to-all-done.refs_0_.refs_1_
  32.1 1.2 %spread.1.refs_2_ = bf16[4,10,128,128]{3,2,1,0:T(8,128)(2,1)} custom-call(bf16[4,3,128,128]{3,2,1,0:T(8,128)(2,1)S(1)} %all-to-all-done.refs_0_.refs_1_, bf16[2,128,128]{2,1,0:T(8,128)(2,1)S(1)} %get-tuple-element.14.refs_1_, bf16[512,256]{1,0:T(8,128)(2,1)S(1)} %collective-permute-done.1.refs_2_.refs_1_), custom_call_target="tpu_custom_call" | custom-call | flops 100000000 | bytes 2000000 | tf_op jit(solution)/shard_map/spread/pallas_call | solution.py:93
  33.4 5.4 %all-to-all-start.1 = ((bf16[4,10,128,128]{3,2,1,0:T(8,128)(2,1)}), bf16[4,10,128,128]{3,2,1,0:T(8,128)(2,1)S(1)}, u32[]{:S(2)}, u32[]{:S(2)}) async-start(bf16[4,10,128,128]{3,2,1,0:T(8,128)(2,1)} %spread.1.refs_2_), calls=%async_computation.1 | async-start | bytes 2621440 | tf_op jit(solution)/shard_map/all_to_all | solution.py:413
  38.8 10.2 %collective-permute-start.6 = (bf16[2,128,256]{2,1,0:T(8,128)(2,1)S(1)}, bf16[2,128,256]{2,1,0:T(8,128)(2,1)S(1)}, u32[]{:S(2)}, u32[]{:S(2)}) collective-permute-start(bf16[2,128,256]{2,1,0:T(8,128)(2,1)S(1)} %get-tuple-element.21), channel_id=1, source_target_pairs={{0,16},{1,17},{2,18},{3,19},{4,20},{5,21},{6,22},{7,23},{8,24},{9,... | collective-permute-start | bytes 393224 | tf_op jit(solution)/shard_map/ppermute | solution.py:422
  49.0 0.0 collective-permute-start.7
  49.0 1.6 %collective-permute-start.8 = (bf16[2,128,256]{2,1,0:T(8,128)(2,1)S(1)}, bf16[2,128,256]{2,1,0:T(8,128)(2,1)S(1)}, u32[]{:S(2)}, u32[]{:S(2)}) collective-permute-start(bf16[2,128,256]{2,1,0:T(8,128)(2,1)S(1)} %get-tuple-element.21), channel_id=1, source_target_pairs={{0,48},{1,49},{2,50},{3,51},{4,52},{5,53},{6,54},{7,55},{8,56},{9,... | collective-permute-start | bytes 393224 | tf_op jit(solution)/shard_map/ppermute | solution.py:422
  50.5 5.1 %collective-permute-done.6.refs_2_ = bf16[2,128,256]{2,1,0:T(8,128)(2,1)S(1)} collective-permute-done((bf16[2,128,256]{2,1,0:T(8,128)(2,1)S(1)}, bf16[2,128,256]{2,1,0:T(8,128)(2,1)S(1)}, u32[]{:S(2)}, u32[]{:S(2)}) %collective-permute-start.6) | collective-permute-done | bytes 131104 | tf_op jit(solution)/shard_map/ppermute | solution.py:422
  55.6 1.4 %collective-permute-done.7.refs_3_ = bf16[2,128,256]{2,1,0:T(8,128)(2,1)S(1)} collective-permute-done((bf16[2,128,256]{2,1,0:T(8,128)(2,1)S(1)}, bf16[2,128,256]{2,1,0:T(8,128)(2,1)S(1)}, u32[]{:S(2)}, u32[]{:S(2)}) %collective-permute-start.7) | collective-permute-done | bytes 131104 | tf_op jit(solution)/shard_map/ppermute | solution.py:422
  57.0 2.0 %collective-permute-done.8.refs_4_ = bf16[2,128,256]{2,1,0:T(8,128)(2,1)S(1)} collective-permute-done((bf16[2,128,256]{2,1,0:T(8,128)(2,1)S(1)}, bf16[2,128,256]{2,1,0:T(8,128)(2,1)S(1)}, u32[]{:S(2)}, u32[]{:S(2)}) %collective-permute-start.8) | collective-permute-done | bytes 131104 | tf_op jit(solution)/shard_map/ppermute | solution.py:422
  59.0 0.0 all-to-all-done.1.refs_2_.refs_5_
  59.0 0.8 stack.35
  59.9 0.0 all-gather.3.cloned.1.call-update
  59.9 0.1 collective-permute-start.2
  60.0 0.1 pad_add_fusion.1.refs_0_
  60.1 3.1 %own.1 = (f32[1,512]{1,0:T(1,128)S(1)}, f32[1,512]{1,0:T(1,128)S(1)}, f32[128,512]{1,0:T(8,128)S(1)}) custom-call(s32[2]{0:T(128)S(1)} %pad_add_fusion.1.refs_0_, bf16[4,3,128,128]{3,2,1,0:T(8,128)(2,1)S(1)} %all-to-all-done.refs_0_.refs_1_, bf16[4,10,128,128]{3,2,1,0:T(8,128)(2,1)S(1)} %all-to-all-done.1.refs_2_.refs_5_), custom_call_target="tpu_custom_call" | custom-call | flops 2000000000 | bytes 2000000 | tf_op jit(solution)/shard_map/own/pallas_call | solution.py:93
  63.2 0.0 collective-permute-done.2.refs_5_.refs_3_
  63.2 4.1 %other.1 = bf16[2,2,256,128]{3,2,1,0:T(8,128)(2,1)} custom-call(s32[2]{0:T(128)S(1)} %pad_add_fusion.1.refs_0_, bf16[4,3,128,128]{3,2,1,0:T(8,128)(2,1)S(1)} %all-to-all-done.refs_0_.refs_1_, f32[1,512]{1,0:T(1,128)S(1)} %get-tuple-element.15.refs_2_, f32[1,512]{1,0:T(1,128)S(1)} %get-tuple-element.16.refs_3_, f32[128,512]{1,0:T(8,128)S(1)} %get-tuple-element.17.refs_4_, ...), custom_call_target="tpu_custom_call" | custom-call | flops 2000000000 | bytes 2000000 | tf_op jit(solution)/shard_map/other/pallas_call | solution.py:93
  67.3 11.9 %all-to-all-start.2 = ((bf16[4,256,128]{2,1,0:T(8,128)(2,1)}), bf16[4,256,128]{2,1,0:T(8,128)(2,1)S(1)}, u32[]{:S(2)}, u32[]{:S(2)}) async-start(bf16[4,256,128]{2,1,0:T(8,128)(2,1)} %bitcast.3), calls=%async_computation.2 | async-start | bytes 524288 | tf_op jit(solution)/shard_map/all_to_all | solution.py:444
  79.2 0.1 pad_add_fusion.refs_0_
  79.3 10.3 %all-to-all-done.2.refs_4_.refs_1_ = bf16[4,256,128]{2,1,0:T(8,128)(2,1)S(1)} async-done(((bf16[4,256,128]{2,1,0:T(8,128)(2,1)}), bf16[4,256,128]{2,1,0:T(8,128)(2,1)S(1)}, u32[]{:S(2)}, u32[]{:S(2)}) %all-to-all-start.2) | async-done | bytes 262176 | tf_op jit(solution)/shard_map/all_to_all | solution.py:444
  89.6 0.0 collective-permute-start.3
  89.6 3.2 %collective-permute-start.4 = (bf16[4,256,128]{2,1,0:T(8,128)(2,1)S(1)}, bf16[4,256,128]{2,1,0:T(8,128)(2,1)S(1)}, u32[]{:S(2)}, u32[]{:S(2)}) collective-permute-start(bf16[4,256,128]{2,1,0:T(8,128)(2,1)S(1)} %all-to-all-done.2.refs_4_.refs_1_), channel_id=1, source_target_pairs={{0,6},{2,0},{4,2},{6,4},{1,7},{3,1},{5,3},{7,5},{8,14},{10,8},{12,... | collective-permute-start | bytes 786440 | tf_op jit(solution)/shard_map/ppermute | solution.py:446
  92.9 0.9 collective-permute-start.5
  93.8 0.1 pad_add_fusion.2.refs_0_
  93.9 2.3 %combine.1 = f32[4,16,1024]{2,1,0:T(8,128)} custom-call(s32[3]{0:T(128)S(1)} %pad_add_fusion.refs_0_, f32[16,1024]{1,0:T(8,128)} %refs_0_.7, bf16[4,10,128,128]{3,2,1,0:T(8,128)(2,1)S(1)} %all-to-all-done.1.refs_2_.refs_5_, bf16[4,10,128,128]{3,2,1,0:T(8,128)(2,1)S(1)} %collective-permute-done.2.refs_5_.refs_3_, ...), custom_call_target="tpu_custom_call" | custom-call | flops 100000000 | bytes 2000000 | tf_op jit(solution)/shard_map/combine/pallas_call | solution.py:93
  96.2 4.0 %all-to-all-start.3 = ((f32[4,16,1024]{2,1,0:T(8,128)}), f32[4,16,1024]{2,1,0:T(8,128)S(1)}, u32[]{:S(2)}, u32[]{:S(2)}) async-start(f32[4,16,1024]{2,1,0:T(8,128)} %combine.1), calls=%async_computation.3 | async-start | bytes 524288 | tf_op jit(solution)/shard_map/all_to_all | solution.py:458
  100.2 0.9 sqrt_multiply_fusion.refs_1_
  101.1 0.0 collective-permute-done.3.refs_2_
  101.1 1.5 %collective-permute-done.4.refs_3_ = bf16[4,256,128]{2,1,0:T(8,128)(2,1)S(1)} collective-permute-done((bf16[4,256,128]{2,1,0:T(8,128)(2,1)S(1)}, bf16[4,256,128]{2,1,0:T(8,128)(2,1)S(1)}, u32[]{:S(2)}, u32[]{:S(2)}) %collective-permute-start.4) | collective-permute-done | bytes 262176 | tf_op jit(solution)/shard_map/ppermute | solution.py:446
  102.6 1.8 %collective-permute-done.5.refs_4_ = bf16[4,256,128]{2,1,0:T(8,128)(2,1)} collective-permute-done((bf16[4,256,128]{2,1,0:T(8,128)(2,1)S(1)}, bf16[4,256,128]{2,1,0:T(8,128)(2,1)}, u32[]{:S(2)}, u32[]{:S(2)}) %collective-permute-start.5) | collective-permute-done | bytes 262176 | tf_op jit(solution)/shard_map/ppermute | solution.py:446
  104.4 3.8 %project.1 = (f32[128,1024]{1,0:T(8,128)S(1)}, bf16[128,1024]{1,0:T(8,128)(2,1)S(1)}) custom-call(s32[2]{0:T(128)S(1)} %pad_add_fusion.2.refs_0_, bf16[4,256,128]{2,1,0:T(8,128)(2,1)S(1)} %all-to-all-done.2.refs_4_.refs_1_, bf16[4,256,128]{2,1,0:T(8,128)(2,1)S(1)} %collective-permute-done.3.refs_2_, bf16[4,256,128]{2,1,0:T(8,128)(2,1)S(1)} %collective-permute-done.4.refs_3_, ...), custom_call_target="tpu_custom_call" | custom-call | flops 2000000000 | bytes 2000000 | tf_op jit(solution)/shard_map/project/pallas_call | solution.py:93
  108.1 0.1 collective-permute-start.9
  108.2 4.0 %mix.1 = bf16[128,1024]{1,0:T(8,128)(2,1)} custom-call(f32[16,1024]{1,0:T(8,128)} %refs_0_.7, f32[16,1024]{1,0:T(8,128)S(1)} %sqrt_multiply_fusion.refs_1_, f32[4,16,1024]{2,1,0:T(8,128)S(1)} %all-to-all-done.3.refs_2_, f32[128,1024]{1,0:T(8,128)} %get-tuple-element.18.refs_3_, f32[128,1024]{1,0:T(8,128)} %get-tuple-element.19.refs_4_), custom_call_target="tpu_custom_call" | custom-call | flops 4000000000 | bytes 2000000 | tf_op jit(solution)/shard_map/mix/pallas_call | solution.py:93
  112.2 2.3 %collective-permute-done.9 = bf16[128,1024]{1,0:T(8,128)(2,1)S(1)} collective-permute-done((bf16[128,1024]{1,0:T(8,128)(2,1)S(1)}, bf16[128,1024]{1,0:T(8,128)(2,1)S(1)}, u32[]{:S(2)}, u32[]{:S(2)}) %collective-permute-start.9) | collective-permute-done | bytes 262176 | tf_op jit(solution)/shard_map/ppermute | solution.py:473
  114.6 0.8 add_convert_fusion
  (10 shorter events, 0.0 us)
Async XLA Ops:
  8.1 12.1 %copy-start.4 = (bf16[512,256]{1,0:T(8,128)(2,1)S(1)}, bf16[512,256]{1,0:T(8,128)(2,1)}, u32[]{:S(2)}) copy-start(bf16[512,256]{1,0:T(8,128)(2,1)} %param.11) | copy-start | bytes 786436
  8.1 5.3 %collective-permute-start = (f32[3,2,1024]{2,1,0:T(2,128)S(1)}, f32[3,2,1024]{2,1,0:T(2,128)S(1)}, u32[]{:S(2)}, u32[]{:S(2)}) collective-permute-start(f32[3,2,1024]{2,1,0:T(2,128)S(1)} %tail.1.refs_1_), channel_id=1, source_target_pairs={{0,8},{1,9},{2,10},{3,11},{4,12},{5,13},{6,14},{7,15},{8,16},{9,17... | collective-permute-start | bytes 73736 | tf_op jit(solution)/shard_map/ppermute | solution.py:378
  11.2 0.8 copy-start
  13.4 0.6 copy-start.1
  14.0 18.2 %all-to-all-start = ((bf16[4,3,128,128]{3,2,1,0:T(8,128)(2,1)}), bf16[4,3,128,128]{3,2,1,0:T(8,128)(2,1)S(1)}, u32[]{:S(2)}, u32[]{:S(2)}) async-start(bf16[4,3,128,128]{3,2,1,0:T(8,128)(2,1)} %gate.1), calls=%async_computation | async-start | bytes 786432 | tf_op jit(solution)/shard_map/all_to_all | solution.py:379
  20.2 11.9 %collective-permute-start.1 = (bf16[512,256]{1,0:T(8,128)(2,1)S(1)}, bf16[512,256]{1,0:T(8,128)(2,1)S(1)}, u32[]{:S(2)}, u32[]{:S(2)}) collective-permute-start(bf16[512,256]{1,0:T(8,128)(2,1)S(1)} %copy-done.4), channel_id=1, source_target_pairs={{0,0},{1,32},{2,64},{3,96},{4,128},{5,160},{6,192},{7,224},{8,8},{... | collective-permute-start | bytes 786440 | tf_op jit(solution)/shard_map/ppermute | solution.py:404
  25.1 0.7 copy-start.2
  33.4 25.6 %all-to-all-start.1 = ((bf16[4,10,128,128]{3,2,1,0:T(8,128)(2,1)}), bf16[4,10,128,128]{3,2,1,0:T(8,128)(2,1)S(1)}, u32[]{:S(2)}, u32[]{:S(2)}) async-start(bf16[4,10,128,128]{3,2,1,0:T(8,128)(2,1)} %spread.1.refs_2_), calls=%async_computation.1 | async-start | bytes 2621440 | tf_op jit(solution)/shard_map/all_to_all | solution.py:413
  38.7 65.6 %all-gather.3.cloned.1.call-start = ((), (), s32[]{:S(2)}) async-start(), calls=%async_computation.4 | async-start | bytes 4718592 | tf_op jit(solution)/shard_map/all_gather | solution.py:428
  38.8 16.9 %collective-permute-start.6 = (bf16[2,128,256]{2,1,0:T(8,128)(2,1)S(1)}, bf16[2,128,256]{2,1,0:T(8,128)(2,1)S(1)}, u32[]{:S(2)}, u32[]{:S(2)}) collective-permute-start(bf16[2,128,256]{2,1,0:T(8,128)(2,1)S(1)} %get-tuple-element.21), channel_id=1, source_target_pairs={{0,16},{1,17},{2,18},{3,19},{4,20},{5,21},{6,22},{7,23},{8,24},{9,... | collective-permute-start | bytes 393224 | tf_op jit(solution)/shard_map/ppermute | solution.py:422
  49.0 8.1 %collective-permute-start.7 = (bf16[2,128,256]{2,1,0:T(8,128)(2,1)S(1)}, bf16[2,128,256]{2,1,0:T(8,128)(2,1)S(1)}, u32[]{:S(2)}, u32[]{:S(2)}) collective-permute-start(bf16[2,128,256]{2,1,0:T(8,128)(2,1)S(1)} %get-tuple-element.20.refs_1_), channel_id=1, source_target_pairs={{0,32},{1,33},{2,34},{3,35},{4,36},{5,37},{6,38},{7,39},{8,40},{9,... | collective-permute-start | bytes 393224 | tf_op jit(solution)/shard_map/ppermute | solution.py:422
  49.0 10.1 %collective-permute-start.8 = (bf16[2,128,256]{2,1,0:T(8,128)(2,1)S(1)}, bf16[2,128,256]{2,1,0:T(8,128)(2,1)S(1)}, u32[]{:S(2)}, u32[]{:S(2)}) collective-permute-start(bf16[2,128,256]{2,1,0:T(8,128)(2,1)S(1)} %get-tuple-element.21), channel_id=1, source_target_pairs={{0,48},{1,49},{2,50},{3,51},{4,52},{5,53},{6,54},{7,55},{8,56},{9,... | collective-permute-start | bytes 393224 | tf_op jit(solution)/shard_map/ppermute | solution.py:422
  59.9 3.3 %collective-permute-start.2 = (bf16[4,10,128,128]{3,2,1,0:T(8,128)(2,1)S(1)}, bf16[4,10,128,128]{3,2,1,0:T(8,128)(2,1)S(1)}, u32[]{:S(2)}, u32[]{:S(2)}) collective-permute-start(bf16[4,10,128,128]{3,2,1,0:T(8,128)(2,1)S(1)} %all-to-all-done.1.refs_2_.refs_5_), channel_id=1, source_target_pairs={{0,8},{8,0},{1,9},{9,1},{2,10},{10,2},{3,11},{11,3},{4,12},{12,4},... | collective-permute-start | bytes 3932168 | tf_op jit(solution)/shard_map/ppermute | solution.py:414
  67.3 22.3 %all-to-all-start.2 = ((bf16[4,256,128]{2,1,0:T(8,128)(2,1)}), bf16[4,256,128]{2,1,0:T(8,128)(2,1)S(1)}, u32[]{:S(2)}, u32[]{:S(2)}) async-start(bf16[4,256,128]{2,1,0:T(8,128)(2,1)} %bitcast.3), calls=%async_computation.2 | async-start | bytes 524288 | tf_op jit(solution)/shard_map/all_to_all | solution.py:444
  89.6 11.5 %collective-permute-start.3 = (bf16[4,256,128]{2,1,0:T(8,128)(2,1)S(1)}, bf16[4,256,128]{2,1,0:T(8,128)(2,1)S(1)}, u32[]{:S(2)}, u32[]{:S(2)}) collective-permute-start(bf16[4,256,128]{2,1,0:T(8,128)(2,1)S(1)} %all-to-all-done.2.refs_4_.refs_1_), channel_id=1, source_target_pairs={{0,2},{2,4},{4,6},{6,0},{1,3},{3,5},{5,7},{7,1},{8,10},{10,12},{12... | collective-permute-start | bytes 786440 | tf_op jit(solution)/shard_map/ppermute | solution.py:446
  89.6 13.0 %collective-permute-start.4 = (bf16[4,256,128]{2,1,0:T(8,128)(2,1)S(1)}, bf16[4,256,128]{2,1,0:T(8,128)(2,1)S(1)}, u32[]{:S(2)}, u32[]{:S(2)}) collective-permute-start(bf16[4,256,128]{2,1,0:T(8,128)(2,1)S(1)} %all-to-all-done.2.refs_4_.refs_1_), channel_id=1, source_target_pairs={{0,6},{2,0},{4,2},{6,4},{1,7},{3,1},{5,3},{7,5},{8,14},{10,8},{12,... | collective-permute-start | bytes 786440 | tf_op jit(solution)/shard_map/ppermute | solution.py:446
  92.9 11.5 %collective-permute-start.5 = (bf16[4,256,128]{2,1,0:T(8,128)(2,1)S(1)}, bf16[4,256,128]{2,1,0:T(8,128)(2,1)}, u32[]{:S(2)}, u32[]{:S(2)}) collective-permute-start(bf16[4,256,128]{2,1,0:T(8,128)(2,1)S(1)} %all-to-all-done.2.refs_4_.refs_1_), channel_id=1, source_target_pairs={{0,4},{2,6},{4,0},{6,2},{1,5},{3,7},{5,1},{7,3},{8,12},{10,14},{12... | collective-permute-start | bytes 786440 | tf_op jit(solution)/shard_map/ppermute | solution.py:446
  93.9 6.4 %copy-start.3 = (f32[16,1024]{1,0:T(8,128)S(1)}, f32[16,1024]{1,0:T(8,128)}, u32[]{:S(2)}) copy-start(f32[16,1024]{1,0:T(8,128)} %param.9) | copy-start | bytes 196612
  96.2 12.0 %all-to-all-start.3 = ((f32[4,16,1024]{2,1,0:T(8,128)}), f32[4,16,1024]{2,1,0:T(8,128)S(1)}, u32[]{:S(2)}, u32[]{:S(2)}) async-start(f32[4,16,1024]{2,1,0:T(8,128)} %combine.1), calls=%async_computation.3 | async-start | bytes 524288 | tf_op jit(solution)/shard_map/all_to_all | solution.py:458
  108.1 6.5 %collective-permute-start.9 = (bf16[128,1024]{1,0:T(8,128)(2,1)S(1)}, bf16[128,1024]{1,0:T(8,128)(2,1)S(1)}, u32[]{:S(2)}, u32[]{:S(2)}) collective-permute-start(bf16[128,1024]{1,0:T(8,128)(2,1)S(1)} %get-tuple-element.23), channel_id=1, source_target_pairs={{0,16},{16,0},{1,17},{17,1},{2,18},{18,2},{3,19},{19,3},{4,20},{20... | collective-permute-start | bytes 786440 | tf_op jit(solution)/shard_map/ppermute | solution.py:473
Sparse Core Ops, SparseCore 0:
  60.0 38.4 all-gather.2

commit v4 on v3

--- a/solution.py
+++ b/solution.py
@@ -132,7 +132,7 @@
 
 
 def ends_kernel(
-    feats, halo_ref, taps_hbm, decay_hbm, out_ref, prod_hbm, gate_hbm, rate_hbm,
+    feats, halo_ref, taps_hbm, decay_hbm, out_ref, prod_hbm, gate_hbm,
     x, taps, rate, prod, gate_rows, ext, sems, out_sems,
 ):
     finished(started(sems, ((feats, x), (taps_hbm, taps), (decay_hbm, rate))))
@@ -142,7 +142,7 @@
         gate_rows[lo : lo + 16] = featured_rows(ext, taps, 0, 0, lo, 16)
         first = featured_rows(ext, taps, 1, 1, lo, 16)
         prod[lo : lo + 16] = first * featured_rows(ext, taps, 2, 2, lo, 16)
-    written = started(out_sems, ((prod, prod_hbm), (gate_rows, gate_hbm), (rate, rate_hbm)))
+    written = started(out_sems, ((prod, prod_hbm), (gate_rows, gate_hbm)))
     decay = jnp.exp(-rate[...])
 
     def body(i, state):
@@ -194,16 +194,25 @@
         out_ref[target] = total
 
 
+def one_less_exp(y):
+    series = 1.0 - y / 9.0
+    for n in range(8, 1, -1):
+        series = 1.0 - y / n * series
+    return jnp.where(y < 0.5, y * series, 1.0 - jnp.exp(-y))
+
+
 def mix_kernel(
-    rate_hbm, rho_ref, parts_ref, prod_hbm, gate_hbm, out_ref, rate, prod, gate_rows, sems
+    rate_hbm, residue_hbm, parts_ref, prod_hbm, gate_hbm, out_ref,
+    rate, residue, prod, gate_rows, sems,
 ):
-    finished(started(sems, ((rate_hbm, rate), (prod_hbm, prod), (gate_hbm, gate_rows))))
+    pairs = ((rate_hbm, rate), (residue_hbm, residue), (prod_hbm, prod), (gate_hbm, gate_rows))
+    finished(started(sems, pairs))
     rows, width = prod.shape
     decay = jnp.exp(-rate[...])
     start = parts_ref[0]
     for z in range(1, NZ):
         start = start + parts_ref[z]
-    rho = rho_ref[...]
+    rho = residue[...] * jnp.sqrt(one_less_exp(2.0 * rate[...]) / rate.shape[0])
     sub = lax.broadcasted_iota(jnp.int32, (8, width), 0)
 
     def body(i, state):
@@ -223,15 +232,13 @@
     lax.fori_loop(0, rows // 16, body, start)
 
 
-def tail_kernel(feats, halo_ref, tail, sems):
-    rows = feats.shape[1]
-    finished(started(sems, [(feats.at[:, pl.ds(rows - 16, 16), :], tail)]))
+def pack_kernel(qkv, feats, out_ref, halo_ref, tail, sems):
+    rows = qkv.shape[1]
+    lanes = [pl.ds(head * HEAD, HEAD) for head in range(NZ)]
+    pairs = [(qkv.at[:, :, lanes[i]], out_ref.at[i]) for i in range(NZ)]
+    pairs.append((feats.at[:, pl.ds(rows - 16, 16), :], tail))
+    finished(started(sems, pairs))
     halo_ref[...] = tail[:, 14:16].astype(jnp.float32)
-
-
-def pack_kernel(qkv, out_ref, sems):
-    lanes = [pl.ds(head * HEAD, HEAD) for head in range(NZ)]
-    finished(started(sems, [(qkv.at[:, :, lanes[i]], out_ref.at[i]) for i in range(NZ)]))
 
 
 def halves_kernel(place_ref, weight_ref, same_ref, other_ref):
@@ -358,34 +365,24 @@
     bf16, f32 = jnp.bfloat16, jnp.float32
     dma = pltpu.SemaphoreType.DMA
 
-    tail = local_call(
-        tail_kernel,
-        short((3, 2, width), f32),
-        (SLOW,),
-        "tail",
-        10**8,
-        (pltpu.VMEM((3, 16, width), bf16), dma((1,))),
-    )(hyena_feats)
-    packed = local_call(
+    packed, tail = local_call(
         pack_kernel,
-        short((NZ, 3, rows, HEAD), bf16),
-        (SLOW,),
+        (short((NZ, 3, rows, HEAD), bf16), short((3, 2, width), f32)),
+        (SLOW, SLOW),
         "pack",
         10**8,
-        (dma((NZ,)),),
-        after=(tail,),
-    )(attn_qkv)
+        (pltpu.VMEM((3, 16, width), bf16), dma((1 + NZ,))),
+    )(attn_qkv, hyena_feats)
+    qkv = lax.all_to_all(packed, ("z1", "z0"), 0, 0)
     halo = lax.ppermute(tail, ALL, moved(next_ctx))
-    qkv = lax.all_to_all(gate(packed, halo), ("z1", "z0"), 0, 0)
     plane = short((rows, width), f32)
     poles = short(decay_rate.shape, f32)
-    ends, prod, gate_rows, rate = local_call(
+    ends, prod, gate_rows = local_call(
         ends_kernel,
         (
             short((2, rows, HEAD), bf16),
             pltpu.HBM(plane.shape, f32),
             pltpu.HBM(plane.shape, f32),
-            pltpu.HBM(poles.shape, f32),
         ),
         (SLOW, FAST, SLOW, SLOW),
         "ends",
@@ -398,7 +395,7 @@
             pltpu.VMEM(plane.shape, f32),
             pltpu.VMEM((3, rows + 8, width), f32),
             dma((3,)),
-            dma((3,)),
+            dma((2,)),
         ),
     )(hyena_feats, halo, short_taps, decay_rate)
     moved_weight = lax.ppermute(out_weight, ALL, moved(place_weight))
@@ -472,20 +469,20 @@
     )(jnp.stack([y, z0]), *groups, weight)
     received = lax.ppermute(other, "z0", swap)
 
-    rho = residue * jnp.sqrt(-jnp.expm1(-2.0 * rate) / rate.shape[0])
     hyena_mixed = local_call(
         mix_kernel,
         short((rows, width), bf16),
-        (SLOW, FAST, FAST, SLOW, SLOW),
+        (SLOW, SLOW, FAST, SLOW, SLOW),
         "mix",
         4 * 10**9,
         (
             pltpu.VMEM(poles.shape, f32),
+            pltpu.VMEM(poles.shape, f32),
             pltpu.VMEM(plane.shape, f32),
             pltpu.VMEM(plane.shape, f32),
-            dma((3,)),
+            dma((4,)),
         ),
-    )(decay_rate, rho, parts, prod, gate_rows)
+    )(decay_rate, residue, parts, prod, gate_rows)
     return hyena_mixed, (mine + received.astype(f32)).astype(bf16)
 
 

time: 123 us -> 115 us (0.935)
  blocking collectives: 0 us -> 20.7 us
  starting transfers between devices: 50.6 us -> 37.4 us
  waiting for transfers between devices: 29.2 us -> 17.8 us
  local copies, waits for them, and re-layouts: 2.1 us -> 0.01 us
    all_to_all x0 -> x1, blocking collectives: none -> 20.7 us  [per_device(): lax.all_to_all(attended.reshape(NH * NZ1, NZ0 * rows, HEAD), ('h', 'z1'),...]
    all_to_all x2 -> x1, starting transfers between devices: 18.1 us -> 6.01 us  [per_device(): qkv = lax.all_to_all(packed, ('z1', 'z0'), 0, 0)]
    all_to_all x2 -> x1, waiting for transfers between devices: 10.3 us -> 0.01 us  [per_device(): qkv = lax.all_to_all(packed, ('z1', 'z0'), 0, 0)]
    ppermute x1, waiting for transfers between devices: 3.34 us -> 0.01 us  [per_device(): moved_weight = lax.ppermute(out_weight, ALL, moved(place_weight))]
    unnamed x10 -> x2, local copies, waits for them, and re-layouts: 2.1 us -> 0.01 us
    ppermute x1, waiting for transfers between devices: 1.37 us -> 3.22 us  [per_device(): halo = lax.ppermute(tail, ALL, moved(next_ctx))]
    ppermute x3, waiting for transfers between devices: 3.23 us -> 4.46 us  [per_device(): lax.ppermute(group, 'y', [(i, (i + step) % NY) for i in range(NY)])]
    pallas_call x11 -> x10, Pallas kernels: 24.3 us -> 23.7 us  [local_call(): return lambda *operands: call(*map(placed, operands, specs), *after)]
  transfers between devices with their start and end apart: 15 -> 14, of which waited for: 9 -> 6; matrix products, arithmetic and copies ran while one was open for 1% -> 0% of each run, Pallas kernels for 17% -> 17%
where the time goes in v4:
time: 115 us
  starting transfers between devices  37.4 us (33%)
  Pallas kernels  23.7 us (21%)
  blocking collectives  20.7 us (18%)
  waiting for transfers between devices  17.8 us (15%)
  between operations  14.2 us (12%)
    pallas_call x10, Pallas kernels, local_call(): return lambda *operands: call(*map(placed, operands, specs), *after)  23.7 us
    all_to_all x1, blocking collectives, per_device(): lax.all_to_all(attended.reshape(NH * NZ1, NZ0 * rows, HEAD), ('h', 'z1'),...  20.7 us
    ppermute x3, starting transfers between devices, per_device(): lax.ppermute(opposite if steps % 2 else same, ALL, along_z(steps))  11.7 us
    ppermute x3, waiting for transfers between devices, per_device(): lax.ppermute(opposite if steps % 2 else same, ALL, along_z(steps))  7.92 us
    all_to_all x1, starting transfers between devices, per_device(): qkv = lax.all_to_all(packed, ('z1', 'z0'), 0, 0)  6.01 us
    all_to_all x1, starting transfers between devices, per_device(): far_own = lax.all_to_all(spread, 'x', 0, 0)  5.05 us
    ppermute x1, starting transfers between devices, per_device(): moved_weight = lax.ppermute(out_weight, ALL, moved(place_weight))  4.91 us
    ppermute x3, waiting for transfers between devices, per_device(): lax.ppermute(group, 'y', [(i, (i + step) % NY) for i in range(NY)])  4.46 us
  transfers between devices with their start and end apart: 14, of which 6 were waited for; matrix products, arithmetic and copies ran while one was open for 0% of the time, Pallas kernels for 17%

profile of v4, /device:TPU:38, one launch (start us, length us, event | category | flops | bytes accessed | tf_op | source)
XLA Modules:
  0.0 114.8 jit_solution(10948736901973025486)
XLA Ops:
  7.2 0.0 copy-start
  7.2 1.9 %pack.1 = (bf16[4,3,128,128]{3,2,1,0:T(8,128)(2,1)}, f32[3,2,1024]{2,1,0:T(2,128)S(1)}) custom-call(bf16[3,128,512]{2,1,0:T(8,128)(2,1)} %refs_0_.3, bf16[3,128,1024]{2,1,0:T(8,128)(2,1)} %refs_0_.4), custom_call_target="tpu_custom_call" | custom-call | flops 100000000 | bytes 2000000 | tf_op jit(solution)/shard_map/pack/pallas_call | solution.py:93
  9.1 6.0 %all-to-all-start = ((bf16[4,3,128,128]{3,2,1,0:T(8,128)(2,1)}), bf16[4,3,128,128]{3,2,1,0:T(8,128)(2,1)S(1)}, u32[]{:S(2)}, u32[]{:S(2)}) async-start(bf16[4,3,128,128]{3,2,1,0:T(8,128)(2,1)} %get-tuple-element.14), calls=%async_computation | async-start | bytes 786432 | tf_op jit(solution)/shard_map/all_to_all | solution.py:376
  15.1 0.0 copy-done
  15.1 4.9 %collective-permute-start.1 = (bf16[512,256]{1,0:T(8,128)(2,1)S(1)}, bf16[512,256]{1,0:T(8,128)(2,1)S(1)}, u32[]{:S(2)}, u32[]{:S(2)}) collective-permute-start(bf16[512,256]{1,0:T(8,128)(2,1)S(1)} %copy-done), channel_id=1, source_target_pairs={{0,0},{1,32},{2,64},{3,96},{4,128},{5,160},{6,192},{7,224},{8,8},{... | collective-permute-start | bytes 786440 | tf_op jit(solution)/shard_map/ppermute | solution.py:401
  20.0 1.9 %collective-permute-start = (f32[3,2,1024]{2,1,0:T(2,128)S(1)}, f32[3,2,1024]{2,1,0:T(2,128)S(1)}, u32[]{:S(2)}, u32[]{:S(2)}) collective-permute-start(f32[3,2,1024]{2,1,0:T(2,128)S(1)} %get-tuple-element.15), channel_id=1, source_target_pairs={{0,8},{1,9},{2,10},{3,11},{4,12},{5,13},{6,14},{7,15},{8,16},{9,17... | collective-permute-start | bytes 73736 | tf_op jit(solution)/shard_map/ppermute | solution.py:377
  22.0 3.2 %collective-permute-done.refs_1_ = f32[3,2,1024]{2,1,0:T(2,128)S(1)} collective-permute-done((f32[3,2,1024]{2,1,0:T(2,128)S(1)}, f32[3,2,1024]{2,1,0:T(2,128)S(1)}, u32[]{:S(2)}, u32[]{:S(2)}) %collective-permute-start) | collective-permute-done | bytes 24608 | tf_op jit(solution)/shard_map/ppermute | solution.py:377
  25.2 2.9 %ends.1 = (bf16[2,128,128]{2,1,0:T(8,128)(2,1)S(1)}, f32[128,1024]{1,0:T(8,128)}, f32[128,1024]{1,0:T(8,128)}) custom-call(bf16[3,128,1024]{2,1,0:T(8,128)(2,1)} %refs_0_.4, f32[3,2,1024]{2,1,0:T(2,128)S(1)} %collective-permute-done.refs_1_, f32[3,3,1024]{2,1,0:T(4,128)} %refs_2_.1, f32[16,1024]{1,0:T(8,128)} %refs_0_.5), custom_call_target="tpu_custom_call" | custom-call | flops 1000000000 | bytes 2000000 | tf_op jit(solution)/shard_map/ends/pallas_call | solution.py:93
  28.1 0.0 collective-permute-done.1.refs_2_.refs_1_
  28.1 0.0 all-to-all-done.refs_0_.refs_1_
  28.1 1.2 %spread.1.refs_2_ = bf16[4,10,128,128]{3,2,1,0:T(8,128)(2,1)} custom-call(bf16[4,3,128,128]{3,2,1,0:T(8,128)(2,1)S(1)} %all-to-all-done.refs_0_.refs_1_, bf16[2,128,128]{2,1,0:T(8,128)(2,1)S(1)} %get-tuple-element.16.refs_1_, bf16[512,256]{1,0:T(8,128)(2,1)S(1)} %collective-permute-done.1.refs_2_.refs_1_), custom_call_target="tpu_custom_call" | custom-call | flops 100000000 | bytes 2000000 | tf_op jit(solution)/shard_map/spread/pallas_call | solution.py:93
  29.4 5.0 %all-to-all-start.1 = ((bf16[4,10,128,128]{3,2,1,0:T(8,128)(2,1)}), bf16[4,10,128,128]{3,2,1,0:T(8,128)(2,1)S(1)}, u32[]{:S(2)}, u32[]{:S(2)}) async-start(bf16[4,10,128,128]{3,2,1,0:T(8,128)(2,1)} %spread.1.refs_2_), calls=%async_computation.1 | async-start | bytes 2621440 | tf_op jit(solution)/shard_map/all_to_all | solution.py:410
  34.4 0.0 all-gather.3.cloned.1.call-start
  34.4 10.2 %collective-permute-start.6 = (bf16[2,128,256]{2,1,0:T(8,128)(2,1)S(1)}, bf16[2,128,256]{2,1,0:T(8,128)(2,1)S(1)}, u32[]{:S(2)}, u32[]{:S(2)}) collective-permute-start(bf16[2,128,256]{2,1,0:T(8,128)(2,1)S(1)} %get-tuple-element.23), channel_id=1, source_target_pairs={{0,16},{1,17},{2,18},{3,19},{4,20},{5,21},{6,22},{7,23},{8,24},{9,... | collective-permute-start | bytes 393224 | tf_op jit(solution)/shard_map/ppermute | solution.py:419
  44.6 0.0 collective-permute-start.7
  44.6 1.6 %collective-permute-start.8 = (bf16[2,128,256]{2,1,0:T(8,128)(2,1)S(1)}, bf16[2,128,256]{2,1,0:T(8,128)(2,1)S(1)}, u32[]{:S(2)}, u32[]{:S(2)}) collective-permute-start(bf16[2,128,256]{2,1,0:T(8,128)(2,1)S(1)} %get-tuple-element.23), channel_id=1, source_target_pairs={{0,48},{1,49},{2,50},{3,51},{4,52},{5,53},{6,54},{7,55},{8,56},{9,... | collective-permute-start | bytes 393224 | tf_op jit(solution)/shard_map/ppermute | solution.py:419
  46.2 6.5 %collective-permute-done.6.refs_2_ = bf16[2,128,256]{2,1,0:T(8,128)(2,1)S(1)} collective-permute-done((bf16[2,128,256]{2,1,0:T(8,128)(2,1)S(1)}, bf16[2,128,256]{2,1,0:T(8,128)(2,1)S(1)}, u32[]{:S(2)}, u32[]{:S(2)}) %collective-permute-start.6) | collective-permute-done | bytes 131104 | tf_op jit(solution)/shard_map/ppermute | solution.py:419
  52.7 1.4 %collective-permute-done.7.refs_3_ = bf16[2,128,256]{2,1,0:T(8,128)(2,1)S(1)} collective-permute-done((bf16[2,128,256]{2,1,0:T(8,128)(2,1)S(1)}, bf16[2,128,256]{2,1,0:T(8,128)(2,1)S(1)}, u32[]{:S(2)}, u32[]{:S(2)}) %collective-permute-start.7) | collective-permute-done | bytes 131104 | tf_op jit(solution)/shard_map/ppermute | solution.py:419
  54.1 0.0 collective-permute-done.8.refs_4_
  54.1 0.0 all-to-all-done.1.refs_2_.refs_5_
  54.1 0.8 stack.35
  54.9 0.0 all-gather.3.cloned.1.call-update
  55.0 0.1 collective-permute-start.2
  55.1 0.1 pad_add_fusion.1.refs_0_
  55.1 3.1 %own.1 = (f32[1,512]{1,0:T(1,128)S(1)}, f32[1,512]{1,0:T(1,128)S(1)}, f32[128,512]{1,0:T(8,128)S(1)}) custom-call(s32[2]{0:T(128)S(1)} %pad_add_fusion.1.refs_0_, bf16[4,3,128,128]{3,2,1,0:T(8,128)(2,1)S(1)} %all-to-all-done.refs_0_.refs_1_, bf16[4,10,128,128]{3,2,1,0:T(8,128)(2,1)S(1)} %all-to-all-done.1.refs_2_.refs_5_), custom_call_target="tpu_custom_call" | custom-call | flops 2000000000 | bytes 2000000 | tf_op jit(solution)/shard_map/own/pallas_call | solution.py:93
  58.3 0.0 collective-permute-done.2.refs_5_.refs_3_
  58.3 3.4 %other.1 = bf16[2,2,256,128]{3,2,1,0:T(8,128)(2,1)S(1)} custom-call(s32[2]{0:T(128)S(1)} %pad_add_fusion.1.refs_0_, bf16[4,3,128,128]{3,2,1,0:T(8,128)(2,1)S(1)} %all-to-all-done.refs_0_.refs_1_, f32[1,512]{1,0:T(1,128)S(1)} %get-tuple-element.17.refs_2_, f32[1,512]{1,0:T(1,128)S(1)} %get-tuple-element.18.refs_3_, f32[128,512]{1,0:T(8,128)S(1)} %get-tuple-element.19.refs_4_, ...), custom_call_target="tpu_custom_call" | custom-call | flops 2000000000 | bytes 2000000 | tf_op jit(solution)/shard_map/other/pallas_call | solution.py:93
  61.7 20.7 %all_to_all.20.refs_4_.refs_1_ = bf16[4,256,128]{2,1,0:T(8,128)(2,1)S(1)} all-to-all(bf16[4,256,128]{2,1,0:T(8,128)(2,1)S(1)} %bitcast.7), channel_id=1, replica_groups=mesh['x'=4,'z1'=2,'z0'=2,'k'=2,'y'=4,'h'=2] {'h','z1'}, dimensions={0} | all-to-all | bytes 524288 | tf_op jit(solution)/shard_map/all_to_all | solution.py:441
  82.4 0.2 collective-permute-start.3
  82.6 3.0 %collective-permute-start.4 = (bf16[4,256,128]{2,1,0:T(8,128)(2,1)S(1)}, bf16[4,256,128]{2,1,0:T(8,128)(2,1)S(1)}, u32[]{:S(2)}, u32[]{:S(2)}) collective-permute-start(bf16[4,256,128]{2,1,0:T(8,128)(2,1)S(1)} %all_to_all.20.refs_4_.refs_1_), channel_id=1, source_target_pairs={{0,6},{2,0},{4,2},{6,4},{1,7},{3,1},{5,3},{7,5},{8,14},{10,8},{12,... | collective-permute-start | bytes 786440 | tf_op jit(solution)/shard_map/ppermute | solution.py:443
  85.6 0.7 collective-permute-start.5
  86.4 0.1 pad_add_fusion.refs_0_
  86.5 2.3 %combine.1 = f32[4,16,1024]{2,1,0:T(8,128)} custom-call(s32[3]{0:T(128)S(1)} %pad_add_fusion.refs_0_, f32[16,1024]{1,0:T(8,128)} %refs_0_.5, bf16[4,10,128,128]{3,2,1,0:T(8,128)(2,1)S(1)} %all-to-all-done.1.refs_2_.refs_5_, bf16[4,10,128,128]{3,2,1,0:T(8,128)(2,1)S(1)} %collective-permute-done.2.refs_5_.refs_3_, ...), custom_call_target="tpu_custom_call" | custom-call | flops 100000000 | bytes 2000000 | tf_op jit(solution)/shard_map/combine/pallas_call | solution.py:93
  88.8 3.7 %all-to-all-start.3 = ((f32[4,16,1024]{2,1,0:T(8,128)}), f32[4,16,1024]{2,1,0:T(8,128)S(1)}, u32[]{:S(2)}, u32[]{:S(2)}) async-start(f32[4,16,1024]{2,1,0:T(8,128)} %combine.1), calls=%async_computation.3 | async-start | bytes 524288 | tf_op jit(solution)/shard_map/all_to_all | solution.py:455
  92.5 0.1 pad_add_fusion.2.refs_0_
  92.5 0.0 collective-permute-done.3.refs_2_
  92.5 2.9 %collective-permute-done.4.refs_3_ = bf16[4,256,128]{2,1,0:T(8,128)(2,1)S(1)} collective-permute-done((bf16[4,256,128]{2,1,0:T(8,128)(2,1)S(1)}, bf16[4,256,128]{2,1,0:T(8,128)(2,1)S(1)}, u32[]{:S(2)}, u32[]{:S(2)}) %collective-permute-start.4) | collective-permute-done | bytes 262176 | tf_op jit(solution)/shard_map/ppermute | solution.py:443
  95.4 1.6 %collective-permute-done.5.refs_4_ = bf16[4,256,128]{2,1,0:T(8,128)(2,1)} collective-permute-done((bf16[4,256,128]{2,1,0:T(8,128)(2,1)S(1)}, bf16[4,256,128]{2,1,0:T(8,128)(2,1)}, u32[]{:S(2)}, u32[]{:S(2)}) %collective-permute-start.5) | collective-permute-done | bytes 262176 | tf_op jit(solution)/shard_map/ppermute | solution.py:443
  97.0 0.0 all-gather.3.cloned.1.call-done
  97.0 3.8 %project.1 = (f32[128,1024]{1,0:T(8,128)S(1)}, bf16[128,1024]{1,0:T(8,128)(2,1)S(1)}) custom-call(s32[2]{0:T(128)S(1)} %pad_add_fusion.2.refs_0_, bf16[4,256,128]{2,1,0:T(8,128)(2,1)S(1)} %all_to_all.20.refs_4_.refs_1_, bf16[4,256,128]{2,1,0:T(8,128)(2,1)S(1)} %collective-permute-done.3.refs_2_, bf16[4,256,128]{2,1,0:T(8,128)(2,1)S(1)} %collective-permute-done.4.refs_3_, ...), custom_call_target="tpu_custom_call" | custom-call | flops 2000000000 | bytes 2000000 | tf_op jit(solution)/shard_map/project/pallas_call | solution.py:93
  100.8 0.1 collective-permute-start.9
  100.9 0.0 all-to-all-done.3.refs_2_
  100.9 4.1 %mix.1 = bf16[128,1024]{1,0:T(8,128)(2,1)} custom-call(f32[16,1024]{1,0:T(8,128)} %refs_0_.5, f32[16,1024]{1,0:T(8,128)} %refs_1_.5, f32[4,16,1024]{2,1,0:T(8,128)S(1)} %all-to-all-done.3.refs_2_, f32[128,1024]{1,0:T(8,128)} %get-tuple-element.20.refs_3_, f32[128,1024]{1,0:T(8,128)} %get-tuple-element.21.refs_4_), custom_call_target="tpu_custom_call" | custom-call | flops 4000000000 | bytes 2000000 | tf_op jit(solution)/shard_map/mix/pallas_call | solution.py:93
  105.0 2.2 %collective-permute-done.9 = bf16[128,1024]{1,0:T(8,128)(2,1)S(1)} collective-permute-done((bf16[128,1024]{1,0:T(8,128)(2,1)S(1)}, bf16[128,1024]{1,0:T(8,128)(2,1)S(1)}, u32[]{:S(2)}, u32[]{:S(2)}) %collective-permute-start.9) | collective-permute-done | bytes 262176 | tf_op jit(solution)/shard_map/ppermute | solution.py:470
  107.2 0.8 add_convert_fusion
  (1 shorter events, 0.0 us)
Async XLA Ops:
  7.2 8.0 %copy-start = (bf16[512,256]{1,0:T(8,128)(2,1)S(1)}, bf16[512,256]{1,0:T(8,128)(2,1)}, u32[]{:S(2)}) copy-start(bf16[512,256]{1,0:T(8,128)(2,1)} %param.11) | copy-start | bytes 786436
  9.1 19.0 %all-to-all-start = ((bf16[4,3,128,128]{3,2,1,0:T(8,128)(2,1)}), bf16[4,3,128,128]{3,2,1,0:T(8,128)(2,1)S(1)}, u32[]{:S(2)}, u32[]{:S(2)}) async-start(bf16[4,3,128,128]{3,2,1,0:T(8,128)(2,1)} %get-tuple-element.14), calls=%async_computation | async-start | bytes 786432 | tf_op jit(solution)/shard_map/all_to_all | solution.py:376
  15.1 13.0 %collective-permute-start.1 = (bf16[512,256]{1,0:T(8,128)(2,1)S(1)}, bf16[512,256]{1,0:T(8,128)(2,1)S(1)}, u32[]{:S(2)}, u32[]{:S(2)}) collective-permute-start(bf16[512,256]{1,0:T(8,128)(2,1)S(1)} %copy-done), channel_id=1, source_target_pairs={{0,0},{1,32},{2,64},{3,96},{4,128},{5,160},{6,192},{7,224},{8,8},{... | collective-permute-start | bytes 786440 | tf_op jit(solution)/shard_map/ppermute | solution.py:401
  20.0 5.1 %collective-permute-start = (f32[3,2,1024]{2,1,0:T(2,128)S(1)}, f32[3,2,1024]{2,1,0:T(2,128)S(1)}, u32[]{:S(2)}, u32[]{:S(2)}) collective-permute-start(f32[3,2,1024]{2,1,0:T(2,128)S(1)} %get-tuple-element.15), channel_id=1, source_target_pairs={{0,8},{1,9},{2,10},{3,11},{4,12},{5,13},{6,14},{7,15},{8,16},{9,17... | collective-permute-start | bytes 73736 | tf_op jit(solution)/shard_map/ppermute | solution.py:377
  29.4 24.7 %all-to-all-start.1 = ((bf16[4,10,128,128]{3,2,1,0:T(8,128)(2,1)}), bf16[4,10,128,128]{3,2,1,0:T(8,128)(2,1)S(1)}, u32[]{:S(2)}, u32[]{:S(2)}) async-start(bf16[4,10,128,128]{3,2,1,0:T(8,128)(2,1)} %spread.1.refs_2_), calls=%async_computation.1 | async-start | bytes 2621440 | tf_op jit(solution)/shard_map/all_to_all | solution.py:410
  34.4 62.6 %all-gather.3.cloned.1.call-start = ((), (), s32[]{:S(2)}) async-start(), calls=%async_computation.4 | async-start | bytes 4718592 | tf_op jit(solution)/shard_map/all_gather | solution.py:425
  34.4 18.3 %collective-permute-start.6 = (bf16[2,128,256]{2,1,0:T(8,128)(2,1)S(1)}, bf16[2,128,256]{2,1,0:T(8,128)(2,1)S(1)}, u32[]{:S(2)}, u32[]{:S(2)}) collective-permute-start(bf16[2,128,256]{2,1,0:T(8,128)(2,1)S(1)} %get-tuple-element.23), channel_id=1, source_target_pairs={{0,16},{1,17},{2,18},{3,19},{4,20},{5,21},{6,22},{7,23},{8,24},{9,... | collective-permute-start | bytes 393224 | tf_op jit(solution)/shard_map/ppermute | solution.py:419
  44.6 9.5 %collective-permute-start.7 = (bf16[2,128,256]{2,1,0:T(8,128)(2,1)S(1)}, bf16[2,128,256]{2,1,0:T(8,128)(2,1)S(1)}, u32[]{:S(2)}, u32[]{:S(2)}) collective-permute-start(bf16[2,128,256]{2,1,0:T(8,128)(2,1)S(1)} %get-tuple-element.22.refs_1_), channel_id=1, source_target_pairs={{0,32},{1,33},{2,34},{3,35},{4,36},{5,37},{6,38},{7,39},{8,40},{9,... | collective-permute-start | bytes 393224 | tf_op jit(solution)/shard_map/ppermute | solution.py:419
  44.6 9.5 %collective-permute-start.8 = (bf16[2,128,256]{2,1,0:T(8,128)(2,1)S(1)}, bf16[2,128,256]{2,1,0:T(8,128)(2,1)S(1)}, u32[]{:S(2)}, u32[]{:S(2)}) collective-permute-start(bf16[2,128,256]{2,1,0:T(8,128)(2,1)S(1)} %get-tuple-element.23), channel_id=1, source_target_pairs={{0,48},{1,49},{2,50},{3,51},{4,52},{5,53},{6,54},{7,55},{8,56},{9,... | collective-permute-start | bytes 393224 | tf_op jit(solution)/shard_map/ppermute | solution.py:419
  55.0 3.3 %collective-permute-start.2 = (bf16[4,10,128,128]{3,2,1,0:T(8,128)(2,1)S(1)}, bf16[4,10,128,128]{3,2,1,0:T(8,128)(2,1)S(1)}, u32[]{:S(2)}, u32[]{:S(2)}) collective-permute-start(bf16[4,10,128,128]{3,2,1,0:T(8,128)(2,1)S(1)} %all-to-all-done.1.refs_2_.refs_5_), channel_id=1, source_target_pairs={{0,8},{8,0},{1,9},{9,1},{2,10},{10,2},{3,11},{11,3},{4,12},{12,4},... | collective-permute-start | bytes 3932168 | tf_op jit(solution)/shard_map/ppermute | solution.py:411
  82.4 10.1 %collective-permute-start.3 = (bf16[4,256,128]{2,1,0:T(8,128)(2,1)S(1)}, bf16[4,256,128]{2,1,0:T(8,128)(2,1)S(1)}, u32[]{:S(2)}, u32[]{:S(2)}) collective-permute-start(bf16[4,256,128]{2,1,0:T(8,128)(2,1)S(1)} %all_to_all.20.refs_4_.refs_1_), channel_id=1, source_target_pairs={{0,2},{2,4},{4,6},{6,0},{1,3},{3,5},{5,7},{7,1},{8,10},{10,12},{12... | collective-permute-start | bytes 786440 | tf_op jit(solution)/shard_map/ppermute | solution.py:443
  82.6 12.8 %collective-permute-start.4 = (bf16[4,256,128]{2,1,0:T(8,128)(2,1)S(1)}, bf16[4,256,128]{2,1,0:T(8,128)(2,1)S(1)}, u32[]{:S(2)}, u32[]{:S(2)}) collective-permute-start(bf16[4,256,128]{2,1,0:T(8,128)(2,1)S(1)} %all_to_all.20.refs_4_.refs_1_), channel_id=1, source_target_pairs={{0,6},{2,0},{4,2},{6,4},{1,7},{3,1},{5,3},{7,5},{8,14},{10,8},{12,... | collective-permute-start | bytes 786440 | tf_op jit(solution)/shard_map/ppermute | solution.py:443
  85.6 11.4 %collective-permute-start.5 = (bf16[4,256,128]{2,1,0:T(8,128)(2,1)S(1)}, bf16[4,256,128]{2,1,0:T(8,128)(2,1)}, u32[]{:S(2)}, u32[]{:S(2)}) collective-permute-start(bf16[4,256,128]{2,1,0:T(8,128)(2,1)S(1)} %all_to_all.20.refs_4_.refs_1_), channel_id=1, source_target_pairs={{0,4},{2,6},{4,0},{6,2},{1,5},{3,7},{5,1},{7,3},{8,12},{10,14},{12... | collective-permute-start | bytes 786440 | tf_op jit(solution)/shard_map/ppermute | solution.py:443
  88.8 12.1 %all-to-all-start.3 = ((f32[4,16,1024]{2,1,0:T(8,128)}), f32[4,16,1024]{2,1,0:T(8,128)S(1)}, u32[]{:S(2)}, u32[]{:S(2)}) async-start(f32[4,16,1024]{2,1,0:T(8,128)} %combine.1), calls=%async_computation.3 | async-start | bytes 524288 | tf_op jit(solution)/shard_map/all_to_all | solution.py:455
  100.8 6.5 %collective-permute-start.9 = (bf16[128,1024]{1,0:T(8,128)(2,1)S(1)}, bf16[128,1024]{1,0:T(8,128)(2,1)S(1)}, u32[]{:S(2)}, u32[]{:S(2)}) collective-permute-start(bf16[128,1024]{1,0:T(8,128)(2,1)S(1)} %get-tuple-element.25), channel_id=1, source_target_pairs={{0,16},{16,0},{1,17},{17,1},{2,18},{18,2},{3,19},{19,3},{4,20},{20... | collective-permute-start | bytes 786440 | tf_op jit(solution)/shard_map/ppermute | solution.py:470
Sparse Core Ops, SparseCore 0:
  55.1 36.4 all-gather.2

commit v5 on v4

--- a/solution.py
+++ b/solution.py
@@ -238,7 +238,7 @@
     pairs = [(qkv.at[:, :, lanes[i]], out_ref.at[i]) for i in range(NZ)]
     pairs.append((feats.at[:, pl.ds(rows - 16, 16), :], tail))
     finished(started(sems, pairs))
-    halo_ref[...] = tail[:, 14:16].astype(jnp.float32)
+    halo_ref[...] = tail[...].astype(jnp.float32)[:, 14:16]
 
 
 def halves_kernel(place_ref, weight_ref, same_ref, other_ref):
@@ -252,17 +252,20 @@
                     ref[part] = weight_ref[lo : lo + HEAD]
 
 
-def stack_kernel(place_ref, *refs):
-    for steps, ref in enumerate(refs[:-1]):
-        refs[-1][(place_ref[0] + NZ - steps) % NZ] = ref[...]
-
-
-def spread_kernel(qkv_ref, ends_ref, out_ref):
-    for z in range(NZ):
-        for i in range(out_ref.shape[0]):
-            out_ref[i, 2 * z : 2 * z + 2] = qkv_ref[z, 1:]
-    for i in range(out_ref.shape[0]):
-        out_ref[i, 2 * NZ :] = ends_ref[...]
+def stack_kernel(place_ref, r0, r1, r2, r3, out, sems):
+    pairs = [
+        (ref, out.at[(place_ref[0] + NZ - steps) % NZ]) for steps, ref in enumerate((r0, r1, r2, r3))
+    ]
+    finished(started(sems, pairs))
+
+
+def spread_kernel(qkv_ref, ends_ref, out, sems):
+    pairs = []
+    for i in range(NX):
+        pairs += [
+            (qkv_ref.at[z, pl.ds(1, 2)], out.at[i, pl.ds(2 * z, 2)]) for z in range(NZ)
+        ] + [(ends_ref, out.at[i, pl.ds(2 * NZ, 2)])]
+    finished(started(sems, pairs))
 
 
 def folded(q, pairs, top, total, acc, visible=None):
@@ -330,13 +333,17 @@
     copies = started(sems, [(w_hbm.at[i], parts.at[i]) for i in range(NX)])
     for step, group in zip((0, 1, 3, 2), (g0, g1, g2, g3)):
         held[step] = group[...]
-    for i in range(NX):
-        step = (2 * y - i + NX) % NX
-        heads = jnp.concatenate([held[step, j] for j in range(NH * NZ1)], axis=1)
-        copies[i].wait()
+    for i in range(0, NX, 2):
+        steps = [(2 * y - i - n + NX) % NX for n in range(2)]
+        heads = jnp.concatenate([held[n, j] for n in steps for j in range(NH * NZ1)], axis=1)
+        finished(copies[i : i + 2])
         for k in range(NK):
             for b in range(2):
-                columns = [parts[i, k, 2 * h + b].reshape(2 * HEAD, 256) for h in range(NH)]
+                columns = [
+                    parts[i + n, k, 2 * h + b].reshape(2 * HEAD, 256)
+                    for n in range(2)
+                    for h in range(NH)
+                ]
                 term = jnp.dot(
                     heads, jnp.concatenate(columns, axis=0), preferred_element_type=jnp.float32
                 )
@@ -401,10 +408,11 @@
     moved_weight = lax.ppermute(out_weight, ALL, moved(place_weight))
     spread = local_call(
         spread_kernel,
-        short((NX, 2 * NZ + 2, rows, HEAD), bf16),
+        pltpu.HBM((NX, 2 * NZ + 2, rows, HEAD), bf16),
         (FAST, FAST),
         "spread",
         10**8,
+        (dma((NX * (NZ + 1),)),),
         after=(moved_weight,),
     )(qkv, ends)
     far_own = lax.all_to_all(spread, "x", 0, 0)
@@ -419,7 +427,8 @@
         lax.ppermute(opposite if steps % 2 else same, ALL, along_z(steps)) for steps in (1, 2, 3)
     ]
     placed = local_call(
-        stack_kernel, short((NZ, *half.shape), bf16), (SMEM,) + (FAST,) * NZ, "stack", 10**8,
+        stack_kernel, pltpu.HBM((NZ, *half.shape), bf16), (SMEM,) + (FAST,) * NZ, "stack", 10**8,
+        (dma((NZ,)),),
         after=(far_own,),
     )(z, *arrived)
     weight = lax.all_gather(placed, ("x", "k")).reshape(NX, NK, *placed.shape)

time: 115 us -> 116 us (level)
  no operation moved by 1% of the time
where the time goes in v5:
time: 116 us; the launch traced here: 115 us
  starting transfers between devices  37.6 us (32%)
  Pallas kernels  23.9 us (21%)
  blocking collectives  20.7 us (18%)
  waiting for transfers between devices  17.8 us (15%)
  between operations  14.2 us (12%)
    pallas_call x10, Pallas kernels, local_call(): return lambda *operands: call(*map(placed, operands, specs), *after)  23.9 us
    all_to_all x1, blocking collectives, per_device(): lax.all_to_all(attended.reshape(NH * NZ1, NZ0 * rows, HEAD), ('h', 'z1'),...  20.7 us
    ppermute x3, starting transfers between devices, per_device(): lax.ppermute(opposite if steps % 2 else same, ALL, along_z(steps))  11.7 us
    ppermute x3, waiting for transfers between devices, per_device(): lax.ppermute(opposite if steps % 2 else same, ALL, along_z(steps))  7.92 us
    all_to_all x1, starting transfers between devices, per_device(): qkv = lax.all_to_all(packed, ('z1', 'z0'), 0, 0)  6.01 us
    all_to_all x1, starting transfers between devices, per_device(): far_own = lax.all_to_all(spread, 'x', 0, 0)  5.19 us
    ppermute x1, starting transfers between devices, per_device(): moved_weight = lax.ppermute(out_weight, ALL, moved(place_weight))  4.91 us
    ppermute x3, waiting for transfers between devices, per_device(): lax.ppermute(group, 'y', [(i, (i + step) % NY) for i in range(NY)])  4.47 us
  transfers between devices with their start and end apart: 14, of which 6 were waited for; matrix products, arithmetic and copies ran while one was open for 0% of the time, Pallas kernels for 17%

profile of v5, /device:TPU:38, one launch (start us, length us, event | category | flops | bytes accessed | tf_op | source)
XLA Modules:
  0.0 115.2 jit_solution(6213868631547574773)
XLA Ops:
  7.2 0.0 copy-start.1
  7.2 1.9 %pack.1 = (bf16[4,3,128,128]{3,2,1,0:T(8,128)(2,1)}, f32[3,2,1024]{2,1,0:T(2,128)S(1)}) custom-call(bf16[3,128,512]{2,1,0:T(8,128)(2,1)} %refs_0_.3, bf16[3,128,1024]{2,1,0:T(8,128)(2,1)} %refs_0_.4), custom_call_target="tpu_custom_call" | custom-call | flops 100000000 | bytes 2000000 | tf_op jit(solution)/shard_map/pack/pallas_call | solution.py:93
  9.1 6.0 %all-to-all-start = ((bf16[4,3,128,128]{3,2,1,0:T(8,128)(2,1)}), bf16[4,3,128,128]{3,2,1,0:T(8,128)(2,1)S(1)}, u32[]{:S(2)}, u32[]{:S(2)}) async-start(bf16[4,3,128,128]{3,2,1,0:T(8,128)(2,1)} %get-tuple-element.14), calls=%async_computation | async-start | bytes 786432 | tf_op jit(solution)/shard_map/all_to_all | solution.py:383
  15.1 0.0 copy-done.1
  15.1 4.9 %collective-permute-start.1 = (bf16[512,256]{1,0:T(8,128)(2,1)S(1)}, bf16[512,256]{1,0:T(8,128)(2,1)S(1)}, u32[]{:S(2)}, u32[]{:S(2)}) collective-permute-start(bf16[512,256]{1,0:T(8,128)(2,1)S(1)} %copy-done.1), channel_id=1, source_target_pairs={{0,0},{1,32},{2,64},{3,96},{4,128},{5,160},{6,192},{7,224},{8,8},{... | collective-permute-start | bytes 786440 | tf_op jit(solution)/shard_map/ppermute | solution.py:408
  20.0 1.9 %collective-permute-start = (f32[3,2,1024]{2,1,0:T(2,128)S(1)}, f32[3,2,1024]{2,1,0:T(2,128)S(1)}, u32[]{:S(2)}, u32[]{:S(2)}) collective-permute-start(f32[3,2,1024]{2,1,0:T(2,128)S(1)} %get-tuple-element.15), channel_id=1, source_target_pairs={{0,8},{1,9},{2,10},{3,11},{4,12},{5,13},{6,14},{7,15},{8,16},{9,17... | collective-permute-start | bytes 73736 | tf_op jit(solution)/shard_map/ppermute | solution.py:384
  22.0 3.2 %collective-permute-done.refs_1_ = f32[3,2,1024]{2,1,0:T(2,128)S(1)} collective-permute-done((f32[3,2,1024]{2,1,0:T(2,128)S(1)}, f32[3,2,1024]{2,1,0:T(2,128)S(1)}, u32[]{:S(2)}, u32[]{:S(2)}) %collective-permute-start) | collective-permute-done | bytes 24608 | tf_op jit(solution)/shard_map/ppermute | solution.py:384
  25.2 2.9 %ends.1 = (bf16[2,128,128]{2,1,0:T(8,128)(2,1)S(1)}, f32[128,1024]{1,0:T(8,128)}, f32[128,1024]{1,0:T(8,128)}) custom-call(bf16[3,128,1024]{2,1,0:T(8,128)(2,1)} %refs_0_.4, f32[3,2,1024]{2,1,0:T(2,128)S(1)} %collective-permute-done.refs_1_, f32[3,3,1024]{2,1,0:T(4,128)} %refs_2_.1, f32[16,1024]{1,0:T(8,128)} %refs_0_.5), custom_call_target="tpu_custom_call" | custom-call | flops 1000000000 | bytes 2000000 | tf_op jit(solution)/shard_map/ends/pallas_call | solution.py:93
  28.1 0.0 collective-permute-done.1.refs_2_.refs_1_
  28.1 0.0 all-to-all-done.refs_0_.refs_1_
  28.1 1.2 %spread.1.refs_2_ = bf16[4,10,128,128]{3,2,1,0:T(8,128)(2,1)} custom-call(bf16[4,3,128,128]{3,2,1,0:T(8,128)(2,1)S(1)} %all-to-all-done.refs_0_.refs_1_, bf16[2,128,128]{2,1,0:T(8,128)(2,1)S(1)} %get-tuple-element.16.refs_1_, bf16[512,256]{1,0:T(8,128)(2,1)S(1)} %collective-permute-done.1.refs_2_.refs_1_), custom_call_target="tpu_custom_call" | custom-call | flops 100000000 | bytes 2000000 | tf_op jit(solution)/shard_map/spread/pallas_call | solution.py:93
  29.4 0.0 copy-start
  29.4 5.2 %all-to-all-start.1 = ((bf16[4,10,128,128]{3,2,1,0:T(8,128)(2,1)}), bf16[4,10,128,128]{3,2,1,0:T(8,128)(2,1)S(1)}, u32[]{:S(2)}, u32[]{:S(2)}) async-start(bf16[4,10,128,128]{3,2,1,0:T(8,128)(2,1)} %spread.1.refs_2_), calls=%async_computation.1 | async-start | bytes 2621440 | tf_op jit(solution)/shard_map/all_to_all | solution.py:418
  34.6 0.0 all-gather.3.cloned.1.call-start
  34.6 0.0 copy-done
  34.6 10.2 %collective-permute-start.6 = (bf16[2,128,256]{2,1,0:T(8,128)(2,1)S(1)}, bf16[2,128,256]{2,1,0:T(8,128)(2,1)S(1)}, u32[]{:S(2)}, u32[]{:S(2)}) collective-permute-start(bf16[2,128,256]{2,1,0:T(8,128)(2,1)S(1)} %get-tuple-element.23), channel_id=1, source_target_pairs={{0,16},{1,17},{2,18},{3,19},{4,20},{5,21},{6,22},{7,23},{8,24},{9,... | collective-permute-start | bytes 393224 | tf_op jit(solution)/shard_map/ppermute | solution.py:427
  44.8 0.0 collective-permute-start.7
  44.8 1.6 %collective-permute-start.8 = (bf16[2,128,256]{2,1,0:T(8,128)(2,1)S(1)}, bf16[2,128,256]{2,1,0:T(8,128)(2,1)S(1)}, u32[]{:S(2)}, u32[]{:S(2)}) collective-permute-start(bf16[2,128,256]{2,1,0:T(8,128)(2,1)S(1)} %get-tuple-element.23), channel_id=1, source_target_pairs={{0,48},{1,49},{2,50},{3,51},{4,52},{5,53},{6,54},{7,55},{8,56},{9,... | collective-permute-start | bytes 393224 | tf_op jit(solution)/shard_map/ppermute | solution.py:427
  46.3 6.5 %collective-permute-done.6.refs_2_ = bf16[2,128,256]{2,1,0:T(8,128)(2,1)S(1)} collective-permute-done((bf16[2,128,256]{2,1,0:T(8,128)(2,1)S(1)}, bf16[2,128,256]{2,1,0:T(8,128)(2,1)S(1)}, u32[]{:S(2)}, u32[]{:S(2)}) %collective-permute-start.6) | collective-permute-done | bytes 131104 | tf_op jit(solution)/shard_map/ppermute | solution.py:427
  52.9 1.4 %collective-permute-done.7.refs_3_ = bf16[2,128,256]{2,1,0:T(8,128)(2,1)S(1)} collective-permute-done((bf16[2,128,256]{2,1,0:T(8,128)(2,1)S(1)}, bf16[2,128,256]{2,1,0:T(8,128)(2,1)S(1)}, u32[]{:S(2)}, u32[]{:S(2)}) %collective-permute-start.7) | collective-permute-done | bytes 131104 | tf_op jit(solution)/shard_map/ppermute | solution.py:427
  54.3 0.0 collective-permute-done.8.refs_4_
  54.3 0.0 all-to-all-done.1.refs_2_.refs_5_
  54.3 0.8 stack.35
  55.1 0.0 all-gather.3.cloned.1.call-update
  55.1 0.1 collective-permute-start.2
  55.2 0.1 pad_add_fusion.1.refs_0_
  55.3 3.1 %own.1 = (f32[1,512]{1,0:T(1,128)S(1)}, f32[1,512]{1,0:T(1,128)S(1)}, f32[128,512]{1,0:T(8,128)S(1)}) custom-call(s32[2]{0:T(128)S(1)} %pad_add_fusion.1.refs_0_, bf16[4,3,128,128]{3,2,1,0:T(8,128)(2,1)S(1)} %all-to-all-done.refs_0_.refs_1_, bf16[4,10,128,128]{3,2,1,0:T(8,128)(2,1)S(1)} %all-to-all-done.1.refs_2_.refs_5_), custom_call_target="tpu_custom_call" | custom-call | flops 2000000000 | bytes 2000000 | tf_op jit(solution)/shard_map/own/pallas_call | solution.py:93
  58.5 0.0 collective-permute-done.2.refs_5_.refs_3_
  58.5 3.4 %other.1 = bf16[2,2,256,128]{3,2,1,0:T(8,128)(2,1)S(1)} custom-call(s32[2]{0:T(128)S(1)} %pad_add_fusion.1.refs_0_, bf16[4,3,128,128]{3,2,1,0:T(8,128)(2,1)S(1)} %all-to-all-done.refs_0_.refs_1_, f32[1,512]{1,0:T(1,128)S(1)} %get-tuple-element.17.refs_2_, f32[1,512]{1,0:T(1,128)S(1)} %get-tuple-element.18.refs_3_, f32[128,512]{1,0:T(8,128)S(1)} %get-tuple-element.19.refs_4_, ...), custom_call_target="tpu_custom_call" | custom-call | flops 2000000000 | bytes 2000000 | tf_op jit(solution)/shard_map/other/pallas_call | solution.py:93
  61.9 20.7 %all_to_all.20.refs_4_.refs_1_ = bf16[4,256,128]{2,1,0:T(8,128)(2,1)S(1)} all-to-all(bf16[4,256,128]{2,1,0:T(8,128)(2,1)S(1)} %bitcast.7), channel_id=1, replica_groups=mesh['x'=4,'z1'=2,'z0'=2,'k'=2,'y'=4,'h'=2] {'h','z1'}, dimensions={0} | all-to-all | bytes 524288 | tf_op jit(solution)/shard_map/all_to_all | solution.py:450
  82.6 0.2 collective-permute-start.3
  82.8 3.0 %collective-permute-start.4 = (bf16[4,256,128]{2,1,0:T(8,128)(2,1)S(1)}, bf16[4,256,128]{2,1,0:T(8,128)(2,1)S(1)}, u32[]{:S(2)}, u32[]{:S(2)}) collective-permute-start(bf16[4,256,128]{2,1,0:T(8,128)(2,1)S(1)} %all_to_all.20.refs_4_.refs_1_), channel_id=1, source_target_pairs={{0,6},{2,0},{4,2},{6,4},{1,7},{3,1},{5,3},{7,5},{8,14},{10,8},{12,... | collective-permute-start | bytes 786440 | tf_op jit(solution)/shard_map/ppermute | solution.py:452
  85.8 0.7 collective-permute-start.5
  86.5 0.1 pad_add_fusion.refs_0_
  86.6 2.3 %combine.1 = f32[4,16,1024]{2,1,0:T(8,128)} custom-call(s32[3]{0:T(128)S(1)} %pad_add_fusion.refs_0_, f32[16,1024]{1,0:T(8,128)} %refs_0_.5, bf16[4,10,128,128]{3,2,1,0:T(8,128)(2,1)S(1)} %all-to-all-done.1.refs_2_.refs_5_, bf16[4,10,128,128]{3,2,1,0:T(8,128)(2,1)S(1)} %collective-permute-done.2.refs_5_.refs_3_, ...), custom_call_target="tpu_custom_call" | custom-call | flops 100000000 | bytes 2000000 | tf_op jit(solution)/shard_map/combine/pallas_call | solution.py:93
  89.0 3.7 %all-to-all-start.3 = ((f32[4,16,1024]{2,1,0:T(8,128)}), f32[4,16,1024]{2,1,0:T(8,128)S(1)}, u32[]{:S(2)}, u32[]{:S(2)}) async-start(f32[4,16,1024]{2,1,0:T(8,128)} %combine.1), calls=%async_computation.3 | async-start | bytes 524288 | tf_op jit(solution)/shard_map/all_to_all | solution.py:464
  92.6 0.1 pad_add_fusion.2.refs_0_
  92.7 0.0 collective-permute-done.3.refs_2_
  92.7 2.9 %collective-permute-done.4.refs_3_ = bf16[4,256,128]{2,1,0:T(8,128)(2,1)S(1)} collective-permute-done((bf16[4,256,128]{2,1,0:T(8,128)(2,1)S(1)}, bf16[4,256,128]{2,1,0:T(8,128)(2,1)S(1)}, u32[]{:S(2)}, u32[]{:S(2)}) %collective-permute-start.4) | collective-permute-done | bytes 262176 | tf_op jit(solution)/shard_map/ppermute | solution.py:452
  95.6 1.6 %collective-permute-done.5.refs_4_ = bf16[4,256,128]{2,1,0:T(8,128)(2,1)} collective-permute-done((bf16[4,256,128]{2,1,0:T(8,128)(2,1)S(1)}, bf16[4,256,128]{2,1,0:T(8,128)(2,1)}, u32[]{:S(2)}, u32[]{:S(2)}) %collective-permute-start.5) | collective-permute-done | bytes 262176 | tf_op jit(solution)/shard_map/ppermute | solution.py:452
  97.2 0.0 all-gather.3.cloned.1.call-done
  97.2 4.0 %project.1 = (f32[128,1024]{1,0:T(8,128)S(1)}, bf16[128,1024]{1,0:T(8,128)(2,1)S(1)}) custom-call(s32[2]{0:T(128)S(1)} %pad_add_fusion.2.refs_0_, bf16[4,256,128]{2,1,0:T(8,128)(2,1)S(1)} %all_to_all.20.refs_4_.refs_1_, bf16[4,256,128]{2,1,0:T(8,128)(2,1)S(1)} %collective-permute-done.3.refs_2_, bf16[4,256,128]{2,1,0:T(8,128)(2,1)S(1)} %collective-permute-done.4.refs_3_, ...), custom_call_target="tpu_custom_call" | custom-call | flops 2000000000 | bytes 2000000 | tf_op jit(solution)/shard_map/project/pallas_call | solution.py:93
  101.1 0.1 collective-permute-start.9
  101.2 0.0 all-to-all-done.3.refs_2_
  101.2 4.1 %mix.1 = bf16[128,1024]{1,0:T(8,128)(2,1)} custom-call(f32[16,1024]{1,0:T(8,128)} %refs_0_.5, f32[16,1024]{1,0:T(8,128)} %refs_1_.5, f32[4,16,1024]{2,1,0:T(8,128)S(1)} %all-to-all-done.3.refs_2_, f32[128,1024]{1,0:T(8,128)} %get-tuple-element.20.refs_3_, f32[128,1024]{1,0:T(8,128)} %get-tuple-element.21.refs_4_), custom_call_target="tpu_custom_call" | custom-call | flops 4000000000 | bytes 2000000 | tf_op jit(solution)/shard_map/mix/pallas_call | solution.py:93
  105.4 2.2 %collective-permute-done.9 = bf16[128,1024]{1,0:T(8,128)(2,1)S(1)} collective-permute-done((bf16[128,1024]{1,0:T(8,128)(2,1)S(1)}, bf16[128,1024]{1,0:T(8,128)(2,1)S(1)}, u32[]{:S(2)}, u32[]{:S(2)}) %collective-permute-start.9) | collective-permute-done | bytes 262176 | tf_op jit(solution)/shard_map/ppermute | solution.py:479
  107.6 0.8 add_convert_fusion
  (1 shorter events, 0.0 us)
Async XLA Ops:
  7.2 7.9 %copy-start.1 = (bf16[512,256]{1,0:T(8,128)(2,1)S(1)}, bf16[512,256]{1,0:T(8,128)(2,1)}, u32[]{:S(2)}) copy-start(bf16[512,256]{1,0:T(8,128)(2,1)} %param.11) | copy-start | bytes 786436
  9.1 19.0 %all-to-all-start = ((bf16[4,3,128,128]{3,2,1,0:T(8,128)(2,1)}), bf16[4,3,128,128]{3,2,1,0:T(8,128)(2,1)S(1)}, u32[]{:S(2)}, u32[]{:S(2)}) async-start(bf16[4,3,128,128]{3,2,1,0:T(8,128)(2,1)} %get-tuple-element.14), calls=%async_computation | async-start | bytes 786432 | tf_op jit(solution)/shard_map/all_to_all | solution.py:383
  15.1 13.0 %collective-permute-start.1 = (bf16[512,256]{1,0:T(8,128)(2,1)S(1)}, bf16[512,256]{1,0:T(8,128)(2,1)S(1)}, u32[]{:S(2)}, u32[]{:S(2)}) collective-permute-start(bf16[512,256]{1,0:T(8,128)(2,1)S(1)} %copy-done.1), channel_id=1, source_target_pairs={{0,0},{1,32},{2,64},{3,96},{4,128},{5,160},{6,192},{7,224},{8,8},{... | collective-permute-start | bytes 786440 | tf_op jit(solution)/shard_map/ppermute | solution.py:408
  20.0 5.1 %collective-permute-start = (f32[3,2,1024]{2,1,0:T(2,128)S(1)}, f32[3,2,1024]{2,1,0:T(2,128)S(1)}, u32[]{:S(2)}, u32[]{:S(2)}) collective-permute-start(f32[3,2,1024]{2,1,0:T(2,128)S(1)} %get-tuple-element.15), channel_id=1, source_target_pairs={{0,8},{1,9},{2,10},{3,11},{4,12},{5,13},{6,14},{7,15},{8,16},{9,17... | collective-permute-start | bytes 73736 | tf_op jit(solution)/shard_map/ppermute | solution.py:384
  29.4 5.2 %copy-start = (bf16[4,10,128,128]{3,2,1,0:T(8,128)(2,1)S(1)}, bf16[4,10,128,128]{3,2,1,0:T(8,128)(2,1)}, u32[]{:S(2)}) copy-start(bf16[4,10,128,128]{3,2,1,0:T(8,128)(2,1)} %spread.1.refs_2_) | copy-start | bytes 3932164
  29.4 24.9 %all-to-all-start.1 = ((bf16[4,10,128,128]{3,2,1,0:T(8,128)(2,1)}), bf16[4,10,128,128]{3,2,1,0:T(8,128)(2,1)S(1)}, u32[]{:S(2)}, u32[]{:S(2)}) async-start(bf16[4,10,128,128]{3,2,1,0:T(8,128)(2,1)} %spread.1.refs_2_), calls=%async_computation.1 | async-start | bytes 2621440 | tf_op jit(solution)/shard_map/all_to_all | solution.py:418
  34.6 62.6 %all-gather.3.cloned.1.call-start = ((), (), s32[]{:S(2)}) async-start(), calls=%async_computation.4 | async-start | bytes 4718592 | tf_op jit(solution)/shard_map/all_gather | solution.py:434
  34.6 18.3 %collective-permute-start.6 = (bf16[2,128,256]{2,1,0:T(8,128)(2,1)S(1)}, bf16[2,128,256]{2,1,0:T(8,128)(2,1)S(1)}, u32[]{:S(2)}, u32[]{:S(2)}) collective-permute-start(bf16[2,128,256]{2,1,0:T(8,128)(2,1)S(1)} %get-tuple-element.23), channel_id=1, source_target_pairs={{0,16},{1,17},{2,18},{3,19},{4,20},{5,21},{6,22},{7,23},{8,24},{9,... | collective-permute-start | bytes 393224 | tf_op jit(solution)/shard_map/ppermute | solution.py:427
  44.8 9.5 %collective-permute-start.7 = (bf16[2,128,256]{2,1,0:T(8,128)(2,1)S(1)}, bf16[2,128,256]{2,1,0:T(8,128)(2,1)S(1)}, u32[]{:S(2)}, u32[]{:S(2)}) collective-permute-start(bf16[2,128,256]{2,1,0:T(8,128)(2,1)S(1)} %get-tuple-element.22.refs_1_), channel_id=1, source_target_pairs={{0,32},{1,33},{2,34},{3,35},{4,36},{5,37},{6,38},{7,39},{8,40},{9,... | collective-permute-start | bytes 393224 | tf_op jit(solution)/shard_map/ppermute | solution.py:427
  44.8 9.5 %collective-permute-start.8 = (bf16[2,128,256]{2,1,0:T(8,128)(2,1)S(1)}, bf16[2,128,256]{2,1,0:T(8,128)(2,1)S(1)}, u32[]{:S(2)}, u32[]{:S(2)}) collective-permute-start(bf16[2,128,256]{2,1,0:T(8,128)(2,1)S(1)} %get-tuple-element.23), channel_id=1, source_target_pairs={{0,48},{1,49},{2,50},{3,51},{4,52},{5,53},{6,54},{7,55},{8,56},{9,... | collective-permute-start | bytes 393224 | tf_op jit(solution)/shard_map/ppermute | solution.py:427
  55.1 3.3 %collective-permute-start.2 = (bf16[4,10,128,128]{3,2,1,0:T(8,128)(2,1)S(1)}, bf16[4,10,128,128]{3,2,1,0:T(8,128)(2,1)S(1)}, u32[]{:S(2)}, u32[]{:S(2)}) collective-permute-start(bf16[4,10,128,128]{3,2,1,0:T(8,128)(2,1)S(1)} %all-to-all-done.1.refs_2_.refs_5_), channel_id=1, source_target_pairs={{0,8},{8,0},{1,9},{9,1},{2,10},{10,2},{3,11},{11,3},{4,12},{12,4},... | collective-permute-start | bytes 3932168 | tf_op jit(solution)/shard_map/ppermute | solution.py:419
  82.6 10.1 %collective-permute-start.3 = (bf16[4,256,128]{2,1,0:T(8,128)(2,1)S(1)}, bf16[4,256,128]{2,1,0:T(8,128)(2,1)S(1)}, u32[]{:S(2)}, u32[]{:S(2)}) collective-permute-start(bf16[4,256,128]{2,1,0:T(8,128)(2,1)S(1)} %all_to_all.20.refs_4_.refs_1_), channel_id=1, source_target_pairs={{0,2},{2,4},{4,6},{6,0},{1,3},{3,5},{5,7},{7,1},{8,10},{10,12},{12... | collective-permute-start | bytes 786440 | tf_op jit(solution)/shard_map/ppermute | solution.py:452
  82.8 12.8 %collective-permute-start.4 = (bf16[4,256,128]{2,1,0:T(8,128)(2,1)S(1)}, bf16[4,256,128]{2,1,0:T(8,128)(2,1)S(1)}, u32[]{:S(2)}, u32[]{:S(2)}) collective-permute-start(bf16[4,256,128]{2,1,0:T(8,128)(2,1)S(1)} %all_to_all.20.refs_4_.refs_1_), channel_id=1, source_target_pairs={{0,6},{2,0},{4,2},{6,4},{1,7},{3,1},{5,3},{7,5},{8,14},{10,8},{12,... | collective-permute-start | bytes 786440 | tf_op jit(solution)/shard_map/ppermute | solution.py:452
  85.8 11.4 %collective-permute-start.5 = (bf16[4,256,128]{2,1,0:T(8,128)(2,1)S(1)}, bf16[4,256,128]{2,1,0:T(8,128)(2,1)}, u32[]{:S(2)}, u32[]{:S(2)}) collective-permute-start(bf16[4,256,128]{2,1,0:T(8,128)(2,1)S(1)} %all_to_all.20.refs_4_.refs_1_), channel_id=1, source_target_pairs={{0,4},{2,6},{4,0},{6,2},{1,5},{3,7},{5,1},{7,3},{8,12},{10,14},{12... | collective-permute-start | bytes 786440 | tf_op jit(solution)/shard_map/ppermute | solution.py:452
  89.0 12.3 %all-to-all-start.3 = ((f32[4,16,1024]{2,1,0:T(8,128)}), f32[4,16,1024]{2,1,0:T(8,128)S(1)}, u32[]{:S(2)}, u32[]{:S(2)}) async-start(f32[4,16,1024]{2,1,0:T(8,128)} %combine.1), calls=%async_computation.3 | async-start | bytes 524288 | tf_op jit(solution)/shard_map/all_to_all | solution.py:464
  101.1 6.5 %collective-permute-start.9 = (bf16[128,1024]{1,0:T(8,128)(2,1)S(1)}, bf16[128,1024]{1,0:T(8,128)(2,1)S(1)}, u32[]{:S(2)}, u32[]{:S(2)}) collective-permute-start(bf16[128,1024]{1,0:T(8,128)(2,1)S(1)} %get-tuple-element.25), channel_id=1, source_target_pairs={{0,16},{16,0},{1,17},{17,1},{2,18},{18,2},{3,19},{19,3},{4,20},{20... | collective-permute-start | bytes 786440 | tf_op jit(solution)/shard_map/ppermute | solution.py:479
Sparse Core Ops, SparseCore 0:
  55.2 36.4 all-gather.2

commit v6 on v4

--- a/solution.py
+++ b/solution.py
@@ -238,7 +238,7 @@
     pairs = [(qkv.at[:, :, lanes[i]], out_ref.at[i]) for i in range(NZ)]
     pairs.append((feats.at[:, pl.ds(rows - 16, 16), :], tail))
     finished(started(sems, pairs))
-    halo_ref[...] = tail[:, 14:16].astype(jnp.float32)
+    halo_ref[...] = tail[...].astype(jnp.float32)[:, 14:16]
 
 
 def halves_kernel(place_ref, weight_ref, same_ref, other_ref):

time: 115 us -> 115 us (level)
  no operation moved by 1% of the time
where the time goes in v6:
time: 115 us
  starting transfers between devices  37.4 us (33%)
  Pallas kernels  23.7 us (21%)
  blocking collectives  20.7 us (18%)
  waiting for transfers between devices  17.8 us (15%)
  between operations  14.2 us (12%)
    pallas_call x10, Pallas kernels, local_call(): return lambda *operands: call(*map(placed, operands, specs), *after)  23.7 us
    all_to_all x1, blocking collectives, per_device(): lax.all_to_all(attended.reshape(NH * NZ1, NZ0 * rows, HEAD), ('h', 'z1'),...  20.7 us
    ppermute x3, starting transfers between devices, per_device(): lax.ppermute(opposite if steps % 2 else same, ALL, along_z(steps))  11.7 us
    ppermute x3, waiting for transfers between devices, per_device(): lax.ppermute(opposite if steps % 2 else same, ALL, along_z(steps))  7.92 us
    all_to_all x1, starting transfers between devices, per_device(): qkv = lax.all_to_all(packed, ('z1', 'z0'), 0, 0)  6.01 us
    all_to_all x1, starting transfers between devices, per_device(): far_own = lax.all_to_all(spread, 'x', 0, 0)  5.05 us
    ppermute x1, starting transfers between devices, per_device(): moved_weight = lax.ppermute(out_weight, ALL, moved(place_weight))  4.91 us
    ppermute x3, waiting for transfers between devices, per_device(): lax.ppermute(group, 'y', [(i, (i + step) % NY) for i in range(NY)])  4.46 us
  transfers between devices with their start and end apart: 14, of which 6 were waited for; matrix products, arithmetic and copies ran while one was open for 0% of the time, Pallas kernels for 17%

profile of v6, /device:TPU:38, one launch (start us, length us, event | category | flops | bytes accessed | tf_op | source)
XLA Modules:
  0.0 114.8 jit_solution(17347059701033179507)
XLA Ops:
  7.2 0.0 copy-start
  7.2 1.9 %pack.1 = (bf16[4,3,128,128]{3,2,1,0:T(8,128)(2,1)}, f32[3,2,1024]{2,1,0:T(2,128)S(1)}) custom-call(bf16[3,128,512]{2,1,0:T(8,128)(2,1)} %refs_0_.3, bf16[3,128,1024]{2,1,0:T(8,128)(2,1)} %refs_0_.4), custom_call_target="tpu_custom_call" | custom-call | flops 100000000 | bytes 2000000 | tf_op jit(solution)/shard_map/pack/pallas_call | solution.py:93
  9.1 6.0 %all-to-all-start = ((bf16[4,3,128,128]{3,2,1,0:T(8,128)(2,1)}), bf16[4,3,128,128]{3,2,1,0:T(8,128)(2,1)S(1)}, u32[]{:S(2)}, u32[]{:S(2)}) async-start(bf16[4,3,128,128]{3,2,1,0:T(8,128)(2,1)} %get-tuple-element.14), calls=%async_computation | async-start | bytes 786432 | tf_op jit(solution)/shard_map/all_to_all | solution.py:376
  15.1 0.0 copy-done
  15.1 4.9 %collective-permute-start.1 = (bf16[512,256]{1,0:T(8,128)(2,1)S(1)}, bf16[512,256]{1,0:T(8,128)(2,1)S(1)}, u32[]{:S(2)}, u32[]{:S(2)}) collective-permute-start(bf16[512,256]{1,0:T(8,128)(2,1)S(1)} %copy-done), channel_id=1, source_target_pairs={{0,0},{1,32},{2,64},{3,96},{4,128},{5,160},{6,192},{7,224},{8,8},{... | collective-permute-start | bytes 786440 | tf_op jit(solution)/shard_map/ppermute | solution.py:401
  20.0 1.9 %collective-permute-start = (f32[3,2,1024]{2,1,0:T(2,128)S(1)}, f32[3,2,1024]{2,1,0:T(2,128)S(1)}, u32[]{:S(2)}, u32[]{:S(2)}) collective-permute-start(f32[3,2,1024]{2,1,0:T(2,128)S(1)} %get-tuple-element.15), channel_id=1, source_target_pairs={{0,8},{1,9},{2,10},{3,11},{4,12},{5,13},{6,14},{7,15},{8,16},{9,17... | collective-permute-start | bytes 73736 | tf_op jit(solution)/shard_map/ppermute | solution.py:377
  22.0 3.2 %collective-permute-done.refs_1_ = f32[3,2,1024]{2,1,0:T(2,128)S(1)} collective-permute-done((f32[3,2,1024]{2,1,0:T(2,128)S(1)}, f32[3,2,1024]{2,1,0:T(2,128)S(1)}, u32[]{:S(2)}, u32[]{:S(2)}) %collective-permute-start) | collective-permute-done | bytes 24608 | tf_op jit(solution)/shard_map/ppermute | solution.py:377
  25.2 2.9 %ends.1 = (bf16[2,128,128]{2,1,0:T(8,128)(2,1)S(1)}, f32[128,1024]{1,0:T(8,128)}, f32[128,1024]{1,0:T(8,128)}) custom-call(bf16[3,128,1024]{2,1,0:T(8,128)(2,1)} %refs_0_.4, f32[3,2,1024]{2,1,0:T(2,128)S(1)} %collective-permute-done.refs_1_, f32[3,3,1024]{2,1,0:T(4,128)} %refs_2_.1, f32[16,1024]{1,0:T(8,128)} %refs_0_.5), custom_call_target="tpu_custom_call" | custom-call | flops 1000000000 | bytes 2000000 | tf_op jit(solution)/shard_map/ends/pallas_call | solution.py:93
  28.1 0.0 collective-permute-done.1.refs_2_.refs_1_
  28.1 0.0 all-to-all-done.refs_0_.refs_1_
  28.1 1.2 %spread.1.refs_2_ = bf16[4,10,128,128]{3,2,1,0:T(8,128)(2,1)} custom-call(bf16[4,3,128,128]{3,2,1,0:T(8,128)(2,1)S(1)} %all-to-all-done.refs_0_.refs_1_, bf16[2,128,128]{2,1,0:T(8,128)(2,1)S(1)} %get-tuple-element.16.refs_1_, bf16[512,256]{1,0:T(8,128)(2,1)S(1)} %collective-permute-done.1.refs_2_.refs_1_), custom_call_target="tpu_custom_call" | custom-call | flops 100000000 | bytes 2000000 | tf_op jit(solution)/shard_map/spread/pallas_call | solution.py:93
  29.4 5.0 %all-to-all-start.1 = ((bf16[4,10,128,128]{3,2,1,0:T(8,128)(2,1)}), bf16[4,10,128,128]{3,2,1,0:T(8,128)(2,1)S(1)}, u32[]{:S(2)}, u32[]{:S(2)}) async-start(bf16[4,10,128,128]{3,2,1,0:T(8,128)(2,1)} %spread.1.refs_2_), calls=%async_computation.1 | async-start | bytes 2621440 | tf_op jit(solution)/shard_map/all_to_all | solution.py:410
  34.4 0.0 all-gather.3.cloned.1.call-start
  34.4 10.2 %collective-permute-start.6 = (bf16[2,128,256]{2,1,0:T(8,128)(2,1)S(1)}, bf16[2,128,256]{2,1,0:T(8,128)(2,1)S(1)}, u32[]{:S(2)}, u32[]{:S(2)}) collective-permute-start(bf16[2,128,256]{2,1,0:T(8,128)(2,1)S(1)} %get-tuple-element.23), channel_id=1, source_target_pairs={{0,16},{1,17},{2,18},{3,19},{4,20},{5,21},{6,22},{7,23},{8,24},{9,... | collective-permute-start | bytes 393224 | tf_op jit(solution)/shard_map/ppermute | solution.py:419
  44.6 0.0 collective-permute-start.7
  44.6 1.6 %collective-permute-start.8 = (bf16[2,128,256]{2,1,0:T(8,128)(2,1)S(1)}, bf16[2,128,256]{2,1,0:T(8,128)(2,1)S(1)}, u32[]{:S(2)}, u32[]{:S(2)}) collective-permute-start(bf16[2,128,256]{2,1,0:T(8,128)(2,1)S(1)} %get-tuple-element.23), channel_id=1, source_target_pairs={{0,48},{1,49},{2,50},{3,51},{4,52},{5,53},{6,54},{7,55},{8,56},{9,... | collective-permute-start | bytes 393224 | tf_op jit(solution)/shard_map/ppermute | solution.py:419
  46.2 6.5 %collective-permute-done.6.refs_2_ = bf16[2,128,256]{2,1,0:T(8,128)(2,1)S(1)} collective-permute-done((bf16[2,128,256]{2,1,0:T(8,128)(2,1)S(1)}, bf16[2,128,256]{2,1,0:T(8,128)(2,1)S(1)}, u32[]{:S(2)}, u32[]{:S(2)}) %collective-permute-start.6) | collective-permute-done | bytes 131104 | tf_op jit(solution)/shard_map/ppermute | solution.py:419
  52.7 1.4 %collective-permute-done.7.refs_3_ = bf16[2,128,256]{2,1,0:T(8,128)(2,1)S(1)} collective-permute-done((bf16[2,128,256]{2,1,0:T(8,128)(2,1)S(1)}, bf16[2,128,256]{2,1,0:T(8,128)(2,1)S(1)}, u32[]{:S(2)}, u32[]{:S(2)}) %collective-permute-start.7) | collective-permute-done | bytes 131104 | tf_op jit(solution)/shard_map/ppermute | solution.py:419
  54.1 0.0 collective-permute-done.8.refs_4_
  54.1 0.0 all-to-all-done.1.refs_2_.refs_5_
  54.1 0.8 stack.35
  54.9 0.0 all-gather.3.cloned.1.call-update
  55.0 0.1 collective-permute-start.2
  55.1 0.1 pad_add_fusion.1.refs_0_
  55.1 3.1 %own.1 = (f32[1,512]{1,0:T(1,128)S(1)}, f32[1,512]{1,0:T(1,128)S(1)}, f32[128,512]{1,0:T(8,128)S(1)}) custom-call(s32[2]{0:T(128)S(1)} %pad_add_fusion.1.refs_0_, bf16[4,3,128,128]{3,2,1,0:T(8,128)(2,1)S(1)} %all-to-all-done.refs_0_.refs_1_, bf16[4,10,128,128]{3,2,1,0:T(8,128)(2,1)S(1)} %all-to-all-done.1.refs_2_.refs_5_), custom_call_target="tpu_custom_call" | custom-call | flops 2000000000 | bytes 2000000 | tf_op jit(solution)/shard_map/own/pallas_call | solution.py:93
  58.3 0.0 collective-permute-done.2.refs_5_.refs_3_
  58.3 3.4 %other.1 = bf16[2,2,256,128]{3,2,1,0:T(8,128)(2,1)S(1)} custom-call(s32[2]{0:T(128)S(1)} %pad_add_fusion.1.refs_0_, bf16[4,3,128,128]{3,2,1,0:T(8,128)(2,1)S(1)} %all-to-all-done.refs_0_.refs_1_, f32[1,512]{1,0:T(1,128)S(1)} %get-tuple-element.17.refs_2_, f32[1,512]{1,0:T(1,128)S(1)} %get-tuple-element.18.refs_3_, f32[128,512]{1,0:T(8,128)S(1)} %get-tuple-element.19.refs_4_, ...), custom_call_target="tpu_custom_call" | custom-call | flops 2000000000 | bytes 2000000 | tf_op jit(solution)/shard_map/other/pallas_call | solution.py:93
  61.7 20.7 %all_to_all.20.refs_4_.refs_1_ = bf16[4,256,128]{2,1,0:T(8,128)(2,1)S(1)} all-to-all(bf16[4,256,128]{2,1,0:T(8,128)(2,1)S(1)} %bitcast.7), channel_id=1, replica_groups=mesh['x'=4,'z1'=2,'z0'=2,'k'=2,'y'=4,'h'=2] {'h','z1'}, dimensions={0} | all-to-all | bytes 524288 | tf_op jit(solution)/shard_map/all_to_all | solution.py:441
  82.4 0.2 collective-permute-start.3
  82.6 3.0 %collective-permute-start.4 = (bf16[4,256,128]{2,1,0:T(8,128)(2,1)S(1)}, bf16[4,256,128]{2,1,0:T(8,128)(2,1)S(1)}, u32[]{:S(2)}, u32[]{:S(2)}) collective-permute-start(bf16[4,256,128]{2,1,0:T(8,128)(2,1)S(1)} %all_to_all.20.refs_4_.refs_1_), channel_id=1, source_target_pairs={{0,6},{2,0},{4,2},{6,4},{1,7},{3,1},{5,3},{7,5},{8,14},{10,8},{12,... | collective-permute-start | bytes 786440 | tf_op jit(solution)/shard_map/ppermute | solution.py:443
  85.6 0.7 collective-permute-start.5
  86.4 0.1 pad_add_fusion.refs_0_
  86.5 2.3 %combine.1 = f32[4,16,1024]{2,1,0:T(8,128)} custom-call(s32[3]{0:T(128)S(1)} %pad_add_fusion.refs_0_, f32[16,1024]{1,0:T(8,128)} %refs_0_.5, bf16[4,10,128,128]{3,2,1,0:T(8,128)(2,1)S(1)} %all-to-all-done.1.refs_2_.refs_5_, bf16[4,10,128,128]{3,2,1,0:T(8,128)(2,1)S(1)} %collective-permute-done.2.refs_5_.refs_3_, ...), custom_call_target="tpu_custom_call" | custom-call | flops 100000000 | bytes 2000000 | tf_op jit(solution)/shard_map/combine/pallas_call | solution.py:93
  88.8 3.7 %all-to-all-start.3 = ((f32[4,16,1024]{2,1,0:T(8,128)}), f32[4,16,1024]{2,1,0:T(8,128)S(1)}, u32[]{:S(2)}, u32[]{:S(2)}) async-start(f32[4,16,1024]{2,1,0:T(8,128)} %combine.1), calls=%async_computation.3 | async-start | bytes 524288 | tf_op jit(solution)/shard_map/all_to_all | solution.py:455
  92.5 0.1 pad_add_fusion.2.refs_0_
  92.5 0.0 collective-permute-done.3.refs_2_
  92.5 2.9 %collective-permute-done.4.refs_3_ = bf16[4,256,128]{2,1,0:T(8,128)(2,1)S(1)} collective-permute-done((bf16[4,256,128]{2,1,0:T(8,128)(2,1)S(1)}, bf16[4,256,128]{2,1,0:T(8,128)(2,1)S(1)}, u32[]{:S(2)}, u32[]{:S(2)}) %collective-permute-start.4) | collective-permute-done | bytes 262176 | tf_op jit(solution)/shard_map/ppermute | solution.py:443
  95.4 1.6 %collective-permute-done.5.refs_4_ = bf16[4,256,128]{2,1,0:T(8,128)(2,1)} collective-permute-done((bf16[4,256,128]{2,1,0:T(8,128)(2,1)S(1)}, bf16[4,256,128]{2,1,0:T(8,128)(2,1)}, u32[]{:S(2)}, u32[]{:S(2)}) %collective-permute-start.5) | collective-permute-done | bytes 262176 | tf_op jit(solution)/shard_map/ppermute | solution.py:443
  97.0 0.0 all-gather.3.cloned.1.call-done
  97.0 3.8 %project.1 = (f32[128,1024]{1,0:T(8,128)S(1)}, bf16[128,1024]{1,0:T(8,128)(2,1)S(1)}) custom-call(s32[2]{0:T(128)S(1)} %pad_add_fusion.2.refs_0_, bf16[4,256,128]{2,1,0:T(8,128)(2,1)S(1)} %all_to_all.20.refs_4_.refs_1_, bf16[4,256,128]{2,1,0:T(8,128)(2,1)S(1)} %collective-permute-done.3.refs_2_, bf16[4,256,128]{2,1,0:T(8,128)(2,1)S(1)} %collective-permute-done.4.refs_3_, ...), custom_call_target="tpu_custom_call" | custom-call | flops 2000000000 | bytes 2000000 | tf_op jit(solution)/shard_map/project/pallas_call | solution.py:93
  100.8 0.1 collective-permute-start.9
  100.9 0.0 all-to-all-done.3.refs_2_
  100.9 4.1 %mix.1 = bf16[128,1024]{1,0:T(8,128)(2,1)} custom-call(f32[16,1024]{1,0:T(8,128)} %refs_0_.5, f32[16,1024]{1,0:T(8,128)} %refs_1_.5, f32[4,16,1024]{2,1,0:T(8,128)S(1)} %all-to-all-done.3.refs_2_, f32[128,1024]{1,0:T(8,128)} %get-tuple-element.20.refs_3_, f32[128,1024]{1,0:T(8,128)} %get-tuple-element.21.refs_4_), custom_call_target="tpu_custom_call" | custom-call | flops 4000000000 | bytes 2000000 | tf_op jit(solution)/shard_map/mix/pallas_call | solution.py:93
  105.0 2.2 %collective-permute-done.9 = bf16[128,1024]{1,0:T(8,128)(2,1)S(1)} collective-permute-done((bf16[128,1024]{1,0:T(8,128)(2,1)S(1)}, bf16[128,1024]{1,0:T(8,128)(2,1)S(1)}, u32[]{:S(2)}, u32[]{:S(2)}) %collective-permute-start.9) | collective-permute-done | bytes 262176 | tf_op jit(solution)/shard_map/ppermute | solution.py:470
  107.2 0.8 add_convert_fusion
  (1 shorter events, 0.0 us)
Async XLA Ops:
  7.2 8.0 %copy-start = (bf16[512,256]{1,0:T(8,128)(2,1)S(1)}, bf16[512,256]{1,0:T(8,128)(2,1)}, u32[]{:S(2)}) copy-start(bf16[512,256]{1,0:T(8,128)(2,1)} %param.11) | copy-start | bytes 786436
  9.1 19.0 %all-to-all-start = ((bf16[4,3,128,128]{3,2,1,0:T(8,128)(2,1)}), bf16[4,3,128,128]{3,2,1,0:T(8,128)(2,1)S(1)}, u32[]{:S(2)}, u32[]{:S(2)}) async-start(bf16[4,3,128,128]{3,2,1,0:T(8,128)(2,1)} %get-tuple-element.14), calls=%async_computation | async-start | bytes 786432 | tf_op jit(solution)/shard_map/all_to_all | solution.py:376
  15.1 13.0 %collective-permute-start.1 = (bf16[512,256]{1,0:T(8,128)(2,1)S(1)}, bf16[512,256]{1,0:T(8,128)(2,1)S(1)}, u32[]{:S(2)}, u32[]{:S(2)}) collective-permute-start(bf16[512,256]{1,0:T(8,128)(2,1)S(1)} %copy-done), channel_id=1, source_target_pairs={{0,0},{1,32},{2,64},{3,96},{4,128},{5,160},{6,192},{7,224},{8,8},{... | collective-permute-start | bytes 786440 | tf_op jit(solution)/shard_map/ppermute | solution.py:401
  20.0 5.1 %collective-permute-start = (f32[3,2,1024]{2,1,0:T(2,128)S(1)}, f32[3,2,1024]{2,1,0:T(2,128)S(1)}, u32[]{:S(2)}, u32[]{:S(2)}) collective-permute-start(f32[3,2,1024]{2,1,0:T(2,128)S(1)} %get-tuple-element.15), channel_id=1, source_target_pairs={{0,8},{1,9},{2,10},{3,11},{4,12},{5,13},{6,14},{7,15},{8,16},{9,17... | collective-permute-start | bytes 73736 | tf_op jit(solution)/shard_map/ppermute | solution.py:377
  29.4 24.7 %all-to-all-start.1 = ((bf16[4,10,128,128]{3,2,1,0:T(8,128)(2,1)}), bf16[4,10,128,128]{3,2,1,0:T(8,128)(2,1)S(1)}, u32[]{:S(2)}, u32[]{:S(2)}) async-start(bf16[4,10,128,128]{3,2,1,0:T(8,128)(2,1)} %spread.1.refs_2_), calls=%async_computation.1 | async-start | bytes 2621440 | tf_op jit(solution)/shard_map/all_to_all | solution.py:410
  34.4 62.6 %all-gather.3.cloned.1.call-start = ((), (), s32[]{:S(2)}) async-start(), calls=%async_computation.4 | async-start | bytes 4718592 | tf_op jit(solution)/shard_map/all_gather | solution.py:425
  34.4 18.3 %collective-permute-start.6 = (bf16[2,128,256]{2,1,0:T(8,128)(2,1)S(1)}, bf16[2,128,256]{2,1,0:T(8,128)(2,1)S(1)}, u32[]{:S(2)}, u32[]{:S(2)}) collective-permute-start(bf16[2,128,256]{2,1,0:T(8,128)(2,1)S(1)} %get-tuple-element.23), channel_id=1, source_target_pairs={{0,16},{1,17},{2,18},{3,19},{4,20},{5,21},{6,22},{7,23},{8,24},{9,... | collective-permute-start | bytes 393224 | tf_op jit(solution)/shard_map/ppermute | solution.py:419
  44.6 9.5 %collective-permute-start.7 = (bf16[2,128,256]{2,1,0:T(8,128)(2,1)S(1)}, bf16[2,128,256]{2,1,0:T(8,128)(2,1)S(1)}, u32[]{:S(2)}, u32[]{:S(2)}) collective-permute-start(bf16[2,128,256]{2,1,0:T(8,128)(2,1)S(1)} %get-tuple-element.22.refs_1_), channel_id=1, source_target_pairs={{0,32},{1,33},{2,34},{3,35},{4,36},{5,37},{6,38},{7,39},{8,40},{9,... | collective-permute-start | bytes 393224 | tf_op jit(solution)/shard_map/ppermute | solution.py:419
  44.6 9.5 %collective-permute-start.8 = (bf16[2,128,256]{2,1,0:T(8,128)(2,1)S(1)}, bf16[2,128,256]{2,1,0:T(8,128)(2,1)S(1)}, u32[]{:S(2)}, u32[]{:S(2)}) collective-permute-start(bf16[2,128,256]{2,1,0:T(8,128)(2,1)S(1)} %get-tuple-element.23), channel_id=1, source_target_pairs={{0,48},{1,49},{2,50},{3,51},{4,52},{5,53},{6,54},{7,55},{8,56},{9,... | collective-permute-start | bytes 393224 | tf_op jit(solution)/shard_map/ppermute | solution.py:419
  55.0 3.3 %collective-permute-start.2 = (bf16[4,10,128,128]{3,2,1,0:T(8,128)(2,1)S(1)}, bf16[4,10,128,128]{3,2,1,0:T(8,128)(2,1)S(1)}, u32[]{:S(2)}, u32[]{:S(2)}) collective-permute-start(bf16[4,10,128,128]{3,2,1,0:T(8,128)(2,1)S(1)} %all-to-all-done.1.refs_2_.refs_5_), channel_id=1, source_target_pairs={{0,8},{8,0},{1,9},{9,1},{2,10},{10,2},{3,11},{11,3},{4,12},{12,4},... | collective-permute-start | bytes 3932168 | tf_op jit(solution)/shard_map/ppermute | solution.py:411
  82.4 10.1 %collective-permute-start.3 = (bf16[4,256,128]{2,1,0:T(8,128)(2,1)S(1)}, bf16[4,256,128]{2,1,0:T(8,128)(2,1)S(1)}, u32[]{:S(2)}, u32[]{:S(2)}) collective-permute-start(bf16[4,256,128]{2,1,0:T(8,128)(2,1)S(1)} %all_to_all.20.refs_4_.refs_1_), channel_id=1, source_target_pairs={{0,2},{2,4},{4,6},{6,0},{1,3},{3,5},{5,7},{7,1},{8,10},{10,12},{12... | collective-permute-start | bytes 786440 | tf_op jit(solution)/shard_map/ppermute | solution.py:443
  82.6 12.8 %collective-permute-start.4 = (bf16[4,256,128]{2,1,0:T(8,128)(2,1)S(1)}, bf16[4,256,128]{2,1,0:T(8,128)(2,1)S(1)}, u32[]{:S(2)}, u32[]{:S(2)}) collective-permute-start(bf16[4,256,128]{2,1,0:T(8,128)(2,1)S(1)} %all_to_all.20.refs_4_.refs_1_), channel_id=1, source_target_pairs={{0,6},{2,0},{4,2},{6,4},{1,7},{3,1},{5,3},{7,5},{8,14},{10,8},{12,... | collective-permute-start | bytes 786440 | tf_op jit(solution)/shard_map/ppermute | solution.py:443
  85.6 11.4 %collective-permute-start.5 = (bf16[4,256,128]{2,1,0:T(8,128)(2,1)S(1)}, bf16[4,256,128]{2,1,0:T(8,128)(2,1)}, u32[]{:S(2)}, u32[]{:S(2)}) collective-permute-start(bf16[4,256,128]{2,1,0:T(8,128)(2,1)S(1)} %all_to_all.20.refs_4_.refs_1_), channel_id=1, source_target_pairs={{0,4},{2,6},{4,0},{6,2},{1,5},{3,7},{5,1},{7,3},{8,12},{10,14},{12... | collective-permute-start | bytes 786440 | tf_op jit(solution)/shard_map/ppermute | solution.py:443
  88.8 12.1 %all-to-all-start.3 = ((f32[4,16,1024]{2,1,0:T(8,128)}), f32[4,16,1024]{2,1,0:T(8,128)S(1)}, u32[]{:S(2)}, u32[]{:S(2)}) async-start(f32[4,16,1024]{2,1,0:T(8,128)} %combine.1), calls=%async_computation.3 | async-start | bytes 524288 | tf_op jit(solution)/shard_map/all_to_all | solution.py:455
  100.8 6.5 %collective-permute-start.9 = (bf16[128,1024]{1,0:T(8,128)(2,1)S(1)}, bf16[128,1024]{1,0:T(8,128)(2,1)S(1)}, u32[]{:S(2)}, u32[]{:S(2)}) collective-permute-start(bf16[128,1024]{1,0:T(8,128)(2,1)S(1)} %get-tuple-element.25), channel_id=1, source_target_pairs={{0,16},{16,0},{1,17},{17,1},{2,18},{18,2},{3,19},{19,3},{4,20},{20... | collective-permute-start | bytes 786440 | tf_op jit(solution)/shard_map/ppermute | solution.py:470
Sparse Core Ops, SparseCore 0:
  55.1 36.4 all-gather.2

commit v7 on v6

--- a/solution.py
+++ b/solution.py
@@ -135,8 +135,12 @@
     feats, halo_ref, taps_hbm, decay_hbm, out_ref, prod_hbm, gate_hbm,
     x, taps, rate, prod, gate_rows, ext, sems, out_sems,
 ):
-    finished(started(sems, ((feats, x), (taps_hbm, taps), (decay_hbm, rate))))
     rows, order = x.shape[1], rate.shape[0]
+    half = rows // 2
+    pieces = [(i, pl.ds(lo, half)) for i in range(3) for lo in (0, half)]
+    pairs = [(taps_hbm, taps), (decay_hbm, rate)]
+    pairs += [(feats.at[i, part, :], x.at[i, part, :]) for i, part in pieces]
+    finished(started(sems, pairs))
     fill_ext(x, halo_ref, ext, (0, 1, 2))
     for lo in range(0, rows, 16):
         gate_rows[lo : lo + 16] = featured_rows(ext, taps, 0, 0, lo, 16)
@@ -327,13 +331,21 @@
 
 def project_kernel(place_ref, g0, g1, g2, g3, w_hbm, mine_ref, other_ref, held, parts, acc, sems):
     y, z0 = place_ref[0], place_ref[1]
-    copies = started(sems, [(w_hbm.at[i], parts.at[i]) for i in range(NX)])
+    copies = started(
+        sems,
+        [
+            (w_hbm.at[i, k, pl.ds(lo, 2)], parts.at[i, k, pl.ds(lo, 2)])
+            for i in range(NX)
+            for k in range(NK)
+            for lo in (0, 2)
+        ],
+    )
     for step, group in zip((0, 1, 3, 2), (g0, g1, g2, g3)):
         held[step] = group[...]
     for i in range(NX):
         step = (2 * y - i + NX) % NX
         heads = jnp.concatenate([held[step, j] for j in range(NH * NZ1)], axis=1)
-        copies[i].wait()
+        finished(copies[4 * i : 4 * i + 4])
         for k in range(NK):
             for b in range(2):
                 columns = [parts[i, k, 2 * h + b].reshape(2 * HEAD, 256) for h in range(NH)]
@@ -394,7 +406,7 @@
             pltpu.VMEM(plane.shape, f32),
             pltpu.VMEM(plane.shape, f32),
             pltpu.VMEM((3, rows + 8, width), f32),
-            dma((3,)),
+            dma((8,)),
             dma((2,)),
         ),
     )(hyena_feats, halo, short_taps, decay_rate)
@@ -464,7 +476,7 @@
             pltpu.VMEM((NY, *group.shape), bf16),
             pltpu.VMEM(weight.shape, bf16),
             pltpu.VMEM((NK, NZ0 * rows, width // 2), f32),
-            dma((NX,)),
+            dma((4 * NX,)),
         ),
     )(jnp.stack([y, z0]), *groups, weight)
     received = lax.ppermute(other, "z0", swap)

time: 115 us -> 115 us (level)
  no operation moved by 1% of the time
where the time goes in v7:
time: 115 us
  starting transfers between devices  37.3 us (32%)
  Pallas kernels  23.9 us (21%)
  blocking collectives  20.7 us (18%)
  waiting for transfers between devices  17.8 us (15%)
  between operations  14.2 us (12%)
    pallas_call x10, Pallas kernels, local_call(): return lambda *operands: call(*map(placed, operands, specs), *after)  23.9 us
    all_to_all x1, blocking collectives, per_device(): lax.all_to_all(attended.reshape(NH * NZ1, NZ0 * rows, HEAD), ('h', 'z1'),...  20.7 us
    ppermute x3, starting transfers between devices, per_device(): lax.ppermute(opposite if steps % 2 else same, ALL, along_z(steps))  11.7 us
    ppermute x3, waiting for transfers between devices, per_device(): lax.ppermute(opposite if steps % 2 else same, ALL, along_z(steps))  7.92 us
    all_to_all x1, starting transfers between devices, per_device(): qkv = lax.all_to_all(packed, ('z1', 'z0'), 0, 0)  6.01 us
    all_to_all x1, starting transfers between devices, per_device(): far_own = lax.all_to_all(spread, 'x', 0, 0)  4.95 us
    ppermute x1, starting transfers between devices, per_device(): moved_weight = lax.ppermute(out_weight, ALL, moved(place_weight))  4.91 us
    ppermute x3, waiting for transfers between devices, per_device(): lax.ppermute(group, 'y', [(i, (i + step) % NY) for i in range(NY)])  4.46 us
  transfers between devices with their start and end apart: 14, of which 6 were waited for; matrix products, arithmetic and copies ran while one was open for 0% of the time, Pallas kernels for 17%

profile of v7, /device:TPU:38, one launch (start us, length us, event | category | flops | bytes accessed | tf_op | source)
XLA Modules:
  0.0 114.9 jit_solution(1601213130756038293)
XLA Ops:
  7.2 0.0 copy-start
  7.2 1.9 %pack.1 = (bf16[4,3,128,128]{3,2,1,0:T(8,128)(2,1)}, f32[3,2,1024]{2,1,0:T(2,128)S(1)}) custom-call(bf16[3,128,512]{2,1,0:T(8,128)(2,1)} %refs_0_.3, bf16[3,128,1024]{2,1,0:T(8,128)(2,1)} %refs_0_.4), custom_call_target="tpu_custom_call" | custom-call | flops 100000000 | bytes 2000000 | tf_op jit(solution)/shard_map/pack/pallas_call | solution.py:93
  9.1 6.0 %all-to-all-start = ((bf16[4,3,128,128]{3,2,1,0:T(8,128)(2,1)}), bf16[4,3,128,128]{3,2,1,0:T(8,128)(2,1)S(1)}, u32[]{:S(2)}, u32[]{:S(2)}) async-start(bf16[4,3,128,128]{3,2,1,0:T(8,128)(2,1)} %get-tuple-element.14), calls=%async_computation | async-start | bytes 786432 | tf_op jit(solution)/shard_map/all_to_all | solution.py:388
  15.1 0.0 copy-done
  15.1 4.9 %collective-permute-start.1 = (bf16[512,256]{1,0:T(8,128)(2,1)S(1)}, bf16[512,256]{1,0:T(8,128)(2,1)S(1)}, u32[]{:S(2)}, u32[]{:S(2)}) collective-permute-start(bf16[512,256]{1,0:T(8,128)(2,1)S(1)} %copy-done), channel_id=1, source_target_pairs={{0,0},{1,32},{2,64},{3,96},{4,128},{5,160},{6,192},{7,224},{8,8},{... | collective-permute-start | bytes 786440 | tf_op jit(solution)/shard_map/ppermute | solution.py:413
  20.0 1.9 %collective-permute-start = (f32[3,2,1024]{2,1,0:T(2,128)S(1)}, f32[3,2,1024]{2,1,0:T(2,128)S(1)}, u32[]{:S(2)}, u32[]{:S(2)}) collective-permute-start(f32[3,2,1024]{2,1,0:T(2,128)S(1)} %get-tuple-element.15), channel_id=1, source_target_pairs={{0,8},{1,9},{2,10},{3,11},{4,12},{5,13},{6,14},{7,15},{8,16},{9,17... | collective-permute-start | bytes 73736 | tf_op jit(solution)/shard_map/ppermute | solution.py:389
  22.0 3.2 %collective-permute-done.refs_1_ = f32[3,2,1024]{2,1,0:T(2,128)S(1)} collective-permute-done((f32[3,2,1024]{2,1,0:T(2,128)S(1)}, f32[3,2,1024]{2,1,0:T(2,128)S(1)}, u32[]{:S(2)}, u32[]{:S(2)}) %collective-permute-start) | collective-permute-done | bytes 24608 | tf_op jit(solution)/shard_map/ppermute | solution.py:389
  25.2 3.1 %ends.1 = (bf16[2,128,128]{2,1,0:T(8,128)(2,1)S(1)}, f32[128,1024]{1,0:T(8,128)}, f32[128,1024]{1,0:T(8,128)}) custom-call(bf16[3,128,1024]{2,1,0:T(8,128)(2,1)} %refs_0_.4, f32[3,2,1024]{2,1,0:T(2,128)S(1)} %collective-permute-done.refs_1_, f32[3,3,1024]{2,1,0:T(4,128)} %refs_2_.1, f32[16,1024]{1,0:T(8,128)} %refs_0_.5), custom_call_target="tpu_custom_call" | custom-call | flops 1000000000 | bytes 2000000 | tf_op jit(solution)/shard_map/ends/pallas_call | solution.py:93
  28.3 0.0 collective-permute-done.1.refs_2_.refs_1_
  28.3 0.0 all-to-all-done.refs_0_.refs_1_
  28.3 1.2 %spread.1.refs_2_ = bf16[4,10,128,128]{3,2,1,0:T(8,128)(2,1)} custom-call(bf16[4,3,128,128]{3,2,1,0:T(8,128)(2,1)S(1)} %all-to-all-done.refs_0_.refs_1_, bf16[2,128,128]{2,1,0:T(8,128)(2,1)S(1)} %get-tuple-element.16.refs_1_, bf16[512,256]{1,0:T(8,128)(2,1)S(1)} %collective-permute-done.1.refs_2_.refs_1_), custom_call_target="tpu_custom_call" | custom-call | flops 100000000 | bytes 2000000 | tf_op jit(solution)/shard_map/spread/pallas_call | solution.py:93
  29.5 4.9 %all-to-all-start.1 = ((bf16[4,10,128,128]{3,2,1,0:T(8,128)(2,1)}), bf16[4,10,128,128]{3,2,1,0:T(8,128)(2,1)S(1)}, u32[]{:S(2)}, u32[]{:S(2)}) async-start(bf16[4,10,128,128]{3,2,1,0:T(8,128)(2,1)} %spread.1.refs_2_), calls=%async_computation.1 | async-start | bytes 2621440 | tf_op jit(solution)/shard_map/all_to_all | solution.py:422
  34.5 0.0 all-gather.3.cloned.1.call-start
  34.5 10.1 %collective-permute-start.6 = (bf16[2,128,256]{2,1,0:T(8,128)(2,1)S(1)}, bf16[2,128,256]{2,1,0:T(8,128)(2,1)S(1)}, u32[]{:S(2)}, u32[]{:S(2)}) collective-permute-start(bf16[2,128,256]{2,1,0:T(8,128)(2,1)S(1)} %get-tuple-element.23), channel_id=1, source_target_pairs={{0,16},{1,17},{2,18},{3,19},{4,20},{5,21},{6,22},{7,23},{8,24},{9,... | collective-permute-start | bytes 393224 | tf_op jit(solution)/shard_map/ppermute | solution.py:431
  44.6 0.0 collective-permute-start.7
  44.6 1.6 %collective-permute-start.8 = (bf16[2,128,256]{2,1,0:T(8,128)(2,1)S(1)}, bf16[2,128,256]{2,1,0:T(8,128)(2,1)S(1)}, u32[]{:S(2)}, u32[]{:S(2)}) collective-permute-start(bf16[2,128,256]{2,1,0:T(8,128)(2,1)S(1)} %get-tuple-element.23), channel_id=1, source_target_pairs={{0,48},{1,49},{2,50},{3,51},{4,52},{5,53},{6,54},{7,55},{8,56},{9,... | collective-permute-start | bytes 393224 | tf_op jit(solution)/shard_map/ppermute | solution.py:431
  46.2 6.5 %collective-permute-done.6.refs_2_ = bf16[2,128,256]{2,1,0:T(8,128)(2,1)S(1)} collective-permute-done((bf16[2,128,256]{2,1,0:T(8,128)(2,1)S(1)}, bf16[2,128,256]{2,1,0:T(8,128)(2,1)S(1)}, u32[]{:S(2)}, u32[]{:S(2)}) %collective-permute-start.6) | collective-permute-done | bytes 131104 | tf_op jit(solution)/shard_map/ppermute | solution.py:431
  52.7 1.4 %collective-permute-done.7.refs_3_ = bf16[2,128,256]{2,1,0:T(8,128)(2,1)S(1)} collective-permute-done((bf16[2,128,256]{2,1,0:T(8,128)(2,1)S(1)}, bf16[2,128,256]{2,1,0:T(8,128)(2,1)S(1)}, u32[]{:S(2)}, u32[]{:S(2)}) %collective-permute-start.7) | collective-permute-done | bytes 131104 | tf_op jit(solution)/shard_map/ppermute | solution.py:431
  54.1 0.0 collective-permute-done.8.refs_4_
  54.1 0.0 all-to-all-done.1.refs_2_.refs_5_
  54.1 0.8 stack.35
  54.9 0.0 all-gather.3.cloned.1.call-update
  55.0 0.1 collective-permute-start.2
  55.1 0.1 pad_add_fusion.1.refs_0_
  55.1 3.1 %own.1 = (f32[1,512]{1,0:T(1,128)S(1)}, f32[1,512]{1,0:T(1,128)S(1)}, f32[128,512]{1,0:T(8,128)S(1)}) custom-call(s32[2]{0:T(128)S(1)} %pad_add_fusion.1.refs_0_, bf16[4,3,128,128]{3,2,1,0:T(8,128)(2,1)S(1)} %all-to-all-done.refs_0_.refs_1_, bf16[4,10,128,128]{3,2,1,0:T(8,128)(2,1)S(1)} %all-to-all-done.1.refs_2_.refs_5_), custom_call_target="tpu_custom_call" | custom-call | flops 2000000000 | bytes 2000000 | tf_op jit(solution)/shard_map/own/pallas_call | solution.py:93
  58.3 0.0 collective-permute-done.2.refs_5_.refs_3_
  58.3 3.4 %other.1 = bf16[2,2,256,128]{3,2,1,0:T(8,128)(2,1)S(1)} custom-call(s32[2]{0:T(128)S(1)} %pad_add_fusion.1.refs_0_, bf16[4,3,128,128]{3,2,1,0:T(8,128)(2,1)S(1)} %all-to-all-done.refs_0_.refs_1_, f32[1,512]{1,0:T(1,128)S(1)} %get-tuple-element.17.refs_2_, f32[1,512]{1,0:T(1,128)S(1)} %get-tuple-element.18.refs_3_, f32[128,512]{1,0:T(8,128)S(1)} %get-tuple-element.19.refs_4_, ...), custom_call_target="tpu_custom_call" | custom-call | flops 2000000000 | bytes 2000000 | tf_op jit(solution)/shard_map/other/pallas_call | solution.py:93
  61.7 20.7 %all_to_all.20.refs_4_.refs_1_ = bf16[4,256,128]{2,1,0:T(8,128)(2,1)S(1)} all-to-all(bf16[4,256,128]{2,1,0:T(8,128)(2,1)S(1)} %bitcast.7), channel_id=1, replica_groups=mesh['x'=4,'z1'=2,'z0'=2,'k'=2,'y'=4,'h'=2] {'h','z1'}, dimensions={0} | all-to-all | bytes 524288 | tf_op jit(solution)/shard_map/all_to_all | solution.py:453
  82.4 0.2 collective-permute-start.3
  82.6 3.0 %collective-permute-start.4 = (bf16[4,256,128]{2,1,0:T(8,128)(2,1)S(1)}, bf16[4,256,128]{2,1,0:T(8,128)(2,1)S(1)}, u32[]{:S(2)}, u32[]{:S(2)}) collective-permute-start(bf16[4,256,128]{2,1,0:T(8,128)(2,1)S(1)} %all_to_all.20.refs_4_.refs_1_), channel_id=1, source_target_pairs={{0,6},{2,0},{4,2},{6,4},{1,7},{3,1},{5,3},{7,5},{8,14},{10,8},{12,... | collective-permute-start | bytes 786440 | tf_op jit(solution)/shard_map/ppermute | solution.py:455
  85.6 0.7 collective-permute-start.5
  86.4 0.1 pad_add_fusion.refs_0_
  86.5 2.3 %combine.1 = f32[4,16,1024]{2,1,0:T(8,128)} custom-call(s32[3]{0:T(128)S(1)} %pad_add_fusion.refs_0_, f32[16,1024]{1,0:T(8,128)} %refs_0_.5, bf16[4,10,128,128]{3,2,1,0:T(8,128)(2,1)S(1)} %all-to-all-done.1.refs_2_.refs_5_, bf16[4,10,128,128]{3,2,1,0:T(8,128)(2,1)S(1)} %collective-permute-done.2.refs_5_.refs_3_, ...), custom_call_target="tpu_custom_call" | custom-call | flops 100000000 | bytes 2000000 | tf_op jit(solution)/shard_map/combine/pallas_call | solution.py:93
  88.8 3.7 %all-to-all-start.3 = ((f32[4,16,1024]{2,1,0:T(8,128)}), f32[4,16,1024]{2,1,0:T(8,128)S(1)}, u32[]{:S(2)}, u32[]{:S(2)}) async-start(f32[4,16,1024]{2,1,0:T(8,128)} %combine.1), calls=%async_computation.3 | async-start | bytes 524288 | tf_op jit(solution)/shard_map/all_to_all | solution.py:467
  92.5 0.1 pad_add_fusion.2.refs_0_
  92.5 0.0 collective-permute-done.3.refs_2_
  92.5 2.9 %collective-permute-done.4.refs_3_ = bf16[4,256,128]{2,1,0:T(8,128)(2,1)S(1)} collective-permute-done((bf16[4,256,128]{2,1,0:T(8,128)(2,1)S(1)}, bf16[4,256,128]{2,1,0:T(8,128)(2,1)S(1)}, u32[]{:S(2)}, u32[]{:S(2)}) %collective-permute-start.4) | collective-permute-done | bytes 262176 | tf_op jit(solution)/shard_map/ppermute | solution.py:455
  95.4 1.6 %collective-permute-done.5.refs_4_ = bf16[4,256,128]{2,1,0:T(8,128)(2,1)} collective-permute-done((bf16[4,256,128]{2,1,0:T(8,128)(2,1)S(1)}, bf16[4,256,128]{2,1,0:T(8,128)(2,1)}, u32[]{:S(2)}, u32[]{:S(2)}) %collective-permute-start.5) | collective-permute-done | bytes 262176 | tf_op jit(solution)/shard_map/ppermute | solution.py:455
  97.0 0.0 all-gather.3.cloned.1.call-done
  97.0 3.8 %project.1 = (f32[128,1024]{1,0:T(8,128)S(1)}, bf16[128,1024]{1,0:T(8,128)(2,1)S(1)}) custom-call(s32[2]{0:T(128)S(1)} %pad_add_fusion.2.refs_0_, bf16[4,256,128]{2,1,0:T(8,128)(2,1)S(1)} %all_to_all.20.refs_4_.refs_1_, bf16[4,256,128]{2,1,0:T(8,128)(2,1)S(1)} %collective-permute-done.3.refs_2_, bf16[4,256,128]{2,1,0:T(8,128)(2,1)S(1)} %collective-permute-done.4.refs_3_, ...), custom_call_target="tpu_custom_call" | custom-call | flops 2000000000 | bytes 2000000 | tf_op jit(solution)/shard_map/project/pallas_call | solution.py:93
  100.9 0.1 collective-permute-start.9
  101.0 0.0 all-to-all-done.3.refs_2_
  101.0 4.1 %mix.1 = bf16[128,1024]{1,0:T(8,128)(2,1)} custom-call(f32[16,1024]{1,0:T(8,128)} %refs_0_.5, f32[16,1024]{1,0:T(8,128)} %refs_1_.5, f32[4,16,1024]{2,1,0:T(8,128)S(1)} %all-to-all-done.3.refs_2_, f32[128,1024]{1,0:T(8,128)} %get-tuple-element.20.refs_3_, f32[128,1024]{1,0:T(8,128)} %get-tuple-element.21.refs_4_), custom_call_target="tpu_custom_call" | custom-call | flops 4000000000 | bytes 2000000 | tf_op jit(solution)/shard_map/mix/pallas_call | solution.py:93
  105.1 2.2 %collective-permute-done.9 = bf16[128,1024]{1,0:T(8,128)(2,1)S(1)} collective-permute-done((bf16[128,1024]{1,0:T(8,128)(2,1)S(1)}, bf16[128,1024]{1,0:T(8,128)(2,1)S(1)}, u32[]{:S(2)}, u32[]{:S(2)}) %collective-permute-start.9) | collective-permute-done | bytes 262176 | tf_op jit(solution)/shard_map/ppermute | solution.py:482
  107.3 0.8 add_convert_fusion
  (1 shorter events, 0.0 us)
Async XLA Ops:
  7.2 8.0 %copy-start = (bf16[512,256]{1,0:T(8,128)(2,1)S(1)}, bf16[512,256]{1,0:T(8,128)(2,1)}, u32[]{:S(2)}) copy-start(bf16[512,256]{1,0:T(8,128)(2,1)} %param.11) | copy-start | bytes 786436
  9.1 19.2 %all-to-all-start = ((bf16[4,3,128,128]{3,2,1,0:T(8,128)(2,1)}), bf16[4,3,128,128]{3,2,1,0:T(8,128)(2,1)S(1)}, u32[]{:S(2)}, u32[]{:S(2)}) async-start(bf16[4,3,128,128]{3,2,1,0:T(8,128)(2,1)} %get-tuple-element.14), calls=%async_computation | async-start | bytes 786432 | tf_op jit(solution)/shard_map/all_to_all | solution.py:388
  15.1 13.2 %collective-permute-start.1 = (bf16[512,256]{1,0:T(8,128)(2,1)S(1)}, bf16[512,256]{1,0:T(8,128)(2,1)S(1)}, u32[]{:S(2)}, u32[]{:S(2)}) collective-permute-start(bf16[512,256]{1,0:T(8,128)(2,1)S(1)} %copy-done), channel_id=1, source_target_pairs={{0,0},{1,32},{2,64},{3,96},{4,128},{5,160},{6,192},{7,224},{8,8},{... | collective-permute-start | bytes 786440 | tf_op jit(solution)/shard_map/ppermute | solution.py:413
  20.0 5.1 %collective-permute-start = (f32[3,2,1024]{2,1,0:T(2,128)S(1)}, f32[3,2,1024]{2,1,0:T(2,128)S(1)}, u32[]{:S(2)}, u32[]{:S(2)}) collective-permute-start(f32[3,2,1024]{2,1,0:T(2,128)S(1)} %get-tuple-element.15), channel_id=1, source_target_pairs={{0,8},{1,9},{2,10},{3,11},{4,12},{5,13},{6,14},{7,15},{8,16},{9,17... | collective-permute-start | bytes 73736 | tf_op jit(solution)/shard_map/ppermute | solution.py:389
  29.5 24.6 %all-to-all-start.1 = ((bf16[4,10,128,128]{3,2,1,0:T(8,128)(2,1)}), bf16[4,10,128,128]{3,2,1,0:T(8,128)(2,1)S(1)}, u32[]{:S(2)}, u32[]{:S(2)}) async-start(bf16[4,10,128,128]{3,2,1,0:T(8,128)(2,1)} %spread.1.refs_2_), calls=%async_computation.1 | async-start | bytes 2621440 | tf_op jit(solution)/shard_map/all_to_all | solution.py:422
  34.5 62.5 %all-gather.3.cloned.1.call-start = ((), (), s32[]{:S(2)}) async-start(), calls=%async_computation.4 | async-start | bytes 4718592 | tf_op jit(solution)/shard_map/all_gather | solution.py:437
  34.5 18.2 %collective-permute-start.6 = (bf16[2,128,256]{2,1,0:T(8,128)(2,1)S(1)}, bf16[2,128,256]{2,1,0:T(8,128)(2,1)S(1)}, u32[]{:S(2)}, u32[]{:S(2)}) collective-permute-start(bf16[2,128,256]{2,1,0:T(8,128)(2,1)S(1)} %get-tuple-element.23), channel_id=1, source_target_pairs={{0,16},{1,17},{2,18},{3,19},{4,20},{5,21},{6,22},{7,23},{8,24},{9,... | collective-permute-start | bytes 393224 | tf_op jit(solution)/shard_map/ppermute | solution.py:431
  44.6 9.5 %collective-permute-start.7 = (bf16[2,128,256]{2,1,0:T(8,128)(2,1)S(1)}, bf16[2,128,256]{2,1,0:T(8,128)(2,1)S(1)}, u32[]{:S(2)}, u32[]{:S(2)}) collective-permute-start(bf16[2,128,256]{2,1,0:T(8,128)(2,1)S(1)} %get-tuple-element.22.refs_1_), channel_id=1, source_target_pairs={{0,32},{1,33},{2,34},{3,35},{4,36},{5,37},{6,38},{7,39},{8,40},{9,... | collective-permute-start | bytes 393224 | tf_op jit(solution)/shard_map/ppermute | solution.py:431
  44.6 9.5 %collective-permute-start.8 = (bf16[2,128,256]{2,1,0:T(8,128)(2,1)S(1)}, bf16[2,128,256]{2,1,0:T(8,128)(2,1)S(1)}, u32[]{:S(2)}, u32[]{:S(2)}) collective-permute-start(bf16[2,128,256]{2,1,0:T(8,128)(2,1)S(1)} %get-tuple-element.23), channel_id=1, source_target_pairs={{0,48},{1,49},{2,50},{3,51},{4,52},{5,53},{6,54},{7,55},{8,56},{9,... | collective-permute-start | bytes 393224 | tf_op jit(solution)/shard_map/ppermute | solution.py:431
  55.0 3.3 %collective-permute-start.2 = (bf16[4,10,128,128]{3,2,1,0:T(8,128)(2,1)S(1)}, bf16[4,10,128,128]{3,2,1,0:T(8,128)(2,1)S(1)}, u32[]{:S(2)}, u32[]{:S(2)}) collective-permute-start(bf16[4,10,128,128]{3,2,1,0:T(8,128)(2,1)S(1)} %all-to-all-done.1.refs_2_.refs_5_), channel_id=1, source_target_pairs={{0,8},{8,0},{1,9},{9,1},{2,10},{10,2},{3,11},{11,3},{4,12},{12,4},... | collective-permute-start | bytes 3932168 | tf_op jit(solution)/shard_map/ppermute | solution.py:423
  82.4 10.1 %collective-permute-start.3 = (bf16[4,256,128]{2,1,0:T(8,128)(2,1)S(1)}, bf16[4,256,128]{2,1,0:T(8,128)(2,1)S(1)}, u32[]{:S(2)}, u32[]{:S(2)}) collective-permute-start(bf16[4,256,128]{2,1,0:T(8,128)(2,1)S(1)} %all_to_all.20.refs_4_.refs_1_), channel_id=1, source_target_pairs={{0,2},{2,4},{4,6},{6,0},{1,3},{3,5},{5,7},{7,1},{8,10},{10,12},{12... | collective-permute-start | bytes 786440 | tf_op jit(solution)/shard_map/ppermute | solution.py:455
  82.6 12.8 %collective-permute-start.4 = (bf16[4,256,128]{2,1,0:T(8,128)(2,1)S(1)}, bf16[4,256,128]{2,1,0:T(8,128)(2,1)S(1)}, u32[]{:S(2)}, u32[]{:S(2)}) collective-permute-start(bf16[4,256,128]{2,1,0:T(8,128)(2,1)S(1)} %all_to_all.20.refs_4_.refs_1_), channel_id=1, source_target_pairs={{0,6},{2,0},{4,2},{6,4},{1,7},{3,1},{5,3},{7,5},{8,14},{10,8},{12,... | collective-permute-start | bytes 786440 | tf_op jit(solution)/shard_map/ppermute | solution.py:455
  85.6 11.4 %collective-permute-start.5 = (bf16[4,256,128]{2,1,0:T(8,128)(2,1)S(1)}, bf16[4,256,128]{2,1,0:T(8,128)(2,1)}, u32[]{:S(2)}, u32[]{:S(2)}) collective-permute-start(bf16[4,256,128]{2,1,0:T(8,128)(2,1)S(1)} %all_to_all.20.refs_4_.refs_1_), channel_id=1, source_target_pairs={{0,4},{2,6},{4,0},{6,2},{1,5},{3,7},{5,1},{7,3},{8,12},{10,14},{12... | collective-permute-start | bytes 786440 | tf_op jit(solution)/shard_map/ppermute | solution.py:455
  88.8 12.2 %all-to-all-start.3 = ((f32[4,16,1024]{2,1,0:T(8,128)}), f32[4,16,1024]{2,1,0:T(8,128)S(1)}, u32[]{:S(2)}, u32[]{:S(2)}) async-start(f32[4,16,1024]{2,1,0:T(8,128)} %combine.1), calls=%async_computation.3 | async-start | bytes 524288 | tf_op jit(solution)/shard_map/all_to_all | solution.py:467
  100.9 6.5 %collective-permute-start.9 = (bf16[128,1024]{1,0:T(8,128)(2,1)S(1)}, bf16[128,1024]{1,0:T(8,128)(2,1)S(1)}, u32[]{:S(2)}, u32[]{:S(2)}) collective-permute-start(bf16[128,1024]{1,0:T(8,128)(2,1)S(1)} %get-tuple-element.25), channel_id=1, source_target_pairs={{0,16},{16,0},{1,17},{17,1},{2,18},{18,2},{3,19},{19,3},{4,20},{20... | collective-permute-start | bytes 786440 | tf_op jit(solution)/shard_map/ppermute | solution.py:482
Sparse Core Ops, SparseCore 0:
  55.1 36.4 all-gather.2

commit v8 on v7

--- a/solution.py
+++ b/solution.py
@@ -334,7 +334,7 @@
     copies = started(
         sems,
         [
-            (w_hbm.at[i, k, pl.ds(lo, 2)], parts.at[i, k, pl.ds(lo, 2)])
+            (w_hbm.at[k, i, pl.ds(lo, 2)], parts.at[i, k, pl.ds(lo, 2)])
             for i in range(NX)
             for k in range(NK)
             for lo in (0, 2)
@@ -434,7 +434,7 @@
         stack_kernel, short((NZ, *half.shape), bf16), (SMEM,) + (FAST,) * NZ, "stack", 10**8,
         after=(far_own,),
     )(z, *arrived)
-    weight = lax.all_gather(placed, ("x", "k")).reshape(NX, NK, *placed.shape)
+    weight = lax.all_gather(placed, ("k", "x")).reshape(NK, NX, *placed.shape)
 
     where = jnp.stack([x, k])
     line = short((1, NZ * rows), f32)
@@ -474,7 +474,7 @@
         2 * 10**9,
         (
             pltpu.VMEM((NY, *group.shape), bf16),
-            pltpu.VMEM(weight.shape, bf16),
+            pltpu.VMEM((NX, NK, *placed.shape), bf16),
             pltpu.VMEM((NK, NZ0 * rows, width // 2), f32),
             dma((4 * NX,)),
         ),

time: 115 us -> 115 us (level)
  no operation moved by 1% of the time
where the time goes in v8:
time: 115 us
  starting transfers between devices  37.3 us (32%)
  Pallas kernels  23.9 us (21%)
  blocking collectives  20.7 us (18%)
  waiting for transfers between devices  17.8 us (15%)
  between operations  14.2 us (12%)
    pallas_call x10, Pallas kernels, local_call(): return lambda *operands: call(*map(placed, operands, specs), *after)  23.9 us
    all_to_all x1, blocking collectives, per_device(): lax.all_to_all(attended.reshape(NH * NZ1, NZ0 * rows, HEAD), ('h', 'z1'),...  20.7 us
    ppermute x3, starting transfers between devices, per_device(): lax.ppermute(opposite if steps % 2 else same, ALL, along_z(steps))  11.7 us
    ppermute x3, waiting for transfers between devices, per_device(): lax.ppermute(opposite if steps % 2 else same, ALL, along_z(steps))  7.92 us
    all_to_all x1, starting transfers between devices, per_device(): qkv = lax.all_to_all(packed, ('z1', 'z0'), 0, 0)  6.01 us
    all_to_all x1, starting transfers between devices, per_device(): far_own = lax.all_to_all(spread, 'x', 0, 0)  4.95 us
    ppermute x1, starting transfers between devices, per_device(): moved_weight = lax.ppermute(out_weight, ALL, moved(place_weight))  4.91 us
    ppermute x3, waiting for transfers between devices, per_device(): lax.ppermute(group, 'y', [(i, (i + step) % NY) for i in range(NY)])  4.46 us
  transfers between devices with their start and end apart: 14, of which 6 were waited for; matrix products, arithmetic and copies ran while one was open for 0% of the time, Pallas kernels for 17%

profile of v8, /device:TPU:38, one launch (start us, length us, event | category | flops | bytes accessed | tf_op | source)
XLA Modules:
  0.0 114.9 jit_solution(11041192748634876010)
XLA Ops:
  7.2 0.0 copy-start
  7.2 1.9 %pack.1 = (bf16[4,3,128,128]{3,2,1,0:T(8,128)(2,1)}, f32[3,2,1024]{2,1,0:T(2,128)S(1)}) custom-call(bf16[3,128,512]{2,1,0:T(8,128)(2,1)} %refs_0_.3, bf16[3,128,1024]{2,1,0:T(8,128)(2,1)} %refs_0_.4), custom_call_target="tpu_custom_call" | custom-call | flops 100000000 | bytes 2000000 | tf_op jit(solution)/shard_map/pack/pallas_call | solution.py:93
  9.1 6.0 %all-to-all-start = ((bf16[4,3,128,128]{3,2,1,0:T(8,128)(2,1)}), bf16[4,3,128,128]{3,2,1,0:T(8,128)(2,1)S(1)}, u32[]{:S(2)}, u32[]{:S(2)}) async-start(bf16[4,3,128,128]{3,2,1,0:T(8,128)(2,1)} %get-tuple-element.14), calls=%async_computation | async-start | bytes 786432 | tf_op jit(solution)/shard_map/all_to_all | solution.py:388
  15.1 0.0 copy-done
  15.1 4.9 %collective-permute-start.1 = (bf16[512,256]{1,0:T(8,128)(2,1)S(1)}, bf16[512,256]{1,0:T(8,128)(2,1)S(1)}, u32[]{:S(2)}, u32[]{:S(2)}) collective-permute-start(bf16[512,256]{1,0:T(8,128)(2,1)S(1)} %copy-done), channel_id=1, source_target_pairs={{0,0},{1,32},{2,64},{3,96},{4,128},{5,160},{6,192},{7,224},{8,8},{... | collective-permute-start | bytes 786440 | tf_op jit(solution)/shard_map/ppermute | solution.py:413
  20.0 1.9 %collective-permute-start = (f32[3,2,1024]{2,1,0:T(2,128)S(1)}, f32[3,2,1024]{2,1,0:T(2,128)S(1)}, u32[]{:S(2)}, u32[]{:S(2)}) collective-permute-start(f32[3,2,1024]{2,1,0:T(2,128)S(1)} %get-tuple-element.15), channel_id=1, source_target_pairs={{0,8},{1,9},{2,10},{3,11},{4,12},{5,13},{6,14},{7,15},{8,16},{9,17... | collective-permute-start | bytes 73736 | tf_op jit(solution)/shard_map/ppermute | solution.py:389
  22.0 3.2 %collective-permute-done.refs_1_ = f32[3,2,1024]{2,1,0:T(2,128)S(1)} collective-permute-done((f32[3,2,1024]{2,1,0:T(2,128)S(1)}, f32[3,2,1024]{2,1,0:T(2,128)S(1)}, u32[]{:S(2)}, u32[]{:S(2)}) %collective-permute-start) | collective-permute-done | bytes 24608 | tf_op jit(solution)/shard_map/ppermute | solution.py:389
  25.2 3.1 %ends.1 = (bf16[2,128,128]{2,1,0:T(8,128)(2,1)S(1)}, f32[128,1024]{1,0:T(8,128)}, f32[128,1024]{1,0:T(8,128)}) custom-call(bf16[3,128,1024]{2,1,0:T(8,128)(2,1)} %refs_0_.4, f32[3,2,1024]{2,1,0:T(2,128)S(1)} %collective-permute-done.refs_1_, f32[3,3,1024]{2,1,0:T(4,128)} %refs_2_.1, f32[16,1024]{1,0:T(8,128)} %refs_0_.5), custom_call_target="tpu_custom_call" | custom-call | flops 1000000000 | bytes 2000000 | tf_op jit(solution)/shard_map/ends/pallas_call | solution.py:93
  28.3 0.0 collective-permute-done.1.refs_2_.refs_1_
  28.3 0.0 all-to-all-done.refs_0_.refs_1_
  28.3 1.2 %spread.1.refs_2_ = bf16[4,10,128,128]{3,2,1,0:T(8,128)(2,1)} custom-call(bf16[4,3,128,128]{3,2,1,0:T(8,128)(2,1)S(1)} %all-to-all-done.refs_0_.refs_1_, bf16[2,128,128]{2,1,0:T(8,128)(2,1)S(1)} %get-tuple-element.16.refs_1_, bf16[512,256]{1,0:T(8,128)(2,1)S(1)} %collective-permute-done.1.refs_2_.refs_1_), custom_call_target="tpu_custom_call" | custom-call | flops 100000000 | bytes 2000000 | tf_op jit(solution)/shard_map/spread/pallas_call | solution.py:93
  29.5 4.9 %all-to-all-start.1 = ((bf16[4,10,128,128]{3,2,1,0:T(8,128)(2,1)}), bf16[4,10,128,128]{3,2,1,0:T(8,128)(2,1)S(1)}, u32[]{:S(2)}, u32[]{:S(2)}) async-start(bf16[4,10,128,128]{3,2,1,0:T(8,128)(2,1)} %spread.1.refs_2_), calls=%async_computation.1 | async-start | bytes 2621440 | tf_op jit(solution)/shard_map/all_to_all | solution.py:422
  34.5 0.0 all-gather.3.cloned.1.call-start
  34.5 10.1 %collective-permute-start.6 = (bf16[2,128,256]{2,1,0:T(8,128)(2,1)S(1)}, bf16[2,128,256]{2,1,0:T(8,128)(2,1)S(1)}, u32[]{:S(2)}, u32[]{:S(2)}) collective-permute-start(bf16[2,128,256]{2,1,0:T(8,128)(2,1)S(1)} %get-tuple-element.23), channel_id=1, source_target_pairs={{0,16},{1,17},{2,18},{3,19},{4,20},{5,21},{6,22},{7,23},{8,24},{9,... | collective-permute-start | bytes 393224 | tf_op jit(solution)/shard_map/ppermute | solution.py:431
  44.6 0.0 collective-permute-start.7
  44.6 1.6 %collective-permute-start.8 = (bf16[2,128,256]{2,1,0:T(8,128)(2,1)S(1)}, bf16[2,128,256]{2,1,0:T(8,128)(2,1)S(1)}, u32[]{:S(2)}, u32[]{:S(2)}) collective-permute-start(bf16[2,128,256]{2,1,0:T(8,128)(2,1)S(1)} %get-tuple-element.23), channel_id=1, source_target_pairs={{0,48},{1,49},{2,50},{3,51},{4,52},{5,53},{6,54},{7,55},{8,56},{9,... | collective-permute-start | bytes 393224 | tf_op jit(solution)/shard_map/ppermute | solution.py:431
  46.2 6.5 %collective-permute-done.6.refs_2_ = bf16[2,128,256]{2,1,0:T(8,128)(2,1)S(1)} collective-permute-done((bf16[2,128,256]{2,1,0:T(8,128)(2,1)S(1)}, bf16[2,128,256]{2,1,0:T(8,128)(2,1)S(1)}, u32[]{:S(2)}, u32[]{:S(2)}) %collective-permute-start.6) | collective-permute-done | bytes 131104 | tf_op jit(solution)/shard_map/ppermute | solution.py:431
  52.7 1.4 %collective-permute-done.7.refs_3_ = bf16[2,128,256]{2,1,0:T(8,128)(2,1)S(1)} collective-permute-done((bf16[2,128,256]{2,1,0:T(8,128)(2,1)S(1)}, bf16[2,128,256]{2,1,0:T(8,128)(2,1)S(1)}, u32[]{:S(2)}, u32[]{:S(2)}) %collective-permute-start.7) | collective-permute-done | bytes 131104 | tf_op jit(solution)/shard_map/ppermute | solution.py:431
  54.1 0.0 collective-permute-done.8.refs_4_
  54.1 0.0 all-to-all-done.1.refs_2_.refs_5_
  54.1 0.8 stack.35
  54.9 0.0 all-gather.3.cloned.1.call-update
  55.0 0.1 collective-permute-start.2
  55.1 0.1 pad_add_fusion.1.refs_0_
  55.1 3.1 %own.1 = (f32[1,512]{1,0:T(1,128)S(1)}, f32[1,512]{1,0:T(1,128)S(1)}, f32[128,512]{1,0:T(8,128)S(1)}) custom-call(s32[2]{0:T(128)S(1)} %pad_add_fusion.1.refs_0_, bf16[4,3,128,128]{3,2,1,0:T(8,128)(2,1)S(1)} %all-to-all-done.refs_0_.refs_1_, bf16[4,10,128,128]{3,2,1,0:T(8,128)(2,1)S(1)} %all-to-all-done.1.refs_2_.refs_5_), custom_call_target="tpu_custom_call" | custom-call | flops 2000000000 | bytes 2000000 | tf_op jit(solution)/shard_map/own/pallas_call | solution.py:93
  58.3 0.0 collective-permute-done.2.refs_5_.refs_3_
  58.3 3.4 %other.1 = bf16[2,2,256,128]{3,2,1,0:T(8,128)(2,1)S(1)} custom-call(s32[2]{0:T(128)S(1)} %pad_add_fusion.1.refs_0_, bf16[4,3,128,128]{3,2,1,0:T(8,128)(2,1)S(1)} %all-to-all-done.refs_0_.refs_1_, f32[1,512]{1,0:T(1,128)S(1)} %get-tuple-element.17.refs_2_, f32[1,512]{1,0:T(1,128)S(1)} %get-tuple-element.18.refs_3_, f32[128,512]{1,0:T(8,128)S(1)} %get-tuple-element.19.refs_4_, ...), custom_call_target="tpu_custom_call" | custom-call | flops 2000000000 | bytes 2000000 | tf_op jit(solution)/shard_map/other/pallas_call | solution.py:93
  61.7 20.7 %all_to_all.20.refs_4_.refs_1_ = bf16[4,256,128]{2,1,0:T(8,128)(2,1)S(1)} all-to-all(bf16[4,256,128]{2,1,0:T(8,128)(2,1)S(1)} %bitcast.7), channel_id=1, replica_groups=mesh['x'=4,'z1'=2,'z0'=2,'k'=2,'y'=4,'h'=2] {'h','z1'}, dimensions={0} | all-to-all | bytes 524288 | tf_op jit(solution)/shard_map/all_to_all | solution.py:453
  82.4 0.2 collective-permute-start.3
  82.6 3.0 %collective-permute-start.4 = (bf16[4,256,128]{2,1,0:T(8,128)(2,1)S(1)}, bf16[4,256,128]{2,1,0:T(8,128)(2,1)S(1)}, u32[]{:S(2)}, u32[]{:S(2)}) collective-permute-start(bf16[4,256,128]{2,1,0:T(8,128)(2,1)S(1)} %all_to_all.20.refs_4_.refs_1_), channel_id=1, source_target_pairs={{0,6},{2,0},{4,2},{6,4},{1,7},{3,1},{5,3},{7,5},{8,14},{10,8},{12,... | collective-permute-start | bytes 786440 | tf_op jit(solution)/shard_map/ppermute | solution.py:455
  85.6 0.7 collective-permute-start.5
  86.4 0.1 pad_add_fusion.refs_0_
  86.5 2.3 %combine.1 = f32[4,16,1024]{2,1,0:T(8,128)} custom-call(s32[3]{0:T(128)S(1)} %pad_add_fusion.refs_0_, f32[16,1024]{1,0:T(8,128)} %refs_0_.5, bf16[4,10,128,128]{3,2,1,0:T(8,128)(2,1)S(1)} %all-to-all-done.1.refs_2_.refs_5_, bf16[4,10,128,128]{3,2,1,0:T(8,128)(2,1)S(1)} %collective-permute-done.2.refs_5_.refs_3_, ...), custom_call_target="tpu_custom_call" | custom-call | flops 100000000 | bytes 2000000 | tf_op jit(solution)/shard_map/combine/pallas_call | solution.py:93
  88.8 3.7 %all-to-all-start.3 = ((f32[4,16,1024]{2,1,0:T(8,128)}), f32[4,16,1024]{2,1,0:T(8,128)S(1)}, u32[]{:S(2)}, u32[]{:S(2)}) async-start(f32[4,16,1024]{2,1,0:T(8,128)} %combine.1), calls=%async_computation.3 | async-start | bytes 524288 | tf_op jit(solution)/shard_map/all_to_all | solution.py:467
  92.5 0.1 pad_add_fusion.2.refs_0_
  92.5 0.0 collective-permute-done.3.refs_2_
  92.5 2.9 %collective-permute-done.4.refs_3_ = bf16[4,256,128]{2,1,0:T(8,128)(2,1)S(1)} collective-permute-done((bf16[4,256,128]{2,1,0:T(8,128)(2,1)S(1)}, bf16[4,256,128]{2,1,0:T(8,128)(2,1)S(1)}, u32[]{:S(2)}, u32[]{:S(2)}) %collective-permute-start.4) | collective-permute-done | bytes 262176 | tf_op jit(solution)/shard_map/ppermute | solution.py:455
  95.4 1.6 %collective-permute-done.5.refs_4_ = bf16[4,256,128]{2,1,0:T(8,128)(2,1)} collective-permute-done((bf16[4,256,128]{2,1,0:T(8,128)(2,1)S(1)}, bf16[4,256,128]{2,1,0:T(8,128)(2,1)}, u32[]{:S(2)}, u32[]{:S(2)}) %collective-permute-start.5) | collective-permute-done | bytes 262176 | tf_op jit(solution)/shard_map/ppermute | solution.py:455
  97.0 0.0 all-gather.3.cloned.1.call-done
  97.0 3.8 %project.1 = (f32[128,1024]{1,0:T(8,128)S(1)}, bf16[128,1024]{1,0:T(8,128)(2,1)S(1)}) custom-call(s32[2]{0:T(128)S(1)} %pad_add_fusion.2.refs_0_, bf16[4,256,128]{2,1,0:T(8,128)(2,1)S(1)} %all_to_all.20.refs_4_.refs_1_, bf16[4,256,128]{2,1,0:T(8,128)(2,1)S(1)} %collective-permute-done.3.refs_2_, bf16[4,256,128]{2,1,0:T(8,128)(2,1)S(1)} %collective-permute-done.4.refs_3_, ...), custom_call_target="tpu_custom_call" | custom-call | flops 2000000000 | bytes 2000000 | tf_op jit(solution)/shard_map/project/pallas_call | solution.py:93
  100.9 0.1 collective-permute-start.9
  101.0 0.0 all-to-all-done.3.refs_2_
  101.0 4.1 %mix.1 = bf16[128,1024]{1,0:T(8,128)(2,1)} custom-call(f32[16,1024]{1,0:T(8,128)} %refs_0_.5, f32[16,1024]{1,0:T(8,128)} %refs_1_.5, f32[4,16,1024]{2,1,0:T(8,128)S(1)} %all-to-all-done.3.refs_2_, f32[128,1024]{1,0:T(8,128)} %get-tuple-element.20.refs_3_, f32[128,1024]{1,0:T(8,128)} %get-tuple-element.21.refs_4_), custom_call_target="tpu_custom_call" | custom-call | flops 4000000000 | bytes 2000000 | tf_op jit(solution)/shard_map/mix/pallas_call | solution.py:93
  105.1 2.2 %collective-permute-done.9 = bf16[128,1024]{1,0:T(8,128)(2,1)S(1)} collective-permute-done((bf16[128,1024]{1,0:T(8,128)(2,1)S(1)}, bf16[128,1024]{1,0:T(8,128)(2,1)S(1)}, u32[]{:S(2)}, u32[]{:S(2)}) %collective-permute-start.9) | collective-permute-done | bytes 262176 | tf_op jit(solution)/shard_map/ppermute | solution.py:482
  107.3 0.8 add_convert_fusion
  (1 shorter events, 0.0 us)
Async XLA Ops:
  7.2 8.0 %copy-start = (bf16[512,256]{1,0:T(8,128)(2,1)S(1)}, bf16[512,256]{1,0:T(8,128)(2,1)}, u32[]{:S(2)}) copy-start(bf16[512,256]{1,0:T(8,128)(2,1)} %param.11) | copy-start | bytes 786436
  9.1 19.2 %all-to-all-start = ((bf16[4,3,128,128]{3,2,1,0:T(8,128)(2,1)}), bf16[4,3,128,128]{3,2,1,0:T(8,128)(2,1)S(1)}, u32[]{:S(2)}, u32[]{:S(2)}) async-start(bf16[4,3,128,128]{3,2,1,0:T(8,128)(2,1)} %get-tuple-element.14), calls=%async_computation | async-start | bytes 786432 | tf_op jit(solution)/shard_map/all_to_all | solution.py:388
  15.1 13.2 %collective-permute-start.1 = (bf16[512,256]{1,0:T(8,128)(2,1)S(1)}, bf16[512,256]{1,0:T(8,128)(2,1)S(1)}, u32[]{:S(2)}, u32[]{:S(2)}) collective-permute-start(bf16[512,256]{1,0:T(8,128)(2,1)S(1)} %copy-done), channel_id=1, source_target_pairs={{0,0},{1,32},{2,64},{3,96},{4,128},{5,160},{6,192},{7,224},{8,8},{... | collective-permute-start | bytes 786440 | tf_op jit(solution)/shard_map/ppermute | solution.py:413
  20.0 5.1 %collective-permute-start = (f32[3,2,1024]{2,1,0:T(2,128)S(1)}, f32[3,2,1024]{2,1,0:T(2,128)S(1)}, u32[]{:S(2)}, u32[]{:S(2)}) collective-permute-start(f32[3,2,1024]{2,1,0:T(2,128)S(1)} %get-tuple-element.15), channel_id=1, source_target_pairs={{0,8},{1,9},{2,10},{3,11},{4,12},{5,13},{6,14},{7,15},{8,16},{9,17... | collective-permute-start | bytes 73736 | tf_op jit(solution)/shard_map/ppermute | solution.py:389
  29.5 24.6 %all-to-all-start.1 = ((bf16[4,10,128,128]{3,2,1,0:T(8,128)(2,1)}), bf16[4,10,128,128]{3,2,1,0:T(8,128)(2,1)S(1)}, u32[]{:S(2)}, u32[]{:S(2)}) async-start(bf16[4,10,128,128]{3,2,1,0:T(8,128)(2,1)} %spread.1.refs_2_), calls=%async_computation.1 | async-start | bytes 2621440 | tf_op jit(solution)/shard_map/all_to_all | solution.py:422
  34.5 62.5 %all-gather.3.cloned.1.call-start = ((), (), s32[]{:S(2)}) async-start(), calls=%async_computation.4 | async-start | bytes 4718592 | tf_op jit(solution)/shard_map/all_gather | solution.py:437
  34.5 18.2 %collective-permute-start.6 = (bf16[2,128,256]{2,1,0:T(8,128)(2,1)S(1)}, bf16[2,128,256]{2,1,0:T(8,128)(2,1)S(1)}, u32[]{:S(2)}, u32[]{:S(2)}) collective-permute-start(bf16[2,128,256]{2,1,0:T(8,128)(2,1)S(1)} %get-tuple-element.23), channel_id=1, source_target_pairs={{0,16},{1,17},{2,18},{3,19},{4,20},{5,21},{6,22},{7,23},{8,24},{9,... | collective-permute-start | bytes 393224 | tf_op jit(solution)/shard_map/ppermute | solution.py:431
  44.6 9.5 %collective-permute-start.7 = (bf16[2,128,256]{2,1,0:T(8,128)(2,1)S(1)}, bf16[2,128,256]{2,1,0:T(8,128)(2,1)S(1)}, u32[]{:S(2)}, u32[]{:S(2)}) collective-permute-start(bf16[2,128,256]{2,1,0:T(8,128)(2,1)S(1)} %get-tuple-element.22.refs_1_), channel_id=1, source_target_pairs={{0,32},{1,33},{2,34},{3,35},{4,36},{5,37},{6,38},{7,39},{8,40},{9,... | collective-permute-start | bytes 393224 | tf_op jit(solution)/shard_map/ppermute | solution.py:431
  44.6 9.5 %collective-permute-start.8 = (bf16[2,128,256]{2,1,0:T(8,128)(2,1)S(1)}, bf16[2,128,256]{2,1,0:T(8,128)(2,1)S(1)}, u32[]{:S(2)}, u32[]{:S(2)}) collective-permute-start(bf16[2,128,256]{2,1,0:T(8,128)(2,1)S(1)} %get-tuple-element.23), channel_id=1, source_target_pairs={{0,48},{1,49},{2,50},{3,51},{4,52},{5,53},{6,54},{7,55},{8,56},{9,... | collective-permute-start | bytes 393224 | tf_op jit(solution)/shard_map/ppermute | solution.py:431
  55.0 3.3 %collective-permute-start.2 = (bf16[4,10,128,128]{3,2,1,0:T(8,128)(2,1)S(1)}, bf16[4,10,128,128]{3,2,1,0:T(8,128)(2,1)S(1)}, u32[]{:S(2)}, u32[]{:S(2)}) collective-permute-start(bf16[4,10,128,128]{3,2,1,0:T(8,128)(2,1)S(1)} %all-to-all-done.1.refs_2_.refs_5_), channel_id=1, source_target_pairs={{0,8},{8,0},{1,9},{9,1},{2,10},{10,2},{3,11},{11,3},{4,12},{12,4},... | collective-permute-start | bytes 3932168 | tf_op jit(solution)/shard_map/ppermute | solution.py:423
  82.4 10.1 %collective-permute-start.3 = (bf16[4,256,128]{2,1,0:T(8,128)(2,1)S(1)}, bf16[4,256,128]{2,1,0:T(8,128)(2,1)S(1)}, u32[]{:S(2)}, u32[]{:S(2)}) collective-permute-start(bf16[4,256,128]{2,1,0:T(8,128)(2,1)S(1)} %all_to_all.20.refs_4_.refs_1_), channel_id=1, source_target_pairs={{0,2},{2,4},{4,6},{6,0},{1,3},{3,5},{5,7},{7,1},{8,10},{10,12},{12... | collective-permute-start | bytes 786440 | tf_op jit(solution)/shard_map/ppermute | solution.py:455
  82.6 12.8 %collective-permute-start.4 = (bf16[4,256,128]{2,1,0:T(8,128)(2,1)S(1)}, bf16[4,256,128]{2,1,0:T(8,128)(2,1)S(1)}, u32[]{:S(2)}, u32[]{:S(2)}) collective-permute-start(bf16[4,256,128]{2,1,0:T(8,128)(2,1)S(1)} %all_to_all.20.refs_4_.refs_1_), channel_id=1, source_target_pairs={{0,6},{2,0},{4,2},{6,4},{1,7},{3,1},{5,3},{7,5},{8,14},{10,8},{12,... | collective-permute-start | bytes 786440 | tf_op jit(solution)/shard_map/ppermute | solution.py:455
  85.6 11.4 %collective-permute-start.5 = (bf16[4,256,128]{2,1,0:T(8,128)(2,1)S(1)}, bf16[4,256,128]{2,1,0:T(8,128)(2,1)}, u32[]{:S(2)}, u32[]{:S(2)}) collective-permute-start(bf16[4,256,128]{2,1,0:T(8,128)(2,1)S(1)} %all_to_all.20.refs_4_.refs_1_), channel_id=1, source_target_pairs={{0,4},{2,6},{4,0},{6,2},{1,5},{3,7},{5,1},{7,3},{8,12},{10,14},{12... | collective-permute-start | bytes 786440 | tf_op jit(solution)/shard_map/ppermute | solution.py:455
  88.8 12.2 %all-to-all-start.3 = ((f32[4,16,1024]{2,1,0:T(8,128)}), f32[4,16,1024]{2,1,0:T(8,128)S(1)}, u32[]{:S(2)}, u32[]{:S(2)}) async-start(f32[4,16,1024]{2,1,0:T(8,128)} %combine.1), calls=%async_computation.3 | async-start | bytes 524288 | tf_op jit(solution)/shard_map/all_to_all | solution.py:467
  100.9 6.5 %collective-permute-start.9 = (bf16[128,1024]{1,0:T(8,128)(2,1)S(1)}, bf16[128,1024]{1,0:T(8,128)(2,1)S(1)}, u32[]{:S(2)}, u32[]{:S(2)}) collective-permute-start(bf16[128,1024]{1,0:T(8,128)(2,1)S(1)} %get-tuple-element.25), channel_id=1, source_target_pairs={{0,16},{16,0},{1,17},{17,1},{2,18},{18,2},{3,19},{19,3},{4,20},{20... | collective-permute-start | bytes 786440 | tf_op jit(solution)/shard_map/ppermute | solution.py:482
Sparse Core Ops, SparseCore 0:
  55.1 36.4 all-gather.2
